TPU v7x, 32 devices: a whole 2x2x4 slice. The times are simulated.
32 devices in a mesh: groups: 2 (over x), rows: 8 (over z, y), layers: 2 (over core).
Axes of the slice: x: 2, y: 2, z: 4, core: 2. Of those that a mesh axis runs over, the one named last changes fastest.
Arguments:
- density: bfloat16 [256, 128, 768], P(('groups', 'rows'), None, 'layers'), parts along dimension 0, may hold values from -0.8984375 to 0.8984375
- columns: int32 [256, 6], P(('groups', 'rows'), 'layers'), parts along dimension 0, may hold values from 0 to 127, as said below
- kept: int32 [256, 6], P(('groups', 'rows'), 'layers'), parts along dimension 0, may hold values from 0 to 127, as said below
Outputs:
- new_density: bfloat16 [256, 128, 768], P(('groups', 'rows'), None, 'layers'), parts along dimension 0
There are 2 independent parts, one for each index of `groups`. A program takes and returns all parts, laid end to end along the dimension named above; each array names one. Nothing has to cross between parts.
Inputs may be any that keep to these rules, and one draw needn't show every extreme that they name: Each block row's 6 block columns are distinct and include the row itself. Block row r lies in index r // 16 of the rows axis; the block rows named by the columns of one such index's 16 block rows lie in that index or in the 2 indices on either side of it, counted around the axis; at most 2 distinct ones lie in any one other index, and exactly 2 in some. Each block row's 6 kept block columns are distinct and include the row itself.
All inputs are finite; a program needn't handle non-finite values.
Results may differ from a plain program's by a relative error of at most 0.0055.
Values may be sent and summed in bfloat16 or wider, within the bound.
No kernel may reach another device: no remote copies, remote signals or barrier semaphores. Data moves between devices by JAX's collectives and lax.ppermute only.
A program may use at most 64 MiB of HBM per device.

v0:
```python
import jax
import jax.numpy as jnp
from jax import lax
from jax.sharding import PartitionSpec as P

CAP = 2
REACH = 2


def from_behind(value, axis, steps):
    count = lax.axis_size(axis)
    pairs = [(source, (source + steps) % count) for source in range(count)]
    return lax.ppermute(value, axis, pairs)


def locate(all_columns, block_rows, peers, myself):
    flat_cols = all_columns.reshape(-1)
    every_row = jnp.arange(peers * block_rows, dtype=jnp.int32)
    hit_table = flat_cols[:, None] == every_row[None, :]
    owner_of = every_row // block_rows
    local_of = every_row % block_rows
    present = jnp.any(hit_table, axis=0) & (owner_of != myself)
    needed = present.reshape(peers, block_rows)
    ranks = jnp.cumsum(needed.astype(jnp.int32), axis=1) - 1
    chosen = needed[:, None, :] & (
        ranks[:, None, :] == jnp.arange(CAP, dtype=jnp.int32)[None, :, None]
    )
    filled = jnp.any(chosen, axis=-1)
    wanted_rows = jnp.sum(
        jnp.where(chosen, jnp.arange(block_rows, dtype=jnp.int32)[None, None, :], 0), axis=-1
    )
    request = jnp.where(filled, wanted_rows, -1)
    return (hit_table, owner_of, local_of, ranks.reshape(-1), request)


def index_from(hit_table, slot_table, shape):
    picked = jnp.sum(jnp.where(hit_table[:, :, None], slot_table[None, :, :], 0), axis=1)
    return picked.reshape(shape)


def row_terms(left_half, table, table_cols, index, targets):
    groups, edge, wide = left_half.shape
    half_width = wide // edge
    halves = index.shape[2]
    count_out = targets.shape[0]
    right_rows = table[index].reshape(groups, half_width, halves, edge, half_width, edge)
    right_cols = table_cols[index]
    matched = (right_cols[:, :, :, :, None] == targets[None, None, None, None, :]).astype(
        jnp.bfloat16
    )
    selected = jnp.einsum(
        "gjhycz,gjhcs->gjysz", right_rows, matched, preferred_element_type=jnp.float32
    ).astype(jnp.bfloat16)
    selected = selected.reshape(groups, half_width * edge, count_out * edge)
    return jnp.einsum("gxk,gkn->xn", left_half, selected, preferred_element_type=jnp.float32)


def local(density, columns, kept):
    block_rows = density.shape[0]
    edge = density.shape[1]
    wide = density.shape[2]
    half_width = columns.shape[1]
    peers = lax.axis_size("rows")
    myself = lax.axis_index("rows")
    left_rows, all_columns, all_kept = (
        lax.all_gather(density[None], "layers", axis=0, tiled=True),
        lax.all_gather(columns[None], "layers", axis=0, tiled=True),
        lax.all_gather(kept[None], "layers", axis=0, tiled=True),
    )
    hit_table, owner_of, local_of, rank_of, request = locate(all_columns, block_rows, peers, myself)
    is_own = owner_of == myself
    distance = (owner_of - myself) % peers
    offsets = [step for reach_step in range(1, REACH + 1) for step in (reach_step, -reach_step)]
    place = sum(
        (jnp.where(distance == step % peers, position, 0) for position, step in enumerate(offsets))
    ).astype(jnp.int32)
    asked = [
        from_behind(jnp.take(request, (myself + step) % peers, axis=0), "rows", step)
        for step in offsets
    ]
    picks = [jnp.maximum(entry, 0) for entry in asked]
    row_list = jnp.arange(block_rows, dtype=jnp.int32)
    slot_table = jnp.where(is_own, local_of, block_rows + place * CAP + rank_of)[:, None]
    index = index_from(hit_table, slot_table, (2, block_rows, half_width, 1))

    def product(right_half, right_cols):
        pieces = []
        piece_cols = []
        for step, chosen in zip(offsets, picks):
            got, got_cols = from_behind((right_half[chosen], right_cols[chosen]), "rows", -step)
            pieces.append(got)
            piece_cols.append(got_cols)
        table = jnp.concatenate([right_half, jnp.stack(pieces).reshape(-1, edge, wide)], axis=0)
        table_cols = jnp.concatenate(
            [right_cols, jnp.stack(piece_cols).reshape(-1, half_width)], axis=0
        )

        def one_row(row_id):
            return row_terms(
                left_rows[:, row_id],
                table,
                table_cols,
                index[:, row_id],
                all_kept[:, row_id].reshape(-1),
            )

        terms = lax.map(one_row, row_list)
        return lax.psum_scatter(terms, "layers", scatter_dimension=2, tiled=True)

    square = product(density, columns).astype(jnp.bfloat16)
    cube = product(square, kept)
    return (3.0 * square.astype(jnp.float32) - 2.0 * cube).astype(jnp.bfloat16)


def solution(mesh):
    in_specs = (
        P(("groups", "rows"), None, "layers"),
        P(("groups", "rows"), "layers"),
        P(("groups", "rows"), "layers"),
    )
    out_specs = P(("groups", "rows"), None, "layers")
    return jax.shard_map(local, mesh=mesh, in_specs=in_specs, out_specs=out_specs, check_vma=False)
```

profile of v0, /device:TPU:0, one launch (start us, length us, event | category | flops | bytes accessed | tf_op | source)
XLA Modules:
  0.0 471.4 jit_solution(10916953990617643314)
XLA Ops:
  10.6 2.9 collective-permute-start
  13.5 3.1 collective-permute-start.2
  16.6 3.8 collective-permute-start.6
  33.8 4.8 %collective-permute-start.1 = (s32[2,3]{1,0:T(2,128)S(1)}, s32[2,3]{1,0:T(2,128)S(1)}, u32[]{:S(2)}, u32[]{:S(2)}) collective-permute-start(s32[2,3]{1,0:T(2,128)S(1)} %gather_fusion.4), channel_id=1, source_target_pairs={{0,14},{2,0},{4,2},{6,4},{8,6},{10,8},{12,10},{14,12},{1,15},{3,1}... | collective-permute-start | bytes 80 | tf_op jit(solution)/shard_map/ppermute | solution.py:13
  38.7 4.5 collective-permute-done.1
  43.2 6.7 %collective-permute-done.3 = s32[2,3]{1,0:T(2,128)S(1)} collective-permute-done((s32[2,3]{1,0:T(2,128)S(1)}, s32[2,3]{1,0:T(2,128)S(1)}, u32[]{:S(2)}, u32[]{:S(2)}) %collective-permute-start.3) | collective-permute-done | bytes 56 | tf_op jit(solution)/shard_map/ppermute | solution.py:13
  50.2 3.3 collective-permute-done.5
  53.5 5.4 %collective-permute-done.7 = s32[2,3]{1,0:T(2,128)S(1)} collective-permute-done((s32[2,3]{1,0:T(2,128)S(1)}, s32[2,3]{1,0:T(2,128)S(1)}, u32[]{:S(2)}, u32[]{:S(2)}) %collective-permute-start.7) | collective-permute-done | bytes 56 | tf_op jit(solution)/shard_map/ppermute | solution.py:13
  60.9 4.1 copy.139
  65.0 3.3 broadcast.376.clone
  68.3 167.8 %while.21 = (s32[]{:T(128)}, f32[16,128,768]{2,1,0:T(8,128)}, s32[16]{0:T(128)S(1)}, bf16[2,16,128,384]{3,2,0,1:T(8,128)(2,1)}, s32[2,16,3,1]{2,0,3,1:T(2,128)S(...) while((s32[]{:T(128)}, f32[16,128,768]{2,1,0:T(8,128)}, ...), condition=%wide.region_6.8_spmd, body=%wide.region_5.7_spmd.sunk | while | flops 155124864 | bytes 9442607 | solution.py:107
  70.7 2.3 gather_fusion
  165.1 2.3 gather_fusion
  175.6 2.3 gather_fusion
  196.5 2.3 gather_fusion
  207.0 2.3 gather_fusion
  217.5 2.3 gather_fusion
  243.2 6.4 %reduce-scatter.3.cloned.1.call-done = f32[16,128,384]{2,1,0:T(8,128)} async-done(((f32[16,128,768]{2,1,0:T(8,128)}), f32[16,128,384]{2,1,0:T(8,128)}) %reduce-scatter.3.cloned.1.call-update) | async-done | bytes 3145744 | tf_op jit(solution)/shard_map/reduce_scatter | solution.py:108
  254.1 4.5 collective-permute-start.16
  261.0 2.9 collective-permute-done.16
  263.9 5.2 %collective-permute-done.17 = bf16[2,128,384]{2,1,0:T(8,128)(2,1)S(1)} collective-permute-done((bf16[2,128,384]{2,1,0:T(8,128)(2,1)S(1)}, bf16[2,128,384]{2,1,0:T(8,128)(2,1)S(1)}, u32[]{:S(2)}, u32[]{:S(2)}) %collective-permute-start.17) | collective-permute-done | bytes 196640 | tf_op jit(solution)/shard_map/ppermute | solution.py:13
  269.1 3.6 collective-permute-done.19
  274.5 3.3 broadcast.376
  277.9 167.6 %while.22 = (s32[]{:T(128)}, f32[16,128,768]{2,1,0:T(8,128)}, s32[16]{0:T(128)S(1)}, bf16[2,16,128,384]{3,2,0,1:T(8,128)(2,1)}, s32[2,16,3,1]{2,0,3,1:T(2,128)S(...) while((s32[]{:T(128)}, f32[16,128,768]{2,1,0:T(8,128)}, ...), condition=%wide.region_9.11_spmd, body=%wide.region_8.10_spmd.sunk | while | flops 155124864 | bytes 9442607 | solution.py:107
  290.7 2.3 gather_fusion.2
  301.2 2.3 gather_fusion.2
  343.1 2.3 gather_fusion.2
  374.5 2.3 gather_fusion.2
  385.0 2.3 gather_fusion.2
  405.9 2.3 gather_fusion.2
  445.5 15.8 %reduce-scatter.5.cloned.1.call-done = f32[16,128,384]{2,1,0:T(8,128)} async-done(((f32[16,128,768]{2,1,0:T(8,128)}), f32[16,128,384]{2,1,0:T(8,128)}) %reduce-scatter.5.cloned.1.call-update) | async-done | bytes 3145744 | tf_op jit(solution)/shard_map/reduce_scatter | solution.py:108
  461.3 3.6 subtract_convert_fusion
  (537 shorter events, 286.8 us)
Async XLA Ops:
  6.5 19.1 %copy-start.1 = (bf16[16,128,384]{2,1,0:T(8,128)(2,1)S(1)}, bf16[16,128,384]{2,1,0:T(8,128)(2,1)}, u32[]{:S(2)}) copy-start(bf16[16,128,384]{2,1,0:T(8,128)(2,1)} %param.9) | copy-start | bytes 4718596
  6.5 52.4 %copy-start.2 = (s32[16,3]{0,1:T(4,128)S(1)}, s32[16,3]{0,1:T(4,128)}, u32[]{:S(2)}) copy-start(s32[16,3]{0,1:T(4,128)} %param.10) | copy-start | bytes 580
  6.5 54.4 %all-gather.7.cloned.1.call-start = ((), (), s32[]{:S(2)}) async-start(), calls=%async_computation.4 | async-start | bytes 4718592 | tf_op jit(solution)/shard_map/all_gather | solution.py:66
  7.3 242.3 %reduce-scatter.3.cloned.1.call-start = ((), (), s32[]{:S(2)}) async-start(), calls=%async_computation.2 | async-start | bytes 9437184 | tf_op jit(solution)/shard_map/reduce_scatter | solution.py:108
  10.6 13.0 %collective-permute-start = (s32[2]{0:T(128)S(1)}, s32[2]{0:T(128)S(1)}, u32[]{:S(2)}, u32[]{:S(2)}) collective-permute-start(s32[2]{0:T(128)S(1)} %get-tuple-element.199), channel_id=1, source_target_pairs={{0,2},{2,4},{4,6},{6,8},{8,10},{10,12},{12,14},{14,0},{1,3},{3,5},... | collective-permute-start | bytes 32 | tf_op jit(solution)/shard_map/ppermute | solution.py:13
  13.5 10.1 %collective-permute-start.2 = (s32[2]{0:T(128)S(1)}, s32[2]{0:T(128)S(1)}, u32[]{:S(2)}, u32[]{:S(2)}) collective-permute-start(s32[2]{0:T(128)S(1)} %get-tuple-element.202), channel_id=1, source_target_pairs={{0,14},{2,0},{4,2},{6,4},{8,6},{10,8},{12,10},{14,12},{1,15},{3,1}... | collective-permute-start | bytes 32 | tf_op jit(solution)/shard_map/ppermute | solution.py:13
  16.6 10.8 %collective-permute-start.4 = (s32[2]{0:T(128)S(1)}, s32[2]{0:T(128)S(1)}, u32[]{:S(2)}, u32[]{:S(2)}) collective-permute-start(s32[2]{0:T(128)S(1)} %get-tuple-element.201), channel_id=1, source_target_pairs={{0,4},{2,6},{4,8},{6,10},{8,12},{10,14},{12,0},{14,2},{1,5},{3,7},... | collective-permute-start | bytes 32 | tf_op jit(solution)/shard_map/ppermute | solution.py:13
  16.6 10.8 %collective-permute-start.6 = (s32[2]{0:T(128)S(1)}, s32[2]{0:T(128)S(1)}, u32[]{:S(2)}, u32[]{:S(2)}) collective-permute-start(s32[2]{0:T(128)S(1)} %get-tuple-element.200), channel_id=1, source_target_pairs={{0,12},{2,14},{4,0},{6,2},{8,4},{10,6},{12,8},{14,10},{1,13},{3,15... | collective-permute-start | bytes 32 | tf_op jit(solution)/shard_map/ppermute | solution.py:13
  29.7 29.4 %collective-permute-start.8 = (bf16[2,128,384]{2,1,0:T(8,128)(2,1)S(1)}, bf16[2,128,384]{2,1,0:T(8,128)(2,1)S(1)}, u32[]{:S(2)}, u32[]{:S(2)}) collective-permute-start(bf16[2,128,384]{2,1,0:T(8,128)(2,1)S(1)} %gather_fusion.8), channel_id=1, source_target_pairs={{0,14},{2,0},{4,2},{6,4},{8,6},{10,8},{12,10},{14,12},{1,15},{3,1}... | collective-permute-start | bytes 589832 | tf_op jit(solution)/shard_map/ppermute | solution.py:13
  30.1 29.0 %collective-permute-start.9 = (bf16[2,128,384]{2,1,0:T(8,128)(2,1)S(1)}, bf16[2,128,384]{2,1,0:T(8,128)(2,1)S(1)}, u32[]{:S(2)}, u32[]{:S(2)}) collective-permute-start(bf16[2,128,384]{2,1,0:T(8,128)(2,1)S(1)} %gather_fusion.9), channel_id=1, source_target_pairs={{0,2},{2,4},{4,6},{6,8},{8,10},{10,12},{12,14},{14,0},{1,3},{3,5},... | collective-permute-start | bytes 589832 | tf_op jit(solution)/shard_map/ppermute | solution.py:13
  31.8 27.3 %collective-permute-start.10 = (bf16[2,128,384]{2,1,0:T(8,128)(2,1)S(1)}, bf16[2,128,384]{2,1,0:T(8,128)(2,1)S(1)}, u32[]{:S(2)}, u32[]{:S(2)}) collective-permute-start(bf16[2,128,384]{2,1,0:T(8,128)(2,1)S(1)} %gather_fusion.10), channel_id=1, source_target_pairs={{0,12},{2,14},{4,0},{6,2},{8,4},{10,6},{12,8},{14,10},{1,13},{3,15... | collective-permute-start | bytes 589832 | tf_op jit(solution)/shard_map/ppermute | solution.py:13
  32.0 27.1 %collective-permute-start.11 = (bf16[2,128,384]{2,1,0:T(8,128)(2,1)S(1)}, bf16[2,128,384]{2,1,0:T(8,128)(2,1)S(1)}, u32[]{:S(2)}, u32[]{:S(2)}) collective-permute-start(bf16[2,128,384]{2,1,0:T(8,128)(2,1)S(1)} %gather_fusion.11), channel_id=1, source_target_pairs={{0,4},{2,6},{4,8},{6,10},{8,12},{10,14},{12,0},{14,2},{1,5},{3,7},... | collective-permute-start | bytes 589832 | tf_op jit(solution)/shard_map/ppermute | solution.py:13
  33.8 9.4 %collective-permute-start.1 = (s32[2,3]{1,0:T(2,128)S(1)}, s32[2,3]{1,0:T(2,128)S(1)}, u32[]{:S(2)}, u32[]{:S(2)}) collective-permute-start(s32[2,3]{1,0:T(2,128)S(1)} %gather_fusion.4), channel_id=1, source_target_pairs={{0,14},{2,0},{4,2},{6,4},{8,6},{10,8},{12,10},{14,12},{1,15},{3,1}... | collective-permute-start | bytes 80 | tf_op jit(solution)/shard_map/ppermute | solution.py:13
  43.2 6.7 %collective-permute-start.3 = (s32[2,3]{1,0:T(2,128)S(1)}, s32[2,3]{1,0:T(2,128)S(1)}, u32[]{:S(2)}, u32[]{:S(2)}) collective-permute-start(s32[2,3]{1,0:T(2,128)S(1)} %gather_fusion.5), channel_id=1, source_target_pairs={{0,2},{2,4},{4,6},{6,8},{8,10},{10,12},{12,14},{14,0},{1,3},{3,5},... | collective-permute-start | bytes 80 | tf_op jit(solution)/shard_map/ppermute | solution.py:13
  49.9 3.6 collective-permute-start.5
  53.5 5.4 %collective-permute-start.7 = (s32[2,3]{1,0:T(2,128)S(1)}, s32[2,3]{1,0:T(2,128)S(1)}, u32[]{:S(2)}, u32[]{:S(2)}) collective-permute-start(s32[2,3]{1,0:T(2,128)S(1)} %gather_fusion.7), channel_id=1, source_target_pairs={{0,4},{2,6},{4,8},{6,10},{8,12},{10,14},{12,0},{14,2},{1,5},{3,7},... | collective-permute-start | bytes 80 | tf_op jit(solution)/shard_map/ppermute | solution.py:13
  236.1 0.7 copy-start.3
  236.1 225.2 %reduce-scatter.5.cloned.1.call-start = ((), (), s32[]{:S(2)}) async-start(), calls=%async_computation.3 | async-start | bytes 9437184 | tf_op jit(solution)/shard_map/reduce_scatter | solution.py:108
  239.1 19.5 %collective-permute-start.12 = (s32[2,3]{1,0:T(2,128)S(1)}, s32[2,3]{1,0:T(2,128)S(1)}, u32[]{:S(2)}, u32[]{:S(2)}) collective-permute-start(s32[2,3]{1,0:T(2,128)S(1)} %gather_fusion.12), channel_id=1, source_target_pairs={{0,14},{2,0},{4,2},{6,4},{8,6},{10,8},{12,10},{14,12},{1,15},{3,1}... | collective-permute-start | bytes 80 | tf_op jit(solution)/shard_map/ppermute | solution.py:13
  241.2 17.4 %collective-permute-start.13 = (s32[2,3]{1,0:T(2,128)S(1)}, s32[2,3]{1,0:T(2,128)S(1)}, u32[]{:S(2)}, u32[]{:S(2)}) collective-permute-start(s32[2,3]{1,0:T(2,128)S(1)} %gather_fusion.13), channel_id=1, source_target_pairs={{0,2},{2,4},{4,6},{6,8},{8,10},{10,12},{12,14},{14,0},{1,3},{3,5},... | collective-permute-start | bytes 80 | tf_op jit(solution)/shard_map/ppermute | solution.py:13
  241.2 18.5 %collective-permute-start.14 = (s32[2,3]{1,0:T(2,128)S(1)}, s32[2,3]{1,0:T(2,128)S(1)}, u32[]{:S(2)}, u32[]{:S(2)}) collective-permute-start(s32[2,3]{1,0:T(2,128)S(1)} %gather_fusion.14), channel_id=1, source_target_pairs={{0,12},{2,14},{4,0},{6,2},{8,4},{10,6},{12,8},{14,10},{1,13},{3,15... | collective-permute-start | bytes 80 | tf_op jit(solution)/shard_map/ppermute | solution.py:13
  241.8 18.9 %collective-permute-start.15 = (s32[2,3]{1,0:T(2,128)S(1)}, s32[2,3]{1,0:T(2,128)S(1)}, u32[]{:S(2)}, u32[]{:S(2)}) collective-permute-start(s32[2,3]{1,0:T(2,128)S(1)} %gather_fusion.15), channel_id=1, source_target_pairs={{0,4},{2,6},{4,8},{6,10},{8,12},{10,14},{12,0},{14,2},{1,5},{3,7},... | collective-permute-start | bytes 80 | tf_op jit(solution)/shard_map/ppermute | solution.py:13
  254.1 9.8 %collective-permute-start.16 = (bf16[2,128,384]{2,1,0:T(8,128)(2,1)S(1)}, bf16[2,128,384]{2,1,0:T(8,128)(2,1)S(1)}, u32[]{:S(2)}, u32[]{:S(2)}) collective-permute-start(bf16[2,128,384]{2,1,0:T(8,128)(2,1)S(1)} %gather_fusion.16), channel_id=1, source_target_pairs={{0,14},{2,0},{4,2},{6,4},{8,6},{10,8},{12,10},{14,12},{1,15},{3,1}... | collective-permute-start | bytes 589832 | tf_op jit(solution)/shard_map/ppermute | solution.py:13
  258.6 10.5 %collective-permute-start.17 = (bf16[2,128,384]{2,1,0:T(8,128)(2,1)S(1)}, bf16[2,128,384]{2,1,0:T(8,128)(2,1)S(1)}, u32[]{:S(2)}, u32[]{:S(2)}) collective-permute-start(bf16[2,128,384]{2,1,0:T(8,128)(2,1)S(1)} %gather_fusion.17), channel_id=1, source_target_pairs={{0,2},{2,4},{4,6},{6,8},{8,10},{10,12},{12,14},{14,0},{1,3},{3,5},... | collective-permute-start | bytes 589832 | tf_op jit(solution)/shard_map/ppermute | solution.py:13
  258.6 10.5 %collective-permute-start.18 = (bf16[2,128,384]{2,1,0:T(8,128)(2,1)S(1)}, bf16[2,128,384]{2,1,0:T(8,128)(2,1)S(1)}, u32[]{:S(2)}, u32[]{:S(2)}) collective-permute-start(bf16[2,128,384]{2,1,0:T(8,128)(2,1)S(1)} %gather_fusion.18), channel_id=1, source_target_pairs={{0,12},{2,14},{4,0},{6,2},{8,4},{10,6},{12,8},{14,10},{1,13},{3,15... | collective-permute-start | bytes 589832 | tf_op jit(solution)/shard_map/ppermute | solution.py:13
  259.7 13.0 %collective-permute-start.19 = (bf16[2,128,384]{2,1,0:T(8,128)(2,1)S(1)}, bf16[2,128,384]{2,1,0:T(8,128)(2,1)S(1)}, u32[]{:S(2)}, u32[]{:S(2)}) collective-permute-start(bf16[2,128,384]{2,1,0:T(8,128)(2,1)S(1)} %gather_fusion.19), channel_id=1, source_target_pairs={{0,4},{2,6},{4,8},{6,10},{8,12},{10,14},{12,0},{14,2},{1,5},{3,7},... | collective-permute-start | bytes 589832 | tf_op jit(solution)/shard_map/ppermute | solution.py:13
  445.5 15.8 %copy-start = (f32[16,128,384]{2,1,0:T(8,128)S(1)}, f32[16,128,384]{2,1,0:T(8,128)}, u32[]{:S(2)}) copy-start(f32[16,128,384]{2,1,0:T(8,128)} %reduce-scatter.3.cloned.1.call-done) | copy-start | bytes 9437188
Sparse Core Ops, SparseCore 0:
  8.9 14.8 all-gather.6
  236.3 13.2 reduce-scatter.2
  445.6 15.6 reduce-scatter.4
where the time goes:
time: 474 us; the launch traced here: 471 us
  local copies, waits for them, and re-layouts  214 us (45%)
  matrix products  88.8 us (19%)
  loops' own time  55.9 us (12%)
  waiting for transfers between devices  54.5 us (11%)
  starting transfers between devices  29.9 us (6%)
  between operations  13.4 us (3%)
  other arithmetic  11 us (2%)
    gather x64, local copies, waits for them, and re-layouts, row_terms(): table[index].reshape(groups, half_width, halves, edge, half_width, edge)  84.9 us
    dot_general x32, matrix products, row_terms(): jnp.einsum('gxk,gkn->xn', left_half, selected, preferred_element_type=jnp...  64.6 us
    another operation x2, loops' own time, product(): terms = lax.map(one_row, row_list)  55.9 us
    reshape x32, local copies, waits for them, and re-layouts, row_terms(): selected = selected.reshape(groups, half_width * edge, count_out * edge)  44.8 us
    ppermute x20, waiting for transfers between devices, from_behind(): return lax.ppermute(value, axis, pairs)  31.6 us
    ppermute x20, starting transfers between devices, from_behind(): return lax.ppermute(value, axis, pairs)  29.8 us
    another operation x34, local copies, waits for them, and re-layouts  25 us
    dot_general x32, matrix products, row_terms(): jnp.einsum('gjhycz,gjhcs->gjysz', right_rows, matched, preferred_element_...  24.2 us
  transfers between devices with their start and end apart: 23, of which 9 were waited for; matrix products, arithmetic and copies ran while one was open for 4% of the time, Pallas kernels for 0%

commit v1 on v0

v1 whole, which is shorter than its diff:
```python
import functools

import jax
import jax.numpy as jnp
from jax import lax
from jax.experimental import pallas as pl
from jax.experimental.pallas import tpu as pltpu
from jax.sharding import PartitionSpec as P

CAP = 2
REACH = 2
OFFSETS = tuple(step for reach in range(1, REACH + 1) for step in (reach, -reach))
VMEM_LIMIT = 24 * 1024 * 1024


def from_ahead(value, steps):
    count = lax.axis_size("rows")
    pairs = [(source, (source - steps) % count) for source in range(count)]
    return lax.ppermute(value, "rows", pairs)


def from_sibling(value):
    return lax.ppermute(value, "layers", [(0, 1), (1, 0)])


def named_rows(columns, owner, block_rows):
    local = columns.reshape(-1) - owner * block_rows
    inside = (local >= 0) & (local < block_rows)
    low = jnp.min(jnp.where(inside, local, block_rows - 1))
    high = jnp.max(jnp.where(inside, local, 0))
    return jnp.stack([low, high]).astype(jnp.int32)


def pick_rows(table, rows):
    hit = rows[:, None, None] == jnp.arange(table.shape[0], dtype=jnp.int32)[None, :, None]
    return jnp.sum(jnp.where(hit, table[None], 0), axis=1)


def block_index(columns, targets, right_cols, slots, half, segments):
    rows, width = columns.shape
    entries = jnp.arange(right_cols.shape[0], dtype=jnp.int32)
    hit = slots[:, :, None] == entries[None, None, :]
    met = jnp.sum(jnp.where(hit[..., None], right_cols[None, None], 0), axis=2)
    own = rows
    far = right_cols.shape[0] - rows
    base = jnp.where(slots < own, slots, slots + own)
    shift = jnp.where(slots < own, own, far)
    empty = segments - 1
    terms = []
    for b in range(width):
        where_b = (b % half) * segments + base + (shift if b >= half else 0)
        terms.append(
            jnp.where(
                met[:, :, b, None] == targets[:, None, :],
                where_b[:, :, None] - empty,
                0,
            )
        )
    return (sum(terms) + empty).reshape(-1).astype(jnp.int32)


def fill(table, parts, sems, half, edge, segments, first):
    copies = []
    begin = 0
    for part in parts:
        size = part.shape[0]
        for b in range(half):
            copies.append(
                pltpu.make_async_copy(
                    part.at[:, :, pl.ds(b * edge, edge)],
                    table.at[pl.ds(b * segments + begin, size)],
                    sems.at[first + len(copies)],
                )
            )
        begin += size
    for copy in copies:
        copy.start()
    return copies


def gather_kernel(rows_ref, density_ref, *refs):
    outs, sems = refs[:-1], refs[-1]
    copies = []
    for position, out in enumerate(outs):
        for k in range(CAP):
            n = position * CAP + k
            copies.append(
                pltpu.make_async_copy(density_ref.at[rows_ref[n]], out.at[k], sems.at[n])
            )
    for copy in copies:
        copy.start()
    for copy in copies:
        copy.wait()


def gather(rows, density):
    piece = jax.ShapeDtypeStruct((CAP,) + density.shape[1:], density.dtype)
    return pl.pallas_call(
        gather_kernel,
        out_shape=[piece] * len(OFFSETS),
        in_specs=[pl.BlockSpec(memory_space=pltpu.SMEM), pl.BlockSpec(memory_space=pl.ANY)],
        out_specs=[pl.BlockSpec(memory_space=pl.ANY)] * len(OFFSETS),
        scratch_shapes=[pltpu.SemaphoreType.DMA((len(OFFSETS) * CAP,))],
        name="gather_rows",
    )(rows, density)


def row_product(table, index_ref, base, left, width, half, edge):
    total = None
    for a in range(0, width, 2):
        pair = range(a, min(a + 2, width))
        lhs = jnp.concatenate([left(k) for k in pair], axis=1)
        rhs = jnp.concatenate(
            [
                jnp.concatenate(
                    [table[index_ref[base + k * half + s]] for s in range(half)], axis=1
                )
                for k in pair
            ],
            axis=0,
        )
        term = jnp.dot(lhs, rhs, preferred_element_type=jnp.float32)
        total = term if total is None else total + term
    return total


def square_kernel(own, edge, half, segments, wanted, rows_ref, index_ref, *refs):
    parts = refs[: 2 + 2 * len(OFFSETS)]
    outs = refs[len(parts) : -2]
    table, sems = refs[-2:]
    copies = fill(table, parts, sems, half, edge, segments, 0)
    width = 2 * half
    for b in range(half):
        table[b * segments + segments - 1] = jnp.zeros((edge, edge), table.dtype)
    for copy in copies:
        copy.wait()

    def one(i, out, place):
        row = rows_ref[i] if wanted else i
        left = lambda k: table[(k % half) * segments + (k // half) * own + row]
        total = row_product(table, index_ref, row * (width * half), left, width, half, edge)
        out[place] = total.astype(out.dtype)

    if wanted:
        for position, out in enumerate(outs):
            for k in range(CAP):
                one(position * CAP + k, out, k)
    else:

        def body(i, carry):
            one(i, outs[0], i)
            return carry

        lax.fori_loop(0, own, body, 0, unroll=2)


def square(rows, index, parts, wanted):
    own, edge, wide = parts[0].shape
    half = wide // edge
    segments = 2 * own + 2 * len(OFFSETS) * CAP + 1
    if wanted:
        shapes = [jax.ShapeDtypeStruct((CAP, edge, wide), parts[0].dtype)] * len(OFFSETS)
        count = len(OFFSETS) * CAP
    else:
        shapes = [jax.ShapeDtypeStruct((own, edge, wide), parts[0].dtype)]
        count = own
    return pl.pallas_call(
        functools.partial(square_kernel, own, edge, half, segments, wanted),
        out_shape=shapes,
        in_specs=[pl.BlockSpec(memory_space=pltpu.SMEM)] * 2
        + [pl.BlockSpec(memory_space=pl.ANY)] * len(parts),
        out_specs=[pl.BlockSpec(memory_space=pltpu.VMEM)] * len(shapes),
        scratch_shapes=[
            pltpu.VMEM((half * segments, edge, edge), parts[0].dtype),
            pltpu.SemaphoreType.DMA((half * len(parts),)),
        ],
        compiler_params=pltpu.CompilerParams(vmem_limit_bytes=VMEM_LIMIT),
        cost_estimate=pl.CostEstimate(
            flops=count * 2 * edge * 2 * wide * wide,
            bytes_accessed=5 * 1024 * 1024,
            transcendentals=0,
        ),
        name="square_wanted" if wanted else "square_rows",
    )(rows, index, *parts)


def cube_kernel(own, edge, half, segments, index_ref, left_own, left_other, *refs):
    out, table, lefts, sems = refs[-4:]
    parts = refs[:-4]
    copies = fill(table, parts, sems, half, edge, segments, 0)
    copies += fill(lefts, (left_own, left_other), sems, half, edge, 2 * own, len(copies))
    width = 2 * half
    for b in range(half):
        table[b * segments + segments - 1] = jnp.zeros((edge, edge), table.dtype)
    for copy in copies:
        copy.wait()

    def body(i, carry):
        left = lambda k: lefts[(k % half) * (2 * own) + (k // half) * own + i]
        total = row_product(table, index_ref, i * (width * half), left, width, half, edge)
        first = jnp.concatenate([table[s * segments + i] for s in range(half)], axis=1)
        out[i] = (3.0 * first.astype(jnp.float32) - 2.0 * total).astype(out.dtype)
        return carry

    lax.fori_loop(0, own, body, 0, unroll=2)


def cube(index, left_own, left_other, parts):
    own, edge, wide = left_own.shape
    half = wide // edge
    segments = 2 * own + 2 * len(OFFSETS) * CAP + 1
    return pl.pallas_call(
        functools.partial(cube_kernel, own, edge, half, segments),
        out_shape=jax.ShapeDtypeStruct(left_own.shape, left_own.dtype),
        in_specs=[pl.BlockSpec(memory_space=pltpu.SMEM)]
        + [pl.BlockSpec(memory_space=pl.ANY)] * (len(parts) + 2),
        out_specs=pl.BlockSpec(memory_space=pltpu.VMEM),
        scratch_shapes=[
            pltpu.VMEM((half * segments, edge, edge), left_own.dtype),
            pltpu.VMEM((half * 2 * own, edge, edge), left_own.dtype),
            pltpu.SemaphoreType.DMA((half * (len(parts) + 2),)),
        ],
        compiler_params=pltpu.CompilerParams(vmem_limit_bytes=VMEM_LIMIT),
        cost_estimate=pl.CostEstimate(
            flops=own * 2 * edge * 2 * wide * wide,
            bytes_accessed=9 * 1024 * 1024,
            transcendentals=0,
        ),
        name="cube_rows",
    )(index, left_own, left_other, *parts)


def local(density, columns, kept):
    own, edge, wide = density.shape
    half = columns.shape[1]
    peers = lax.axis_size("rows")
    me = lax.axis_index("rows")

    numbers = jnp.concatenate([columns, kept], axis=1)
    other_numbers = from_sibling(numbers)
    all_columns = jnp.concatenate([columns, other_numbers[:, :half]], axis=1)
    all_kept = jnp.concatenate([kept, other_numbers[:, half:]], axis=1)
    all_numbers = jnp.concatenate([all_columns, all_kept], axis=1)
    near = {step: from_ahead(all_numbers, step) for step in OFFSETS}
    other_density = from_sibling(density)

    width = 2 * half
    sends = jnp.concatenate([named_rows(near[-step][:, :width], me, own) for step in OFFSETS])
    wants = [named_rows(all_columns, (me + step) % peers, own) for step in OFFSETS]

    got = [
        from_ahead(piece, step)
        for step, piece in zip(OFFSETS, gather(sends, density))
    ]
    got_other = [from_sibling(piece) for piece in got]

    owner = all_columns // own
    distance = (owner - me) % peers
    slots = all_columns - me * own
    for position, (step, want) in enumerate(zip(OFFSETS, wants)):
        local_row = all_columns - ((me + step) % peers) * own
        slots = jnp.where(
            distance == step % peers,
            own + position * CAP + (local_row != want[0]).astype(jnp.int32),
            slots,
        )
    far = jnp.concatenate(
        [pick_rows(near[step], want) for step, want in zip(OFFSETS, wants)], axis=0
    )
    segments = 2 * own + 2 * len(OFFSETS) * CAP + 1
    square_index = block_index(
        all_columns, kept, jnp.concatenate([all_columns, far[:, :width]]), slots, half, segments
    )
    cube_index = block_index(
        all_columns, kept, jnp.concatenate([all_kept, far[:, width:]]), slots, half, segments
    )

    parts = [density, other_density, *got, *got_other]
    wanted = square(sends, square_index, parts, True)
    got_square = [from_ahead(piece, step) for step, piece in zip(OFFSETS, wanted)]
    (squares,) = square(sends, square_index, parts, False)
    other_squares = from_sibling(squares)
    got_square_other = [from_sibling(piece) for piece in got_square]
    return cube(
        cube_index,
        density,
        other_density,
        [squares, other_squares, *got_square, *got_square_other],
    )


def solution(mesh):
    in_specs = (
        P(("groups", "rows"), None, "layers"),
        P(("groups", "rows"), "layers"),
        P(("groups", "rows"), "layers"),
    )
    out_specs = P(("groups", "rows"), None, "layers")
    return jax.shard_map(local, mesh=mesh, in_specs=in_specs, out_specs=out_specs, check_vma=False)
```

time: 474 us -> 127 us (0.27)
  local copies, waits for them, and re-layouts: 214 us -> 25.5 us
  matrix products: 88.8 us -> 0 us
  loops' own time: 55.9 us -> 0 us
  Pallas kernels: 0 us -> 43.3 us
  waiting for transfers between devices: 54.5 us -> 13.2 us
  between operations: 13.4 us -> 0.2 us
  other arithmetic: 11 us -> 20.2 us
  starting transfers between devices: 29.9 us -> 23 us
    gather x112 -> x0, local copies, waits for them, and re-layouts: 113 us -> none  [the longest x64 84.9 us: row_terms(): table[index].reshape(groups, half_width, halves, edge, half_width, edge)]
    dot_general x64 -> x0, matrix products: 88.8 us -> none  [the longest x32 64.6 us: row_terms(): jnp.einsum('gxk,gkn->xn', left_half, selected, preferred_element_type=jnp...]
    another operation x2 -> x0, loops' own time: 55.9 us -> none  [product(): terms = lax.map(one_row, row_list)]
    reshape x35 -> x0, local copies, waits for them, and re-layouts: 45.1 us -> none  [the longest x32 44.8 us: row_terms(): selected = selected.reshape(groups, half_width * edge, count_out * edge)]
    pallas_call x0 -> x4, Pallas kernels: none -> 43.3 us  [the longest x1 25.8 us: gather(): pl.pallas_call(gather_kernel, out_shape=[piece] * len(OFFSETS), in_specs=...]
    another operation x34 -> x0, local copies, waits for them, and re-layouts: 25 us -> none
    reduce_scatter x2 -> x0, waiting for transfers between devices: 22.2 us -> none  [product(): return lax.psum_scatter(terms, 'layers', scatter_dimension=2, tiled=True)]
    dynamic_slice x64 -> x0, local copies, waits for them, and re-layouts: 18.8 us -> none  [the longest x32 18.5 us: product(): terms = lax.map(one_row, row_list)]
  transfers between devices with their start and end apart: 23 -> 23, of which waited for: 9 -> 5; matrix products, arithmetic and copies ran while one was open for 4% -> 36% of each run, Pallas kernels for 0% -> 24%
where the time goes in v1:
time: 127 us; the launch traced here: 125 us
  Pallas kernels  43.3 us (34%)
  local copies, waits for them, and re-layouts  25.5 us (20%)
  starting transfers between devices  23 us (18%)
  other arithmetic  20.2 us (16%)
  waiting for transfers between devices  13.2 us (10%)
    pallas_call x1, Pallas kernels, gather(): pl.pallas_call(gather_kernel, out_shape=[piece] * len(OFFSETS), in_specs=...  25.8 us
    ppermute x12, starting transfers between devices, from_ahead(): return lax.ppermute(value, 'rows', pairs)  20.8 us
    ppermute x12, waiting for transfers between devices, from_ahead(): return lax.ppermute(value, 'rows', pairs)  12.7 us
    eq x12, local copies, waits for them, and re-layouts, block_index(): met[:, :, b, None] == targets[:, None, :]  11.4 us
    pallas_call x2, Pallas kernels, square(): pl.pallas_call(functools.partial(square_kernel, own, edge, half, segments...  10.5 us
    pallas_call x1, Pallas kernels, cube(): pl.pallas_call(functools.partial(cube_kernel, own, edge, half, segments),...  7.04 us
    concatenate x1, local copies, waits for them, and re-layouts, local(): jnp.concatenate([named_rows(near[-step][:, :width], me, own) for step in...  5.62 us
    another operation x4, other arithmetic, named_rows(): return jnp.stack([low, high]).astype(jnp.int32)  5.23 us
  transfers between devices with their start and end apart: 23, of which 5 were waited for; matrix products, arithmetic and copies ran while one was open for 36% of the time, Pallas kernels for 24%

profile of v1, /device:TPU:0, one launch (start us, length us, event | category | flops | bytes accessed | tf_op | source)
XLA Modules:
  0.0 125.4 jit_solution(7274821164679021914)
XLA Ops:
  2.1 1.5 %select_reduce_fusion.17 = (s32[]{:T(128)}, s32[]{:T(128)}, s32[]{:T(128)}, s32[]{:T(128)}, s32[]{:T(128)}, /*index=5*/s32[]{:T(128)}, s32[]{:T(128)}, s32[]{:T(128)}) fusion(s32[]{:T(128)S(6)} %mul.26, s32[16,3]{0,1:T(4,128)S(1)} %get-tuple-element.62, s32[16,3]{0,1:T(4,128)} %param.4, s32[]{:T(128)S(6)} %mul.12, s32[]{:T(128)S(6)} %mul.10, s32[]{:T(128)S(6)} %mul.11), kind=kLoop, calls=%fused_computation.47 | loop fusion | flops 3160 | bytes 432 | tf_op jit(solution)/shard_map/reduce_max | solution.py:30
  3.6 3.1 %broadcast_add_fusion.1 = (s32[16,6]{0,1:T(8,128)S(1)}, s32[16,6]{0,1:T(8,128)S(1)}) fusion(s32[]{:T(128)S(6)} %mul.27, s32[]{:T(128)} %get-tuple-element.63, s32[]{:T(128)S(6)} %mul.26, s32[]{:T(128)} %get-tuple-element.35, s32[]{:T(128)S(6)} %mul.12, s32[]{:T(128)} %get-tuple-element.36, s32[]{:T(128)S(6)} %mul.11, s32[]{:T(128)} %get-tuple-element.37, ...), kind=kLoop, calls=%fused_computation.64 | loop fusion | flops 5472 | bytes 1192 | tf_op jit(solution)/shard_map/sub | solution.py:55
  7.5 3.1 %collective-permute-start.4 = (s32[16,12]{0,1:T(8,128)S(1)}, s32[16,12]{0,1:T(8,128)S(1)}, u32[]{:S(2)}, u32[]{:S(2)}) collective-permute-start(s32[16,12]{0,1:T(8,128)S(1)} %pad_add_fusion), channel_id=1, source_target_pairs={{0,4},{2,6},{4,8},{6,10},{8,12},{10,14},{12,0},{14,2},{1,5},{3,7},... | collective-permute-start | bytes 2312 | tf_op jit(solution)/shard_map/ppermute | solution.py:19
  10.6 2.1 %collective-permute-start.3 = (s32[16,12]{0,1:T(8,128)S(1)}, s32[16,12]{0,1:T(8,128)S(1)}, u32[]{:S(2)}, u32[]{:S(2)}) collective-permute-start(s32[16,12]{0,1:T(8,128)S(1)} %pad_add_fusion), channel_id=1, source_target_pairs={{0,12},{2,14},{4,0},{6,2},{8,4},{10,6},{12,8},{14,10},{1,13},{3,15... | collective-permute-start | bytes 2312 | tf_op jit(solution)/shard_map/ppermute | solution.py:19
  12.7 1.7 %collective-permute-start.2 = (s32[16,12]{0,1:T(8,128)S(1)}, s32[16,12]{0,1:T(8,128)S(1)}, u32[]{:S(2)}, u32[]{:S(2)}) collective-permute-start(s32[16,12]{0,1:T(8,128)S(1)} %pad_add_fusion), channel_id=1, source_target_pairs={{0,2},{2,4},{4,6},{6,8},{8,10},{10,12},{12,14},{14,0},{1,3},{3,5},... | collective-permute-start | bytes 2312 | tf_op jit(solution)/shard_map/ppermute | solution.py:19
  14.3 3.0 %collective-permute-start.1 = (s32[16,12]{0,1:T(8,128)S(1)}, s32[16,12]{0,1:T(8,128)S(1)}, u32[]{:S(2)}, u32[]{:S(2)}) collective-permute-start(s32[16,12]{0,1:T(8,128)S(1)} %pad_add_fusion), channel_id=1, source_target_pairs={{0,14},{2,0},{4,2},{6,4},{8,6},{10,8},{12,10},{14,12},{1,15},{3,1}... | collective-permute-start | bytes 2312 | tf_op jit(solution)/shard_map/ppermute | solution.py:19
  17.4 1.3 %pad_add_fusion.6 = s32[2]{0:T(128)S(1)} fusion(s32[1]{0:T(128)} %bitcast.1, s32[1]{0:T(128)} %bitcast), kind=kLoop, calls=%fused_computation.71 | loop fusion | flops 2 | bytes 16 | tf_op jit(solution)/shard_map/stack | solution.py:31
  18.7 1.4 %pad_add_fusion.7 = s32[2]{0:T(128)S(1)} fusion(s32[1]{0:T(128)} %bitcast.3, s32[1]{0:T(128)} %bitcast.2), kind=kLoop, calls=%fused_computation.72 | loop fusion | flops 2 | bytes 16 | tf_op jit(solution)/shard_map/stack | solution.py:31
  20.2 1.2 pad_add_fusion.9
  21.5 1.3 %pad_add_fusion.8 = s32[2]{0:T(128)S(1)} fusion(s32[1]{0:T(128)} %bitcast.5, s32[1]{0:T(128)} %bitcast.4), kind=kLoop, calls=%fused_computation.73 | loop fusion | flops 2 | bytes 16 | tf_op jit(solution)/shard_map/stack | solution.py:31
  29.0 1.9 %select_reduce_fusion = (s32[16,6,6]{0,2,1:T(8,128)S(1)}, s32[16,6,6]{0,2,1:T(8,128)}) fusion(s32[24,6]{0,1:T(8,128)S(1)} %get-tuple-element.65, pred[16,6,24]{2,0,1:T(8,128)(4,1)S(1)} %iota_compare_fusion, s32[24,6]{0,1:T(8,128)S(1)} %get-tuple-element.64), kind=kLoop, calls=%fused_computation | loop fusion | flops 54144 | bytes 8064 | tf_op jit(solution)/shard_map/reduce_sum | solution.py:43
  37.7 5.6 %concatenate.173.rows_ref = s32[8]{0:T(128)} concatenate(s32[1]{0:T(128)} %bitcast.14, s32[1]{0:T(128)} %bitcast.15, s32[1]{0:T(128)} %bitcast.16, s32[1]{0:T(128)} %bitcast.17, s32[1]{0:T(128)} %bitcast.18, s32[1]{0:T(128)} %bitcast.19, s32[1]{0:T(128)} %bitcast.20, s32[1]{0:T(128)} %bitcast.21), dimensions={0} | concatenate | bytes 64 | tf_op jit(solution)/shard_map/concatenate | solution.py:248
  43.3 25.8 %gather_rows.1 = (bf16[2,128,384]{2,1,0:T(8,128)(2,1)}, bf16[2,128,384]{2,1,0:T(8,128)(2,1)}, bf16[2,128,384]{2,1,0:T(8,128)(2,1)}, bf16[2,128,384]{2,1,0:T(8,128)(2,1)}) custom-call(s32[8]{0:T(128)} %concatenate.173.rows_ref, bf16[16,128,384]{2,1,0:T(8,128)(2,1)} %left_own.1), custom_call_target="tpu_custom_call" | custom-call | tf_op jit(solution)/shard_map/gather_rows/pallas_call | solution.py:98
  69.4 1.8 %collective-permute-start.7 = (bf16[2,128,384]{2,1,0:T(8,128)(2,1)}, bf16[2,128,384]{2,1,0:T(8,128)(2,1)S(1)}, u32[]{:S(2)}, u32[]{:S(2)}) collective-permute-start(bf16[2,128,384]{2,1,0:T(8,128)(2,1)} %get-tuple-element.14), channel_id=1, source_target_pairs={{0,2},{2,4},{4,6},{6,8},{8,10},{10,12},{12,14},{14,0},{1,3},{3,5},... | collective-permute-start | bytes 589832 | tf_op jit(solution)/shard_map/ppermute | solution.py:19
  71.4 1.9 %collective-permute-start.9 = (bf16[2,128,384]{2,1,0:T(8,128)(2,1)}, bf16[2,128,384]{2,1,0:T(8,128)(2,1)}, u32[]{:S(2)}, u32[]{:S(2)}) collective-permute-start(bf16[2,128,384]{2,1,0:T(8,128)(2,1)} %get-tuple-element.16), channel_id=1, source_target_pairs={{0,4},{2,6},{4,8},{6,10},{8,12},{10,14},{12,0},{14,2},{1,5},{3,7},... | collective-permute-start | bytes 589832 | tf_op jit(solution)/shard_map/ppermute | solution.py:19
  73.2 1.6 %fusion.8 = (s32[16,6,1]{0,2,1:T(1,128)}, s32[16,6,1]{0,2,1:T(1,128)}, s32[16,6,1]{0,2,1:T(1,128)}, s32[16,6,1]{0,2,1:T(1,128)}, s32[16,6,1]{0,2,1:T(1,128)}, /*index=5*/s32[16,6,1]{0,2,1:T(1,128)S(1)}) fusion(s32[16,6,6]{0,2,1:T(8,128)} %get-tuple-element.22), kind=kLoop, calls=%fused_computation.76 | loop fusion | bytes 4608 | tf_op jit(solution)/shard_map/slice | solution.py:54
  74.8 1.4 %copy.75 = s32[16,6,1]{1,0,2:T(8,128)} copy(s32[16,6,1]{0,2,1:T(1,128)} %get-tuple-element.48) | data formatting | bytes 768 | tf_op jit(solution)/shard_map/eq | solution.py:54
  76.2 1.3 %copy.80 = s32[16,6,1]{1,0,2:T(8,128)} copy(s32[16,6,1]{0,2,1:T(1,128)} %get-tuple-element.49) | data formatting | bytes 768 | tf_op jit(solution)/shard_map/eq | solution.py:54
  77.5 1.3 %copy.79 = s32[16,6,1]{1,0,2:T(8,128)} copy(s32[16,6,1]{0,2,1:T(1,128)} %get-tuple-element.50) | data formatting | bytes 768 | tf_op jit(solution)/shard_map/eq | solution.py:54
  78.8 1.3 %copy.78 = s32[16,6,1]{1,0,2:T(8,128)} copy(s32[16,6,1]{0,2,1:T(1,128)} %get-tuple-element.51) | data formatting | bytes 768 | tf_op jit(solution)/shard_map/eq | solution.py:54
  80.2 1.4 %copy.77 = s32[16,6,1]{1,0,2:T(8,128)} copy(s32[16,6,1]{0,2,1:T(1,128)} %get-tuple-element.52) | data formatting | bytes 768 | tf_op jit(solution)/shard_map/eq | solution.py:54
  83.2 1.9 %add_add_fusion = (s32[16,6,3]{2,1,0:T(8,128)}, s32[16,6,3]{2,1,0:T(8,128)}) fusion(s32[16,6]{1,0:T(8,128)} %bitcast.29, s32[16,6]{1,0:T(8,128)} %bitcast.30, s32[16,6]{1,0:T(8,128)} %bitcast.31, s32[16,6]{1,0:T(8,128)} %bitcast.32, s32[16,6]{1,0:T(8,128)} %bitcast.33, s32[16,6]{1,0:T(8,128)} %bitcast.28, s32[16,6]{1,0:T(8,128)} %copy.68, s32[16,6]{1,0:T(8,128)} %copy.66, ...), kind=kLoop, calls=%fused_computation.2 | loop fusion | flops 10368 | bytes 9408 | tf_op jit(solution)/shard_map/add | solution.py:59
  85.1 1.0 reshape.722.index_ref
  86.2 6.8 %square_rows.1.refs_0_ = bf16[16,128,384]{2,1,0:T(8,128)(2,1)} custom-call(s32[8]{0:T(128)S(1)} %copy-done.1, s32[288]{0:T(512)S(1)} %reshape.722.index_ref, bf16[16,128,384]{2,1,0:T(8,128)(2,1)S(1)} %copy-done, bf16[16,128,384]{2,1,0:T(8,128)(2,1)S(1)} %collective-permute-done.5.refs_1_.left_other, bf16[2,128,384]{2,1,0:T(8,128)(2,1)S(1)} %collective-permute-done.6.refs_2_, ...), custom_call_target="tpu_custom_call" | custom-call | flops 1207959552 | bytes 5242880 | tf_op jit(solution)/shard_map/square_rows/pallas_call | solution.py:167
  93.1 3.7 %square_wanted.1 = (bf16[2,128,384]{2,1,0:T(8,128)(2,1)S(1)}, bf16[2,128,384]{2,1,0:T(8,128)(2,1)S(1)}, bf16[2,128,384]{2,1,0:T(8,128)(2,1)S(1)}, bf16[2,128,384]{2,1,0:T(8,128)(2,1)S(1)}) custom-call(s32[8]{0:T(128)S(1)} %copy-done.1, s32[288]{0:T(512)S(1)} %reshape.722.index_ref, bf16[16,128,384]{2,1,0:T(8,128)(2,1)S(1)} %copy-done, ...), custom_call_target="tpu_custom_call" | custom-call | flops 603979776 | bytes 5242880 | tf_op jit(solution)/shard_map/square_wanted/pallas_call | solution.py:167
  96.8 4.8 %collective-permute-start.15 = (bf16[2,128,384]{2,1,0:T(8,128)(2,1)S(1)}, bf16[2,128,384]{2,1,0:T(8,128)(2,1)S(1)}, u32[]{:S(2)}, u32[]{:S(2)}) collective-permute-start(bf16[2,128,384]{2,1,0:T(8,128)(2,1)S(1)} %get-tuple-element.17), channel_id=1, source_target_pairs={{0,14},{2,0},{4,2},{6,4},{8,6},{10,8},{12,10},{14,12},{1,15},{3,1}... | collective-permute-start | bytes 589832 | tf_op jit(solution)/shard_map/ppermute | solution.py:19
  102.2 1.4 %collective-permute-start.18 = (bf16[2,128,384]{2,1,0:T(8,128)(2,1)S(1)}, bf16[2,128,384]{2,1,0:T(8,128)(2,1)}, u32[]{:S(2)}, u32[]{:S(2)}) collective-permute-start(bf16[2,128,384]{2,1,0:T(8,128)(2,1)S(1)} %get-tuple-element.20), channel_id=1, source_target_pairs={{0,4},{2,6},{4,8},{6,10},{8,12},{10,14},{12,0},{14,2},{1,5},{3,7},... | collective-permute-start | bytes 589832 | tf_op jit(solution)/shard_map/ppermute | solution.py:19
  103.6 3.2 %collective-permute-done.15.refs_2_ = bf16[2,128,384]{2,1,0:T(8,128)(2,1)S(1)} collective-permute-done((bf16[2,128,384]{2,1,0:T(8,128)(2,1)S(1)}, bf16[2,128,384]{2,1,0:T(8,128)(2,1)S(1)}, u32[]{:S(2)}, u32[]{:S(2)}) %collective-permute-start.15) | collective-permute-done | bytes 196640 | tf_op jit(solution)/shard_map/ppermute | solution.py:19
  106.9 5.2 %collective-permute-done.16.refs_3_ = bf16[2,128,384]{2,1,0:T(8,128)(2,1)S(1)} collective-permute-done((bf16[2,128,384]{2,1,0:T(8,128)(2,1)S(1)}, bf16[2,128,384]{2,1,0:T(8,128)(2,1)S(1)}, u32[]{:S(2)}, u32[]{:S(2)}) %collective-permute-start.16) | collective-permute-done | bytes 196640 | tf_op jit(solution)/shard_map/ppermute | solution.py:19
  112.1 4.2 %collective-permute-done.17.refs_4_ = bf16[2,128,384]{2,1,0:T(8,128)(2,1)} collective-permute-done((bf16[2,128,384]{2,1,0:T(8,128)(2,1)S(1)}, bf16[2,128,384]{2,1,0:T(8,128)(2,1)}, u32[]{:S(2)}, u32[]{:S(2)}) %collective-permute-start.17) | collective-permute-done | bytes 196640 | tf_op jit(solution)/shard_map/ppermute | solution.py:19
  116.8 1.0 reshape.720.index_ref
  118.3 7.0 %cube_rows.1 = bf16[16,128,384]{2,1,0:T(8,128)(2,1)} custom-call(s32[288]{0:T(512)S(1)} %reshape.720.index_ref, bf16[16,128,384]{2,1,0:T(8,128)(2,1)S(1)} %copy-done, bf16[16,128,384]{2,1,0:T(8,128)(2,1)S(1)} %collective-permute-done.5.refs_1_.left_other, bf16[16,128,384]{2,1,0:T(8,128)(2,1)} %square_rows.1.refs_0_, ...), custom_call_target="tpu_custom_call" | custom-call | flops 1207959552 | bytes 9437184 | tf_op jit(solution)/shard_map/cube_rows/pallas_call | solution.py:212
  (74 shorter events, 20.0 us)
Async XLA Ops:
  0.0 86.2 %copy-start = (bf16[16,128,384]{2,1,0:T(8,128)(2,1)S(1)}, bf16[16,128,384]{2,1,0:T(8,128)(2,1)}, u32[]{:S(2)}) copy-start(bf16[16,128,384]{2,1,0:T(8,128)(2,1)} %left_own.1) | copy-start | bytes 4718596
  0.8 1.3 %collective-permute-start = (s32[16,6]{0,1:T(8,128)S(1)}, s32[16,6]{0,1:T(8,128)S(1)}, u32[]{:S(2)}, u32[]{:S(2)}) collective-permute-start(s32[16,6]{0,1:T(8,128)S(1)} %pad_add_fusion.2), channel_id=1, source_target_pairs={{0,1},{1,0},{2,3},{3,2},{4,5},{5,4},{6,7},{7,6},{8,9},{9,8},{10,11... | collective-permute-start | bytes 1160 | tf_op jit(solution)/shard_map/ppermute | solution.py:23
  1.3 84.9 %collective-permute-start.5 = (bf16[16,128,384]{2,1,0:T(8,128)(2,1)}, bf16[16,128,384]{2,1,0:T(8,128)(2,1)S(1)}, u32[]{:S(2)}, u32[]{:S(2)}) collective-permute-start(bf16[16,128,384]{2,1,0:T(8,128)(2,1)} %left_own.1), channel_id=1, source_target_pairs={{0,1},{1,0},{2,3},{3,2},{4,5},{5,4},{6,7},{7,6},{8,9},{9,8},{10,11... | collective-permute-start | bytes 4718600 | tf_op jit(solution)/shard_map/ppermute | solution.py:23
  7.5 19.4 %collective-permute-start.4 = (s32[16,12]{0,1:T(8,128)S(1)}, s32[16,12]{0,1:T(8,128)S(1)}, u32[]{:S(2)}, u32[]{:S(2)}) collective-permute-start(s32[16,12]{0,1:T(8,128)S(1)} %pad_add_fusion), channel_id=1, source_target_pairs={{0,4},{2,6},{4,8},{6,10},{8,12},{10,14},{12,0},{14,2},{1,5},{3,7},... | collective-permute-start | bytes 2312 | tf_op jit(solution)/shard_map/ppermute | solution.py:19
  10.6 16.7 %collective-permute-start.3 = (s32[16,12]{0,1:T(8,128)S(1)}, s32[16,12]{0,1:T(8,128)S(1)}, u32[]{:S(2)}, u32[]{:S(2)}) collective-permute-start(s32[16,12]{0,1:T(8,128)S(1)} %pad_add_fusion), channel_id=1, source_target_pairs={{0,12},{2,14},{4,0},{6,2},{8,4},{10,6},{12,8},{14,10},{1,13},{3,15... | collective-permute-start | bytes 2312 | tf_op jit(solution)/shard_map/ppermute | solution.py:19
  12.7 14.9 %collective-permute-start.2 = (s32[16,12]{0,1:T(8,128)S(1)}, s32[16,12]{0,1:T(8,128)S(1)}, u32[]{:S(2)}, u32[]{:S(2)}) collective-permute-start(s32[16,12]{0,1:T(8,128)S(1)} %pad_add_fusion), channel_id=1, source_target_pairs={{0,2},{2,4},{4,6},{6,8},{8,10},{10,12},{12,14},{14,0},{1,3},{3,5},... | collective-permute-start | bytes 2312 | tf_op jit(solution)/shard_map/ppermute | solution.py:19
  14.3 13.5 %collective-permute-start.1 = (s32[16,12]{0,1:T(8,128)S(1)}, s32[16,12]{0,1:T(8,128)S(1)}, u32[]{:S(2)}, u32[]{:S(2)}) collective-permute-start(s32[16,12]{0,1:T(8,128)S(1)} %pad_add_fusion), channel_id=1, source_target_pairs={{0,14},{2,0},{4,2},{6,4},{8,6},{10,8},{12,10},{14,12},{1,15},{3,1}... | collective-permute-start | bytes 2312 | tf_op jit(solution)/shard_map/ppermute | solution.py:19
  43.3 42.9 %copy-start.1 = (s32[8]{0:T(128)S(1)}, s32[8]{0:T(128)}, u32[]{:S(2)}) copy-start(s32[8]{0:T(128)} %concatenate.173.rows_ref) | copy-start | bytes 100
  69.1 13.1 %collective-permute-start.6 = (bf16[2,128,384]{2,1,0:T(8,128)(2,1)}, bf16[2,128,384]{2,1,0:T(8,128)(2,1)S(1)}, u32[]{:S(2)}, u32[]{:S(2)}) collective-permute-start(bf16[2,128,384]{2,1,0:T(8,128)(2,1)} %get-tuple-element.13), channel_id=1, source_target_pairs={{0,14},{2,0},{4,2},{6,4},{8,6},{10,8},{12,10},{14,12},{1,15},{3,1}... | collective-permute-start | bytes 589832 | tf_op jit(solution)/shard_map/ppermute | solution.py:19
  69.4 12.8 %collective-permute-start.7 = (bf16[2,128,384]{2,1,0:T(8,128)(2,1)}, bf16[2,128,384]{2,1,0:T(8,128)(2,1)S(1)}, u32[]{:S(2)}, u32[]{:S(2)}) collective-permute-start(bf16[2,128,384]{2,1,0:T(8,128)(2,1)} %get-tuple-element.14), channel_id=1, source_target_pairs={{0,2},{2,4},{4,6},{6,8},{8,10},{10,12},{12,14},{14,0},{1,3},{3,5},... | collective-permute-start | bytes 589832 | tf_op jit(solution)/shard_map/ppermute | solution.py:19
  71.2 11.5 %collective-permute-start.8 = (bf16[2,128,384]{2,1,0:T(8,128)(2,1)}, bf16[2,128,384]{2,1,0:T(8,128)(2,1)}, u32[]{:S(2)}, u32[]{:S(2)}) collective-permute-start(bf16[2,128,384]{2,1,0:T(8,128)(2,1)} %get-tuple-element.15), channel_id=1, source_target_pairs={{0,12},{2,14},{4,0},{6,2},{8,4},{10,6},{12,8},{14,10},{1,13},{3,15... | collective-permute-start | bytes 589832 | tf_op jit(solution)/shard_map/ppermute | solution.py:19
  71.4 11.4 %collective-permute-start.9 = (bf16[2,128,384]{2,1,0:T(8,128)(2,1)}, bf16[2,128,384]{2,1,0:T(8,128)(2,1)}, u32[]{:S(2)}, u32[]{:S(2)}) collective-permute-start(bf16[2,128,384]{2,1,0:T(8,128)(2,1)} %get-tuple-element.16), channel_id=1, source_target_pairs={{0,4},{2,6},{4,8},{6,10},{8,12},{10,14},{12,0},{14,2},{1,5},{3,7},... | collective-permute-start | bytes 589832 | tf_op jit(solution)/shard_map/ppermute | solution.py:19
  82.2 3.9 %collective-permute-start.10 = (bf16[2,128,384]{2,1,0:T(8,128)(2,1)S(1)}, bf16[2,128,384]{2,1,0:T(8,128)(2,1)}, u32[]{:S(2)}, u32[]{:S(2)}) collective-permute-start(bf16[2,128,384]{2,1,0:T(8,128)(2,1)S(1)} %collective-permute-done.6.refs_2_), channel_id=1, source_target_pairs={{0,1},{1,0},{2,3},{3,2},{4,5},{5,4},{6,7},{7,6},{8,9},{9,8},{10,11... | collective-permute-start | bytes 589832 | tf_op jit(solution)/shard_map/ppermute | solution.py:23
  82.2 3.9 %collective-permute-start.11 = (bf16[2,128,384]{2,1,0:T(8,128)(2,1)S(1)}, bf16[2,128,384]{2,1,0:T(8,128)(2,1)}, u32[]{:S(2)}, u32[]{:S(2)}) collective-permute-start(bf16[2,128,384]{2,1,0:T(8,128)(2,1)S(1)} %collective-permute-done.7.refs_3_), channel_id=1, source_target_pairs={{0,1},{1,0},{2,3},{3,2},{4,5},{5,4},{6,7},{7,6},{8,9},{9,8},{10,11... | collective-permute-start | bytes 589832 | tf_op jit(solution)/shard_map/ppermute | solution.py:23
  82.7 3.4 %collective-permute-start.12 = (bf16[2,128,384]{2,1,0:T(8,128)(2,1)}, bf16[2,128,384]{2,1,0:T(8,128)(2,1)}, u32[]{:S(2)}, u32[]{:S(2)}) collective-permute-start(bf16[2,128,384]{2,1,0:T(8,128)(2,1)} %collective-permute-done.8.refs_4_), channel_id=1, source_target_pairs={{0,1},{1,0},{2,3},{3,2},{4,5},{5,4},{6,7},{7,6},{8,9},{9,8},{10,11... | collective-permute-start | bytes 589832 | tf_op jit(solution)/shard_map/ppermute | solution.py:23
  82.8 3.4 %collective-permute-start.13 = (bf16[2,128,384]{2,1,0:T(8,128)(2,1)}, bf16[2,128,384]{2,1,0:T(8,128)(2,1)}, u32[]{:S(2)}, u32[]{:S(2)}) collective-permute-start(bf16[2,128,384]{2,1,0:T(8,128)(2,1)} %collective-permute-done.9.refs_5_), channel_id=1, source_target_pairs={{0,1},{1,0},{2,3},{3,2},{4,5},{5,4},{6,7},{7,6},{8,9},{9,8},{10,11... | collective-permute-start | bytes 589832 | tf_op jit(solution)/shard_map/ppermute | solution.py:23
  93.0 25.3 %collective-permute-start.14 = (bf16[16,128,384]{2,1,0:T(8,128)(2,1)}, bf16[16,128,384]{2,1,0:T(8,128)(2,1)}, u32[]{:S(2)}, u32[]{:S(2)}) collective-permute-start(bf16[16,128,384]{2,1,0:T(8,128)(2,1)} %square_rows.1.refs_0_), channel_id=1, source_target_pairs={{0,1},{1,0},{2,3},{3,2},{4,5},{5,4},{6,7},{7,6},{8,9},{9,8},{10,11... | collective-permute-start | bytes 4718600 | tf_op jit(solution)/shard_map/ppermute | solution.py:23
  96.8 10.1 %collective-permute-start.15 = (bf16[2,128,384]{2,1,0:T(8,128)(2,1)S(1)}, bf16[2,128,384]{2,1,0:T(8,128)(2,1)S(1)}, u32[]{:S(2)}, u32[]{:S(2)}) collective-permute-start(bf16[2,128,384]{2,1,0:T(8,128)(2,1)S(1)} %get-tuple-element.17), channel_id=1, source_target_pairs={{0,14},{2,0},{4,2},{6,4},{8,6},{10,8},{12,10},{14,12},{1,15},{3,1}... | collective-permute-start | bytes 589832 | tf_op jit(solution)/shard_map/ppermute | solution.py:19
  101.6 10.5 %collective-permute-start.16 = (bf16[2,128,384]{2,1,0:T(8,128)(2,1)S(1)}, bf16[2,128,384]{2,1,0:T(8,128)(2,1)S(1)}, u32[]{:S(2)}, u32[]{:S(2)}) collective-permute-start(bf16[2,128,384]{2,1,0:T(8,128)(2,1)S(1)} %get-tuple-element.18), channel_id=1, source_target_pairs={{0,2},{2,4},{4,6},{6,8},{8,10},{10,12},{12,14},{14,0},{1,3},{3,5},... | collective-permute-start | bytes 589832 | tf_op jit(solution)/shard_map/ppermute | solution.py:19
  101.6 14.7 %collective-permute-start.17 = (bf16[2,128,384]{2,1,0:T(8,128)(2,1)S(1)}, bf16[2,128,384]{2,1,0:T(8,128)(2,1)}, u32[]{:S(2)}, u32[]{:S(2)}) collective-permute-start(bf16[2,128,384]{2,1,0:T(8,128)(2,1)S(1)} %get-tuple-element.19), channel_id=1, source_target_pairs={{0,12},{2,14},{4,0},{6,2},{8,4},{10,6},{12,8},{14,10},{1,13},{3,15... | collective-permute-start | bytes 589832 | tf_op jit(solution)/shard_map/ppermute | solution.py:19
  102.2 14.0 %collective-permute-start.18 = (bf16[2,128,384]{2,1,0:T(8,128)(2,1)S(1)}, bf16[2,128,384]{2,1,0:T(8,128)(2,1)}, u32[]{:S(2)}, u32[]{:S(2)}) collective-permute-start(bf16[2,128,384]{2,1,0:T(8,128)(2,1)S(1)} %get-tuple-element.20), channel_id=1, source_target_pairs={{0,4},{2,6},{4,8},{6,10},{8,12},{10,14},{12,0},{14,2},{1,5},{3,7},... | collective-permute-start | bytes 589832 | tf_op jit(solution)/shard_map/ppermute | solution.py:19
  106.8 10.9 %collective-permute-start.19 = (bf16[2,128,384]{2,1,0:T(8,128)(2,1)S(1)}, bf16[2,128,384]{2,1,0:T(8,128)(2,1)}, u32[]{:S(2)}, u32[]{:S(2)}) collective-permute-start(bf16[2,128,384]{2,1,0:T(8,128)(2,1)S(1)} %collective-permute-done.15.refs_2_), channel_id=1, source_target_pairs={{0,1},{1,0},{2,3},{3,2},{4,5},{5,4},{6,7},{7,6},{8,9},{9,8},{10,11... | collective-permute-start | bytes 589832 | tf_op jit(solution)/shard_map/ppermute | solution.py:23
  112.1 5.7 %collective-permute-start.20 = (bf16[2,128,384]{2,1,0:T(8,128)(2,1)S(1)}, bf16[2,128,384]{2,1,0:T(8,128)(2,1)}, u32[]{:S(2)}, u32[]{:S(2)}) collective-permute-start(bf16[2,128,384]{2,1,0:T(8,128)(2,1)S(1)} %collective-permute-done.16.refs_3_), channel_id=1, source_target_pairs={{0,1},{1,0},{2,3},{3,2},{4,5},{5,4},{6,7},{7,6},{8,9},{9,8},{10,11... | collective-permute-start | bytes 589832 | tf_op jit(solution)/shard_map/ppermute | solution.py:23
  116.2 1.8 %collective-permute-start.21 = (bf16[2,128,384]{2,1,0:T(8,128)(2,1)}, bf16[2,128,384]{2,1,0:T(8,128)(2,1)}, u32[]{:S(2)}, u32[]{:S(2)}) collective-permute-start(bf16[2,128,384]{2,1,0:T(8,128)(2,1)} %collective-permute-done.17.refs_4_), channel_id=1, source_target_pairs={{0,1},{1,0},{2,3},{3,2},{4,5},{5,4},{6,7},{7,6},{8,9},{9,8},{10,11... | collective-permute-start | bytes 589832 | tf_op jit(solution)/shard_map/ppermute | solution.py:23
  116.2 2.1 %collective-permute-start.22 = (bf16[2,128,384]{2,1,0:T(8,128)(2,1)}, bf16[2,128,384]{2,1,0:T(8,128)(2,1)}, u32[]{:S(2)}, u32[]{:S(2)}) collective-permute-start(bf16[2,128,384]{2,1,0:T(8,128)(2,1)} %collective-permute-done.18.refs_5_), channel_id=1, source_target_pairs={{0,1},{1,0},{2,3},{3,2},{4,5},{5,4},{6,7},{7,6},{8,9},{9,8},{10,11... | collective-permute-start | bytes 589832 | tf_op jit(solution)/shard_map/ppermute | solution.py:23

commit v2 on v1

v2 whole, which is shorter than its diff:
```python
import functools

import jax
import jax.numpy as jnp
from jax import lax
from jax.experimental import pallas as pl
from jax.experimental.pallas import tpu as pltpu
from jax.sharding import PartitionSpec as P

CAP = 2
REACH = 2
OFFSETS = tuple(step for reach in range(1, REACH + 1) for step in (reach, -reach))
BEHIND = tuple(OFFSETS.index(-step) for step in OFFSETS)
SUBLANES, LANES = 8, 128
VMEM_LIMIT = 24 * 1024 * 1024


def from_ahead(value, steps):
    count = lax.axis_size("rows")
    pairs = [(source, (source - steps) % count) for source in range(count)]
    return lax.ppermute(value, "rows", pairs)


def from_sibling(value):
    return lax.ppermute(value, "layers", [(0, 1), (1, 0)])


def spread(columns, kept):
    table = jnp.concatenate([columns, kept], axis=1).T
    return jnp.pad(table, ((0, SUBLANES - table.shape[0]), (0, LANES - table.shape[1])))


def named_rows(own_slots, other_slots, owner, own):
    low, high = [], []
    for slots in (own_slots, other_slots):
        local = slots - owner * own
        lane = lax.broadcasted_iota(jnp.int32, local.shape, 1)
        inside = (local >= 0) & (local < own) & (lane < own)
        low.append(jnp.where(inside, local, own - 1))
        high.append(jnp.where(inside, local, 0))
    return jnp.minimum(*low), jnp.maximum(*high)


def fill(table, parts, sems, half, edge, segments, first):
    copies = []
    begin = 0
    for part in parts:
        size = part.shape[0]
        for b in range(half):
            copies.append(
                pltpu.make_async_copy(
                    part.at[:, :, pl.ds(b * edge, edge)],
                    table.at[pl.ds(b * segments + begin, size)],
                    sems.at[first + len(copies)],
                )
            )
        begin += size
    for copy in copies:
        copy.start()
    return copies


def gather_kernel(own, half, density_ref, *refs):
    near, (rows_ref, *outs), sems = refs[: len(OFFSETS)], refs[len(OFFSETS) : -1], refs[-1]
    me = lax.axis_index("rows")
    copies = []
    for position, out in enumerate(outs):
        numbers = near[BEHIND[position]]
        low, high = named_rows(
            numbers[0:half], numbers[SUBLANES : SUBLANES + half], me, own
        )
        for k, row in enumerate((jnp.min(low), jnp.max(high))):
            n = position * CAP + k
            rows_ref[n] = row
            copies.append(pltpu.make_async_copy(density_ref.at[row], out.at[k], sems.at[n]))
            copies[-1].start()
    for copy in copies:
        copy.wait()


def gather(density, near, half):
    piece = jax.ShapeDtypeStruct((CAP,) + density.shape[1:], density.dtype)
    return pl.pallas_call(
        functools.partial(gather_kernel, density.shape[0], half),
        out_shape=[jax.ShapeDtypeStruct((len(OFFSETS) * CAP,), jnp.int32)]
        + [piece] * len(OFFSETS),
        in_specs=[pl.BlockSpec(memory_space=pl.ANY)]
        + [pl.BlockSpec(memory_space=pltpu.VMEM)] * len(OFFSETS),
        out_specs=[pl.BlockSpec(memory_space=pltpu.SMEM)]
        + [pl.BlockSpec(memory_space=pltpu.VMEM)] * len(OFFSETS),
        scratch_shapes=[pltpu.SemaphoreType.DMA((len(OFFSETS) * CAP,))],
        compiler_params=pltpu.CompilerParams(vmem_limit_bytes=VMEM_LIMIT),
        cost_estimate=pl.CostEstimate(flops=0, bytes_accessed=1024 * 1024, transcendentals=0),
        name="gather_rows",
    )(density, *near)


def tables_kernel(own, half, peers, segments, mine_ref, *refs):
    near, (square_ref, cube_ref) = refs[: len(OFFSETS)], refs[len(OFFSETS) :]
    me = lax.axis_index("rows")
    shape = (SUBLANES, LANES)
    lane = lax.broadcasted_iota(jnp.int32, shape, 1)
    own_columns, own_kept = mine_ref[0:half], mine_ref[half : 2 * half]
    other_columns = mine_ref[SUBLANES : SUBLANES + half]
    other_kept = mine_ref[SUBLANES + half : SUBLANES + 2 * half]
    pad = jnp.zeros((SUBLANES - 2 * half, LANES), jnp.int32)
    columns = jnp.concatenate([own_columns, other_columns, pad], axis=0)
    column_table = columns
    kept_table = jnp.concatenate([own_kept, other_kept, pad], axis=0)
    slots = columns - me * own
    for position, step in enumerate(OFFSETS):
        owner = lax.rem(me + step + peers, peers)
        low, high = named_rows(own_columns, other_columns, owner, own)
        low = jnp.min(jnp.min(low, axis=0, keepdims=True), axis=1, keepdims=True)
        high = jnp.max(jnp.max(high, axis=0, keepdims=True), axis=1, keepdims=True)
        local = columns - owner * own
        first = own + position * CAP
        slots = jnp.where(
            (local >= 0) & (local < own), first + (local != low).astype(jnp.int32), slots
        )
        numbers = near[position]
        far_columns = jnp.concatenate([numbers[0:half], numbers[SUBLANES : SUBLANES + half], pad])
        far_kept = jnp.concatenate(
            [numbers[half : 2 * half], numbers[SUBLANES + half : SUBLANES + 2 * half], pad]
        )
        source = jnp.where(lane == first, low, high)
        here = (lane == first) | (lane == first + 1)
        column_table = jnp.where(
            here, jnp.take_along_axis(far_columns, source, axis=1), column_table
        )
        kept_table = jnp.where(here, jnp.take_along_axis(far_kept, source, axis=1), kept_table)
    slots = jnp.where(lane < own, jnp.clip(slots, 0, LANES - 1), 0)
    far = len(OFFSETS) * CAP
    base = jnp.where(slots < own, slots, slots + own)
    shift = jnp.where(slots < own, own, far)
    empty = half * segments - 1
    for out, table in ((square_ref, column_table), (cube_ref, kept_table)):
        met = [
            jnp.take_along_axis(jnp.broadcast_to(table[b : b + 1], shape), slots, axis=1)
            for b in range(2 * half)
        ]
        for s in range(half):
            index = jnp.full(shape, empty, jnp.int32)
            for b in range(2 * half):
                place = (b % half) * segments + base + (shift if b >= half else 0)
                index = jnp.where(met[b] == own_kept[s : s + 1], place, index)
            out[s * SUBLANES : (s + 1) * SUBLANES] = index


def tables(mine, near, own, half, peers, segments):
    shape = jax.ShapeDtypeStruct((half * SUBLANES, LANES), jnp.int32)
    return pl.pallas_call(
        functools.partial(tables_kernel, own, half, peers, segments),
        out_shape=[shape] * 2,
        cost_estimate=pl.CostEstimate(flops=0, bytes_accessed=64 * 1024, transcendentals=0),
        name="block_tables",
    )(mine, *near)


def row_product(table, index_ref, row, left, width, half, edge):
    total = None
    for a in range(0, width, 2):
        pair = range(a, min(a + 2, width))
        lhs = jnp.concatenate([left(k) for k in pair], axis=1)
        rhs = jnp.concatenate(
            [
                jnp.concatenate(
                    [table[index_ref[s * SUBLANES + k, row]] for s in range(half)], axis=1
                )
                for k in pair
            ],
            axis=0,
        )
        term = jnp.dot(lhs, rhs, preferred_element_type=jnp.float32)
        total = term if total is None else total + term
    return total


def square_kernel(own, edge, half, segments, wanted, rows_ref, index_ref, *refs):
    parts = refs[: 2 + 2 * len(OFFSETS)]
    outs = refs[-2 - (len(OFFSETS) if wanted else 1) : -2]
    table, sems = refs[-2:]
    copies = fill(table, parts, sems, half, edge, segments, 0)
    width = 2 * half
    table[half * segments - 1] = jnp.zeros((edge, edge), table.dtype)
    for copy in copies:
        copy.wait()

    def one(i, out, place):
        row = rows_ref[i] if wanted else i
        left = lambda k: table[(k % half) * segments + (k // half) * own + row]
        total = row_product(table, index_ref, row, left, width, half, edge)
        out[place] = total.astype(out.dtype)

    if wanted:
        for position, out in enumerate(outs):
            for k in range(CAP):
                one(position * CAP + k, out, k)
    else:

        def body(i, carry):
            one(i, outs[0], i)
            return carry

        lax.fori_loop(0, own, body, 0, unroll=2)


def square(rows, index, parts, wanted, after=()):
    own, edge, wide = parts[0].shape
    half = wide // edge
    segments = 2 * own + 2 * len(OFFSETS) * CAP + 1
    if wanted:
        shapes = [jax.ShapeDtypeStruct((CAP, edge, wide), parts[0].dtype)] * len(OFFSETS)
        count = len(OFFSETS) * CAP
    else:
        shapes = [jax.ShapeDtypeStruct((own, edge, wide), parts[0].dtype)]
        count = own
    return pl.pallas_call(
        functools.partial(square_kernel, own, edge, half, segments, wanted),
        out_shape=shapes,
        in_specs=[pl.BlockSpec(memory_space=pltpu.SMEM)] * 2
        + [pl.BlockSpec(memory_space=pl.ANY)] * (len(parts) + len(after)),
        out_specs=[pl.BlockSpec(memory_space=pltpu.VMEM)] * len(shapes),
        scratch_shapes=[
            pltpu.VMEM((half * segments, edge, edge), parts[0].dtype),
            pltpu.SemaphoreType.DMA((half * len(parts),)),
        ],
        compiler_params=pltpu.CompilerParams(vmem_limit_bytes=VMEM_LIMIT),
        cost_estimate=pl.CostEstimate(
            flops=count * 2 * edge * 2 * wide * wide,
            bytes_accessed=5 * 1024 * 1024,
            transcendentals=0,
        ),
        name="square_wanted" if wanted else "square_rows",
    )(rows, index, *parts, *after)


def cube_kernel(own, edge, half, segments, index_ref, left_own, left_other, *refs):
    out, table, lefts, sems = refs[-4:]
    parts = refs[:-4]
    copies = fill(table, parts, sems, half, edge, segments, 0)
    copies += fill(lefts, (left_own, left_other), sems, half, edge, 2 * own, len(copies))
    width = 2 * half
    table[half * segments - 1] = jnp.zeros((edge, edge), table.dtype)
    for copy in copies:
        copy.wait()

    def body(i, carry):
        left = lambda k: lefts[(k % half) * (2 * own) + (k // half) * own + i]
        total = row_product(table, index_ref, i, left, width, half, edge)
        first = jnp.concatenate([table[s * segments + i] for s in range(half)], axis=1)
        out[i] = (3.0 * first.astype(jnp.float32) - 2.0 * total).astype(out.dtype)
        return carry

    lax.fori_loop(0, own, body, 0, unroll=2)


def cube(index, left_own, left_other, parts):
    own, edge, wide = left_own.shape
    half = wide // edge
    segments = 2 * own + 2 * len(OFFSETS) * CAP + 1
    return pl.pallas_call(
        functools.partial(cube_kernel, own, edge, half, segments),
        out_shape=jax.ShapeDtypeStruct(left_own.shape, left_own.dtype),
        in_specs=[pl.BlockSpec(memory_space=pltpu.SMEM)]
        + [pl.BlockSpec(memory_space=pl.ANY)] * (len(parts) + 2),
        out_specs=pl.BlockSpec(memory_space=pltpu.VMEM),
        scratch_shapes=[
            pltpu.VMEM((half * segments, edge, edge), left_own.dtype),
            pltpu.VMEM((half * 2 * own, edge, edge), left_own.dtype),
            pltpu.SemaphoreType.DMA((half * (len(parts) + 2),)),
        ],
        compiler_params=pltpu.CompilerParams(vmem_limit_bytes=VMEM_LIMIT),
        cost_estimate=pl.CostEstimate(
            flops=own * 2 * edge * 2 * wide * wide,
            bytes_accessed=9 * 1024 * 1024,
            transcendentals=0,
        ),
        name="cube_rows",
    )(index, left_own, left_other, *parts)


def local(density, columns, kept):
    own, edge, wide = density.shape
    half = columns.shape[1]
    peers = lax.axis_size("rows")
    numbers = spread(columns, kept)
    mine = jnp.concatenate([numbers, from_sibling(numbers)], axis=0)
    near = [from_ahead(mine, step) for step in OFFSETS]
    other_density = from_sibling(density)
    sends, *pieces = gather(density, near, half)
    got = [from_ahead(piece, step) for step, piece in zip(OFFSETS, pieces)]
    got_other = [from_sibling(piece) for piece in got]
    segments = 2 * own + 2 * len(OFFSETS) * CAP + 1
    square_index, cube_index = tables(mine, near, own, half, peers, segments)

    parts = [density, other_density, *got, *got_other]
    wanted = square(sends, square_index, parts, True)
    got_square = [from_ahead(piece, step) for step, piece in zip(OFFSETS, wanted)]
    (squares,) = square(sends, square_index, parts, False, wanted[:1])
    other_squares = from_sibling(squares)
    got_square_other = [from_sibling(piece) for piece in got_square]
    return cube(
        cube_index,
        density,
        other_density,
        [squares, other_squares, *got_square, *got_square_other],
    )


def solution(mesh):
    in_specs = (
        P(("groups", "rows"), None, "layers"),
        P(("groups", "rows"), "layers"),
        P(("groups", "rows"), "layers"),
    )
    out_specs = P(("groups", "rows"), None, "layers")
    return jax.shard_map(local, mesh=mesh, in_specs=in_specs, out_specs=out_specs, check_vma=False)
```

time: 127 us -> 76.1 us (0.60)
  Pallas kernels: 43.3 us -> 20.5 us
  local copies, waits for them, and re-layouts: 25.5 us -> 2.82 us
  other arithmetic: 20.2 us -> 0.71 us
  waiting for transfers between devices: 13.2 us -> 22.9 us
  starting transfers between devices: 23 us -> 27.6 us
    pallas_call x1 -> x2, Pallas kernels: 25.8 us -> 4.21 us  [the longest x1 2.5 us: gather(): pl.pallas_call(functools.partial(gather_kernel, density.shape[0], half),...]
    eq x12 -> x0, local copies, waits for them, and re-layouts: 11.4 us -> none  [block_index(): met[:, :, b, None] == targets[:, None, :]]
    ppermute x12, waiting for transfers between devices: 12.7 us -> 19.3 us  [from_ahead(): return lax.ppermute(value, 'rows', pairs)]
    concatenate x1 -> x0, local copies, waits for them, and re-layouts: 5.62 us -> none  [local(): jnp.concatenate([named_rows(near[-step][:, :width], me, own) for step in...]
    another operation x4 -> x0, other arithmetic: 5.23 us -> none  [named_rows(): return jnp.stack([low, high]).astype(jnp.int32)]
    ppermute x12, starting transfers between devices: 20.8 us -> 25.4 us  [from_ahead(): return lax.ppermute(value, 'rows', pairs)]
    reduce_max x5 -> x0, other arithmetic: 4.23 us -> none  [named_rows(): high = jnp.max(jnp.where(inside, local, 0))]
    sub x6 -> x0, local copies, waits for them, and re-layouts: 4.03 us -> none  [block_index(): where_b[:, :, None] - empty]
  transfers between devices with their start and end apart: 23 -> 23, of which waited for: 5 -> 11; matrix products, arithmetic and copies ran while one was open for 36% -> 1% of each run, Pallas kernels for 24% -> 6%
where the time goes in v2:
time: 76.1 us; the launch traced here: 74.7 us
  starting transfers between devices  27.6 us (36%)
  waiting for transfers between devices  22.9 us (30%)
  Pallas kernels  20.5 us (27%)
  local copies, waits for them, and re-layouts  2.82 us (4%)
    ppermute x12, starting transfers between devices, from_ahead(): return lax.ppermute(value, 'rows', pairs)  25.4 us
    ppermute x12, waiting for transfers between devices, from_ahead(): return lax.ppermute(value, 'rows', pairs)  19.3 us
    pallas_call x2, Pallas kernels, square(): pl.pallas_call(functools.partial(square_kernel, own, edge, half, segments...  9.69 us
    pallas_call x1, Pallas kernels, cube(): pl.pallas_call(functools.partial(cube_kernel, own, edge, half, segments),...  6.57 us
    ppermute x11, waiting for transfers between devices, from_sibling(): return lax.ppermute(value, 'layers', [(0, 1), (1, 0)])  3.67 us
    unnamed x24, local copies, waits for them, and re-layouts  2.81 us
    pallas_call x1, Pallas kernels, gather(): pl.pallas_call(functools.partial(gather_kernel, density.shape[0], half),...  2.5 us
    ppermute x11, starting transfers between devices, from_sibling(): return lax.ppermute(value, 'layers', [(0, 1), (1, 0)])  2.23 us
  transfers between devices with their start and end apart: 23, of which 11 were waited for; matrix products, arithmetic and copies ran while one was open for 1% of the time, Pallas kernels for 6%

profile of v2, /device:TPU:0, one launch (start us, length us, event | category | flops | bytes accessed | tf_op | source)
XLA Modules:
  0.0 74.7 jit_solution(8959810291905446497)
XLA Ops:
  0.0 0.5 collective-permute-start.5
  0.5 0.7 add_bitcast_fusion
  1.3 2.2 %collective-permute-done = s32[8,128]{1,0:T(8,128)S(1)} collective-permute-done((s32[8,128]{1,0:T(8,128)S(1)}, s32[8,128]{1,0:T(8,128)S(1)}, u32[]{:S(2)}, u32[]{:S(2)}) %collective-permute-start) | collective-permute-done | bytes 4128 | tf_op jit(solution)/shard_map/ppermute | solution.py:25
  3.5 2.9 %collective-permute-start.4 = (s32[16,128]{1,0:T(8,128)S(1)}, s32[16,128]{1,0:T(8,128)S(1)}, u32[]{:S(2)}, u32[]{:S(2)}) collective-permute-start(s32[16,128]{1,0:T(8,128)S(1)} %pad_add_fusion.mine_ref), channel_id=1, source_target_pairs={{0,4},{2,6},{4,8},{6,10},{8,12},{10,14},{12,0},{14,2},{1,5},{3,7},... | collective-permute-start | bytes 24584 | tf_op jit(solution)/shard_map/ppermute | solution.py:21
  6.4 2.1 %collective-permute-start.3 = (s32[16,128]{1,0:T(8,128)S(1)}, s32[16,128]{1,0:T(8,128)S(1)}, u32[]{:S(2)}, u32[]{:S(2)}) collective-permute-start(s32[16,128]{1,0:T(8,128)S(1)} %pad_add_fusion.mine_ref), channel_id=1, source_target_pairs={{0,12},{2,14},{4,0},{6,2},{8,4},{10,6},{12,8},{14,10},{1,13},{3,15... | collective-permute-start | bytes 24584 | tf_op jit(solution)/shard_map/ppermute | solution.py:21
  8.5 1.7 %collective-permute-start.2 = (s32[16,128]{1,0:T(8,128)S(1)}, s32[16,128]{1,0:T(8,128)S(1)}, u32[]{:S(2)}, u32[]{:S(2)}) collective-permute-start(s32[16,128]{1,0:T(8,128)S(1)} %pad_add_fusion.mine_ref), channel_id=1, source_target_pairs={{0,2},{2,4},{4,6},{6,8},{8,10},{10,12},{12,14},{14,0},{1,3},{3,5},... | collective-permute-start | bytes 24584 | tf_op jit(solution)/shard_map/ppermute | solution.py:21
  10.2 3.0 %collective-permute-start.1 = (s32[16,128]{1,0:T(8,128)S(1)}, s32[16,128]{1,0:T(8,128)S(1)}, u32[]{:S(2)}, u32[]{:S(2)}) collective-permute-start(s32[16,128]{1,0:T(8,128)S(1)} %pad_add_fusion.mine_ref), channel_id=1, source_target_pairs={{0,14},{2,0},{4,2},{6,4},{8,6},{10,8},{12,10},{14,12},{1,15},{3,1}... | collective-permute-start | bytes 24584 | tf_op jit(solution)/shard_map/ppermute | solution.py:21
  13.3 1.6 %collective-permute-done.2.refs_1_ = s32[16,128]{1,0:T(8,128)S(1)} collective-permute-done((s32[16,128]{1,0:T(8,128)S(1)}, s32[16,128]{1,0:T(8,128)S(1)}, u32[]{:S(2)}, u32[]{:S(2)}) %collective-permute-start.2) | collective-permute-done | bytes 8224 | tf_op jit(solution)/shard_map/ppermute | solution.py:21
  14.9 1.4 %copy-done = bf16[16,128,384]{2,1,0:T(8,128)(2,1)S(1)} copy-done((bf16[16,128,384]{2,1,0:T(8,128)(2,1)S(1)}, bf16[16,128,384]{2,1,0:T(8,128)(2,1)}, u32[]{:S(2)}) %copy-start) | copy-done | bytes 1572888
  16.3 2.5 %gather_rows.1 = (s32[8]{0:T(128)S(1)}, bf16[2,128,384]{2,1,0:T(8,128)(2,1)S(1)}, bf16[2,128,384]{2,1,0:T(8,128)(2,1)S(1)}, bf16[2,128,384]{2,1,0:T(8,128)(2,1)S(1)}, bf16[2,128,384]{2,1,0:T(8,128)(2,1)S(1)}) custom-call(bf16[16,128,384]{2,1,0:T(8,128)(2,1)S(1)} %copy-done, s32[16,128]{1,0:T(8,128)S(1)} %collective-permute-done.1.refs_0_, ...), custom_call_target="tpu_custom_call" | custom-call | bytes 1048576 | tf_op jit(solution)/shard_map/gather_rows/pallas_call | solution.py:83
  18.8 4.8 %collective-permute-start.6 = (bf16[2,128,384]{2,1,0:T(8,128)(2,1)S(1)}, bf16[2,128,384]{2,1,0:T(8,128)(2,1)S(1)}, u32[]{:S(2)}, u32[]{:S(2)}) collective-permute-start(bf16[2,128,384]{2,1,0:T(8,128)(2,1)S(1)} %get-tuple-element.19), channel_id=1, source_target_pairs={{0,14},{2,0},{4,2},{6,4},{8,6},{10,8},{12,10},{14,12},{1,15},{3,1}... | collective-permute-start | bytes 589832 | tf_op jit(solution)/shard_map/ppermute | solution.py:21
  23.6 0.6 collective-permute-start.8
  24.2 1.4 %collective-permute-start.9 = (bf16[2,128,384]{2,1,0:T(8,128)(2,1)S(1)}, bf16[2,128,384]{2,1,0:T(8,128)(2,1)}, u32[]{:S(2)}, u32[]{:S(2)}) collective-permute-start(bf16[2,128,384]{2,1,0:T(8,128)(2,1)S(1)} %get-tuple-element.22), channel_id=1, source_target_pairs={{0,4},{2,6},{4,8},{6,10},{8,12},{10,14},{12,0},{14,2},{1,5},{3,7},... | collective-permute-start | bytes 589832 | tf_op jit(solution)/shard_map/ppermute | solution.py:21
  25.6 3.3 %collective-permute-done.6.refs_2_ = bf16[2,128,384]{2,1,0:T(8,128)(2,1)S(1)} collective-permute-done((bf16[2,128,384]{2,1,0:T(8,128)(2,1)S(1)}, bf16[2,128,384]{2,1,0:T(8,128)(2,1)S(1)}, u32[]{:S(2)}, u32[]{:S(2)}) %collective-permute-start.6) | collective-permute-done | bytes 196640 | tf_op jit(solution)/shard_map/ppermute | solution.py:21
  29.0 5.2 %collective-permute-done.7.refs_3_ = bf16[2,128,384]{2,1,0:T(8,128)(2,1)S(1)} collective-permute-done((bf16[2,128,384]{2,1,0:T(8,128)(2,1)S(1)}, bf16[2,128,384]{2,1,0:T(8,128)(2,1)S(1)}, u32[]{:S(2)}, u32[]{:S(2)}) %collective-permute-start.7) | collective-permute-done | bytes 196640 | tf_op jit(solution)/shard_map/ppermute | solution.py:21
  34.2 0.6 collective-permute-start.12
  34.8 1.7 %block_tables.1 = (s32[24,128]{1,0:T(8,128)}, s32[24,128]{1,0:T(8,128)}) custom-call(s32[16,128]{1,0:T(8,128)} %copy-done.11, s32[16,128]{1,0:T(8,128)} %copy-done.6, s32[16,128]{1,0:T(8,128)} %copy-done.5, s32[16,128]{1,0:T(8,128)} %copy-done.4, s32[16,128]{1,0:T(8,128)} %copy-done.3), custom_call_target="tpu_custom_call" | custom-call | bytes 65536 | tf_op jit(solution)/shard_map/block_tables/pallas_call | solution.py:152
  36.6 0.7 copy-done.2
  37.3 0.7 copy-done.9
  38.0 3.9 %square_wanted.1 = (bf16[2,128,384]{2,1,0:T(8,128)(2,1)S(1)}, bf16[2,128,384]{2,1,0:T(8,128)(2,1)S(1)}, bf16[2,128,384]{2,1,0:T(8,128)(2,1)S(1)}, bf16[2,128,384]{2,1,0:T(8,128)(2,1)S(1)}) custom-call(s32[8]{0:T(128)S(1)} %copy-done.9, s32[24,128]{1,0:T(8,128)S(1)} %copy-done.2, bf16[16,128,384]{2,1,0:T(8,128)(2,1)S(1)} %copy-done.1, ...), custom_call_target="tpu_custom_call" | custom-call | flops 603979776 | bytes 5242880 | tf_op jit(solution)/shard_map/square_wanted/pallas_call | solution.py:218
  41.9 5.8 %square_rows.1.refs_0_ = bf16[16,128,384]{2,1,0:T(8,128)(2,1)S(1)} custom-call(s32[8]{0:T(128)S(1)} %copy-done.10, s32[24,128]{1,0:T(8,128)S(1)} %copy-done.2, bf16[16,128,384]{2,1,0:T(8,128)(2,1)S(1)} %copy-done.1, bf16[16,128,384]{2,1,0:T(8,128)(2,1)S(1)} %collective-permute-done.5.refs_1_.left_other, ...), custom_call_target="tpu_custom_call" | custom-call | flops 1207959552 | bytes 5242880 | tf_op jit(solution)/shard_map/square_rows/pallas_call | solution.py:218
  47.7 0.5 collective-permute-start.14
  48.2 5.6 %collective-permute-start.16 = (bf16[2,128,384]{2,1,0:T(8,128)(2,1)S(1)}, bf16[2,128,384]{2,1,0:T(8,128)(2,1)S(1)}, u32[]{:S(2)}, u32[]{:S(2)}) collective-permute-start(bf16[2,128,384]{2,1,0:T(8,128)(2,1)S(1)} %get-tuple-element.24), channel_id=1, source_target_pairs={{0,2},{2,4},{4,6},{6,8},{8,10},{10,12},{12,14},{14,0},{1,3},{3,5},... | collective-permute-start | bytes 589832 | tf_op jit(solution)/shard_map/ppermute | solution.py:21
  53.8 2.0 %collective-permute-start.18 = (bf16[2,128,384]{2,1,0:T(8,128)(2,1)S(1)}, bf16[2,128,384]{2,1,0:T(8,128)(2,1)S(1)}, u32[]{:S(2)}, u32[]{:S(2)}) collective-permute-start(bf16[2,128,384]{2,1,0:T(8,128)(2,1)S(1)} %get-tuple-element.26), channel_id=1, source_target_pairs={{0,4},{2,6},{4,8},{6,10},{8,12},{10,14},{12,0},{14,2},{1,5},{3,7},... | collective-permute-start | bytes 589832 | tf_op jit(solution)/shard_map/ppermute | solution.py:21
  55.8 1.2 %collective-permute-start.15 = (bf16[2,128,384]{2,1,0:T(8,128)(2,1)S(1)}, bf16[2,128,384]{2,1,0:T(8,128)(2,1)S(1)}, u32[]{:S(2)}, u32[]{:S(2)}) collective-permute-start(bf16[2,128,384]{2,1,0:T(8,128)(2,1)S(1)} %get-tuple-element.23.refs_10_), channel_id=1, source_target_pairs={{0,14},{2,0},{4,2},{6,4},{8,6},{10,8},{12,10},{14,12},{1,15},{3,1}... | collective-permute-start | bytes 589832 | tf_op jit(solution)/shard_map/ppermute | solution.py:21
  57.1 1.7 %collective-permute-done.16.refs_3_ = bf16[2,128,384]{2,1,0:T(8,128)(2,1)S(1)} collective-permute-done((bf16[2,128,384]{2,1,0:T(8,128)(2,1)S(1)}, bf16[2,128,384]{2,1,0:T(8,128)(2,1)S(1)}, u32[]{:S(2)}, u32[]{:S(2)}) %collective-permute-start.16) | collective-permute-done | bytes 196640 | tf_op jit(solution)/shard_map/ppermute | solution.py:21
  58.7 7.1 %collective-permute-done.17.refs_4_ = bf16[2,128,384]{2,1,0:T(8,128)(2,1)S(1)} collective-permute-done((bf16[2,128,384]{2,1,0:T(8,128)(2,1)S(1)}, bf16[2,128,384]{2,1,0:T(8,128)(2,1)S(1)}, u32[]{:S(2)}, u32[]{:S(2)}) %collective-permute-start.17) | collective-permute-done | bytes 196640 | tf_op jit(solution)/shard_map/ppermute | solution.py:21
  65.8 0.5 collective-permute-start.22
  66.3 0.3 collective-permute-done.15.refs_2_
  66.7 0.6 collective-permute-done.21.refs_8_
  67.5 0.6 collective-permute-done.19.refs_6_
  68.1 6.6 %cube_rows.1 = bf16[16,128,384]{2,1,0:T(8,128)(2,1)} custom-call(s32[24,128]{1,0:T(8,128)S(1)} %copy-done.7, bf16[16,128,384]{2,1,0:T(8,128)(2,1)S(1)} %copy-done.1, bf16[16,128,384]{2,1,0:T(8,128)(2,1)S(1)} %collective-permute-done.5.refs_1_.left_other, bf16[16,128,384]{2,1,0:T(8,128)(2,1)S(1)} %square_rows.1.refs_0_, ...), custom_call_target="tpu_custom_call" | custom-call | flops 1207959552 | bytes 9437184 | tf_op jit(solution)/shard_map/cube_rows/pallas_call | solution.py:262
  (46 shorter events, 0.6 us)
Async XLA Ops:
  0.0 36.6 %collective-permute-start.5 = (bf16[16,128,384]{2,1,0:T(8,128)(2,1)}, bf16[16,128,384]{2,1,0:T(8,128)(2,1)S(1)}, u32[]{:S(2)}, u32[]{:S(2)}) collective-permute-start(bf16[16,128,384]{2,1,0:T(8,128)(2,1)} %left_own.1), channel_id=1, source_target_pairs={{0,1},{1,0},{2,3},{3,2},{4,5},{5,4},{6,7},{7,6},{8,9},{9,8},{10,11... | collective-permute-start | bytes 4718600 | tf_op jit(solution)/shard_map/ppermute | solution.py:25
  1.2 2.3 %collective-permute-start = (s32[8,128]{1,0:T(8,128)S(1)}, s32[8,128]{1,0:T(8,128)S(1)}, u32[]{:S(2)}, u32[]{:S(2)}) collective-permute-start(s32[8,128]{1,0:T(8,128)S(1)} %pad.4), channel_id=1, source_target_pairs={{0,1},{1,0},{2,3},{3,2},{4,5},{5,4},{6,7},{7,6},{8,9},{9,8},{10,11... | collective-permute-start | bytes 12296 | tf_op jit(solution)/shard_map/ppermute | solution.py:25
  3.5 15.3 %copy-start.11 = (s32[16,128]{1,0:T(8,128)}, s32[16,128]{1,0:T(8,128)S(1)}, u32[]{:S(2)}) copy-start(s32[16,128]{1,0:T(8,128)S(1)} %pad_add_fusion.mine_ref) | copy-start | bytes 24580
  3.5 9.8 %collective-permute-start.4 = (s32[16,128]{1,0:T(8,128)S(1)}, s32[16,128]{1,0:T(8,128)S(1)}, u32[]{:S(2)}, u32[]{:S(2)}) collective-permute-start(s32[16,128]{1,0:T(8,128)S(1)} %pad_add_fusion.mine_ref), channel_id=1, source_target_pairs={{0,4},{2,6},{4,8},{6,10},{8,12},{10,14},{12,0},{14,2},{1,5},{3,7},... | collective-permute-start | bytes 24584 | tf_op jit(solution)/shard_map/ppermute | solution.py:21
  6.4 6.8 %collective-permute-start.3 = (s32[16,128]{1,0:T(8,128)S(1)}, s32[16,128]{1,0:T(8,128)S(1)}, u32[]{:S(2)}, u32[]{:S(2)}) collective-permute-start(s32[16,128]{1,0:T(8,128)S(1)} %pad_add_fusion.mine_ref), channel_id=1, source_target_pairs={{0,12},{2,14},{4,0},{6,2},{8,4},{10,6},{12,8},{14,10},{1,13},{3,15... | collective-permute-start | bytes 24584 | tf_op jit(solution)/shard_map/ppermute | solution.py:21
  8.5 6.3 %collective-permute-start.2 = (s32[16,128]{1,0:T(8,128)S(1)}, s32[16,128]{1,0:T(8,128)S(1)}, u32[]{:S(2)}, u32[]{:S(2)}) collective-permute-start(s32[16,128]{1,0:T(8,128)S(1)} %pad_add_fusion.mine_ref), channel_id=1, source_target_pairs={{0,2},{2,4},{4,6},{6,8},{8,10},{10,12},{12,14},{14,0},{1,3},{3,5},... | collective-permute-start | bytes 24584 | tf_op jit(solution)/shard_map/ppermute | solution.py:21
  10.2 4.7 %collective-permute-start.1 = (s32[16,128]{1,0:T(8,128)S(1)}, s32[16,128]{1,0:T(8,128)S(1)}, u32[]{:S(2)}, u32[]{:S(2)}) collective-permute-start(s32[16,128]{1,0:T(8,128)S(1)} %pad_add_fusion.mine_ref), channel_id=1, source_target_pairs={{0,14},{2,0},{4,2},{6,4},{8,6},{10,8},{12,10},{14,12},{1,15},{3,1}... | collective-permute-start | bytes 24584 | tf_op jit(solution)/shard_map/ppermute | solution.py:21
  13.3 21.6 %copy-start.3 = (s32[16,128]{1,0:T(8,128)}, s32[16,128]{1,0:T(8,128)S(1)}, u32[]{:S(2)}) copy-start(s32[16,128]{1,0:T(8,128)S(1)} %collective-permute-done.4.refs_3_) | copy-start | bytes 24580
  13.3 21.6 %copy-start.4 = (s32[16,128]{1,0:T(8,128)}, s32[16,128]{1,0:T(8,128)S(1)}, u32[]{:S(2)}) copy-start(s32[16,128]{1,0:T(8,128)S(1)} %collective-permute-done.3.refs_2_) | copy-start | bytes 24580
  14.9 19.3 %copy-start.5 = (s32[16,128]{1,0:T(8,128)}, s32[16,128]{1,0:T(8,128)S(1)}, u32[]{:S(2)}) copy-start(s32[16,128]{1,0:T(8,128)S(1)} %collective-permute-done.2.refs_1_) | copy-start | bytes 24580
  16.3 17.8 %copy-start.6 = (s32[16,128]{1,0:T(8,128)}, s32[16,128]{1,0:T(8,128)S(1)}, u32[]{:S(2)}) copy-start(s32[16,128]{1,0:T(8,128)S(1)} %collective-permute-done.1.refs_0_) | copy-start | bytes 24580
  16.3 20.3 %copy-start.1 = (bf16[16,128,384]{2,1,0:T(8,128)(2,1)S(1)}, bf16[16,128,384]{2,1,0:T(8,128)(2,1)}, u32[]{:S(2)}) copy-start(bf16[16,128,384]{2,1,0:T(8,128)(2,1)} %left_own.1) | copy-start | bytes 4718596
  18.8 15.3 %copy-start.8 = (s32[8]{0:T(128)}, s32[8]{0:T(128)S(1)}, u32[]{:S(2)}) copy-start(s32[8]{0:T(128)S(1)} %get-tuple-element.17.rows_ref) | copy-start | bytes 100
  18.8 10.1 %collective-permute-start.6 = (bf16[2,128,384]{2,1,0:T(8,128)(2,1)S(1)}, bf16[2,128,384]{2,1,0:T(8,128)(2,1)S(1)}, u32[]{:S(2)}, u32[]{:S(2)}) collective-permute-start(bf16[2,128,384]{2,1,0:T(8,128)(2,1)S(1)} %get-tuple-element.19), channel_id=1, source_target_pairs={{0,14},{2,0},{4,2},{6,4},{8,6},{10,8},{12,10},{14,12},{1,15},{3,1}... | collective-permute-start | bytes 589832 | tf_op jit(solution)/shard_map/ppermute | solution.py:21
  23.6 10.5 %collective-permute-start.7 = (bf16[2,128,384]{2,1,0:T(8,128)(2,1)S(1)}, bf16[2,128,384]{2,1,0:T(8,128)(2,1)S(1)}, u32[]{:S(2)}, u32[]{:S(2)}) collective-permute-start(bf16[2,128,384]{2,1,0:T(8,128)(2,1)S(1)} %get-tuple-element.20), channel_id=1, source_target_pairs={{0,2},{2,4},{4,6},{6,8},{8,10},{10,12},{12,14},{14,0},{1,3},{3,5},... | collective-permute-start | bytes 589832 | tf_op jit(solution)/shard_map/ppermute | solution.py:21
  23.6 10.6 %collective-permute-start.8 = (bf16[2,128,384]{2,1,0:T(8,128)(2,1)S(1)}, bf16[2,128,384]{2,1,0:T(8,128)(2,1)}, u32[]{:S(2)}, u32[]{:S(2)}) collective-permute-start(bf16[2,128,384]{2,1,0:T(8,128)(2,1)S(1)} %get-tuple-element.21), channel_id=1, source_target_pairs={{0,12},{2,14},{4,0},{6,2},{8,4},{10,6},{12,8},{14,10},{1,13},{3,15... | collective-permute-start | bytes 589832 | tf_op jit(solution)/shard_map/ppermute | solution.py:21
  24.2 10.6 %collective-permute-start.9 = (bf16[2,128,384]{2,1,0:T(8,128)(2,1)S(1)}, bf16[2,128,384]{2,1,0:T(8,128)(2,1)}, u32[]{:S(2)}, u32[]{:S(2)}) collective-permute-start(bf16[2,128,384]{2,1,0:T(8,128)(2,1)S(1)} %get-tuple-element.22), channel_id=1, source_target_pairs={{0,4},{2,6},{4,8},{6,10},{8,12},{10,14},{12,0},{14,2},{1,5},{3,7},... | collective-permute-start | bytes 589832 | tf_op jit(solution)/shard_map/ppermute | solution.py:21
  29.0 7.6 %collective-permute-start.10 = (bf16[2,128,384]{2,1,0:T(8,128)(2,1)S(1)}, bf16[2,128,384]{2,1,0:T(8,128)(2,1)}, u32[]{:S(2)}, u32[]{:S(2)}) collective-permute-start(bf16[2,128,384]{2,1,0:T(8,128)(2,1)S(1)} %collective-permute-done.6.refs_2_), channel_id=1, source_target_pairs={{0,1},{1,0},{2,3},{3,2},{4,5},{5,4},{6,7},{7,6},{8,9},{9,8},{10,11... | collective-permute-start | bytes 589832 | tf_op jit(solution)/shard_map/ppermute | solution.py:25
  34.1 2.4 %collective-permute-start.11 = (bf16[2,128,384]{2,1,0:T(8,128)(2,1)S(1)}, bf16[2,128,384]{2,1,0:T(8,128)(2,1)}, u32[]{:S(2)}, u32[]{:S(2)}) collective-permute-start(bf16[2,128,384]{2,1,0:T(8,128)(2,1)S(1)} %collective-permute-done.7.refs_3_), channel_id=1, source_target_pairs={{0,1},{1,0},{2,3},{3,2},{4,5},{5,4},{6,7},{7,6},{8,9},{9,8},{10,11... | collective-permute-start | bytes 589832 | tf_op jit(solution)/shard_map/ppermute | solution.py:25
  34.2 2.4 %collective-permute-start.12 = (bf16[2,128,384]{2,1,0:T(8,128)(2,1)}, bf16[2,128,384]{2,1,0:T(8,128)(2,1)}, u32[]{:S(2)}, u32[]{:S(2)}) collective-permute-start(bf16[2,128,384]{2,1,0:T(8,128)(2,1)} %collective-permute-done.8.refs_4_), channel_id=1, source_target_pairs={{0,1},{1,0},{2,3},{3,2},{4,5},{5,4},{6,7},{7,6},{8,9},{9,8},{10,11... | collective-permute-start | bytes 589832 | tf_op jit(solution)/shard_map/ppermute | solution.py:25
  34.8 1.8 %collective-permute-start.13 = (bf16[2,128,384]{2,1,0:T(8,128)(2,1)}, bf16[2,128,384]{2,1,0:T(8,128)(2,1)}, u32[]{:S(2)}, u32[]{:S(2)}) collective-permute-start(bf16[2,128,384]{2,1,0:T(8,128)(2,1)} %collective-permute-done.9.refs_5_), channel_id=1, source_target_pairs={{0,1},{1,0},{2,3},{3,2},{4,5},{5,4},{6,7},{7,6},{8,9},{9,8},{10,11... | collective-permute-start | bytes 589832 | tf_op jit(solution)/shard_map/ppermute | solution.py:25
  38.0 3.9 %copy-start.10 = (s32[8]{0:T(128)S(1)}, s32[8]{0:T(128)}, u32[]{:S(2)}) copy-start(s32[8]{0:T(128)} %copy-done.8) | copy-start | bytes 100
  41.9 26.3 %copy-start.7 = (s32[24,128]{1,0:T(8,128)S(1)}, s32[24,128]{1,0:T(8,128)}, u32[]{:S(2)}) copy-start(s32[24,128]{1,0:T(8,128)} %get-tuple-element.16.index_ref) | copy-start | bytes 36868
  47.7 20.4 %collective-permute-start.14 = (bf16[16,128,384]{2,1,0:T(8,128)(2,1)S(1)}, bf16[16,128,384]{2,1,0:T(8,128)(2,1)S(1)}, u32[]{:S(2)}, u32[]{:S(2)}) collective-permute-start(bf16[16,128,384]{2,1,0:T(8,128)(2,1)S(1)} %square_rows.1.refs_0_), channel_id=1, source_target_pairs={{0,1},{1,0},{2,3},{3,2},{4,5},{5,4},{6,7},{7,6},{8,9},{9,8},{10,11... | collective-permute-start | bytes 4718600 | tf_op jit(solution)/shard_map/ppermute | solution.py:25
  48.2 10.5 %collective-permute-start.16 = (bf16[2,128,384]{2,1,0:T(8,128)(2,1)S(1)}, bf16[2,128,384]{2,1,0:T(8,128)(2,1)S(1)}, u32[]{:S(2)}, u32[]{:S(2)}) collective-permute-start(bf16[2,128,384]{2,1,0:T(8,128)(2,1)S(1)} %get-tuple-element.24), channel_id=1, source_target_pairs={{0,2},{2,4},{4,6},{6,8},{8,10},{10,12},{12,14},{14,0},{1,3},{3,5},... | collective-permute-start | bytes 589832 | tf_op jit(solution)/shard_map/ppermute | solution.py:21
  53.8 12.0 %collective-permute-start.17 = (bf16[2,128,384]{2,1,0:T(8,128)(2,1)S(1)}, bf16[2,128,384]{2,1,0:T(8,128)(2,1)S(1)}, u32[]{:S(2)}, u32[]{:S(2)}) collective-permute-start(bf16[2,128,384]{2,1,0:T(8,128)(2,1)S(1)} %get-tuple-element.25), channel_id=1, source_target_pairs={{0,12},{2,14},{4,0},{6,2},{8,4},{10,6},{12,8},{14,10},{1,13},{3,15... | collective-permute-start | bytes 589832 | tf_op jit(solution)/shard_map/ppermute | solution.py:21
  53.8 12.0 %collective-permute-start.18 = (bf16[2,128,384]{2,1,0:T(8,128)(2,1)S(1)}, bf16[2,128,384]{2,1,0:T(8,128)(2,1)S(1)}, u32[]{:S(2)}, u32[]{:S(2)}) collective-permute-start(bf16[2,128,384]{2,1,0:T(8,128)(2,1)S(1)} %get-tuple-element.26), channel_id=1, source_target_pairs={{0,4},{2,6},{4,8},{6,10},{8,12},{10,14},{12,0},{14,2},{1,5},{3,7},... | collective-permute-start | bytes 589832 | tf_op jit(solution)/shard_map/ppermute | solution.py:21
  55.8 10.8 %collective-permute-start.15 = (bf16[2,128,384]{2,1,0:T(8,128)(2,1)S(1)}, bf16[2,128,384]{2,1,0:T(8,128)(2,1)S(1)}, u32[]{:S(2)}, u32[]{:S(2)}) collective-permute-start(bf16[2,128,384]{2,1,0:T(8,128)(2,1)S(1)} %get-tuple-element.23.refs_10_), channel_id=1, source_target_pairs={{0,14},{2,0},{4,2},{6,4},{8,6},{10,8},{12,10},{14,12},{1,15},{3,1}... | collective-permute-start | bytes 589832 | tf_op jit(solution)/shard_map/ppermute | solution.py:21
  58.7 7.9 %collective-permute-start.20 = (bf16[2,128,384]{2,1,0:T(8,128)(2,1)S(1)}, bf16[2,128,384]{2,1,0:T(8,128)(2,1)S(1)}, u32[]{:S(2)}, u32[]{:S(2)}) collective-permute-start(bf16[2,128,384]{2,1,0:T(8,128)(2,1)S(1)} %collective-permute-done.16.refs_3_), channel_id=1, source_target_pairs={{0,1},{1,0},{2,3},{3,2},{4,5},{5,4},{6,7},{7,6},{8,9},{9,8},{10,11... | collective-permute-start | bytes 589832 | tf_op jit(solution)/shard_map/ppermute | solution.py:25
  65.8 1.4 %collective-permute-start.21 = (bf16[2,128,384]{2,1,0:T(8,128)(2,1)S(1)}, bf16[2,128,384]{2,1,0:T(8,128)(2,1)S(1)}, u32[]{:S(2)}, u32[]{:S(2)}) collective-permute-start(bf16[2,128,384]{2,1,0:T(8,128)(2,1)S(1)} %collective-permute-done.17.refs_4_), channel_id=1, source_target_pairs={{0,1},{1,0},{2,3},{3,2},{4,5},{5,4},{6,7},{7,6},{8,9},{9,8},{10,11... | collective-permute-start | bytes 589832 | tf_op jit(solution)/shard_map/ppermute | solution.py:25
  65.8 1.7 %collective-permute-start.22 = (bf16[2,128,384]{2,1,0:T(8,128)(2,1)S(1)}, bf16[2,128,384]{2,1,0:T(8,128)(2,1)S(1)}, u32[]{:S(2)}, u32[]{:S(2)}) collective-permute-start(bf16[2,128,384]{2,1,0:T(8,128)(2,1)S(1)} %collective-permute-done.18.refs_5_), channel_id=1, source_target_pairs={{0,1},{1,0},{2,3},{3,2},{4,5},{5,4},{6,7},{7,6},{8,9},{9,8},{10,11... | collective-permute-start | bytes 589832 | tf_op jit(solution)/shard_map/ppermute | solution.py:25
  66.7 1.4 %collective-permute-start.19 = (bf16[2,128,384]{2,1,0:T(8,128)(2,1)S(1)}, bf16[2,128,384]{2,1,0:T(8,128)(2,1)S(1)}, u32[]{:S(2)}, u32[]{:S(2)}) collective-permute-start(bf16[2,128,384]{2,1,0:T(8,128)(2,1)S(1)} %collective-permute-done.15.refs_2_), channel_id=1, source_target_pairs={{0,1},{1,0},{2,3},{3,2},{4,5},{5,4},{6,7},{7,6},{8,9},{9,8},{10,11... | collective-permute-start | bytes 589832 | tf_op jit(solution)/shard_map/ppermute | solution.py:25
  (3 other events, 2.8 us)

commit v3 on v0

v3 whole, which is shorter than its diff:
```python
import functools

import jax
import jax.numpy as jnp
from jax import lax
from jax.experimental import pallas as pl
from jax.experimental.pallas import tpu as pltpu
from jax.sharding import PartitionSpec as P

CAP = 2
REACH = 2
OFFSETS = tuple(step for reach in range(1, REACH + 1) for step in (reach, -reach))
FAR = len(OFFSETS) * CAP
SUBLANES, LANES = 8, 128
VMEM_LIMIT = 40 * 1024 * 1024
PARAMS = pltpu.CompilerParams(vmem_limit_bytes=VMEM_LIMIT)
VMEM = pl.BlockSpec(memory_space=pltpu.VMEM)
SMEM = pl.BlockSpec(memory_space=pltpu.SMEM)


def cost(flops, size):
    return pl.CostEstimate(flops=flops, bytes_accessed=size, transcendentals=0)


def like(value):
    return jax.ShapeDtypeStruct(value.shape, value.dtype)


def from_ahead(value, steps):
    count = lax.axis_size("rows")
    pairs = [(source, (source - steps) % count) for source in range(count)]
    return lax.ppermute(value, "rows", pairs)


def from_sibling(value):
    return lax.ppermute(value, "layers", [(0, 1), (1, 0)])


def everyones(columns, kept):
    table = jnp.concatenate([columns, kept], axis=1).T
    table = jnp.pad(table, ((0, SUBLANES - table.shape[0]), (0, LANES - table.shape[1])))
    count = lax.axis_size("rows") * lax.axis_size("layers")
    table = jnp.broadcast_to(table[None], (count,) + table.shape)
    return lax.all_to_all(table, ("rows", "layers"), 0, 0, tiled=True)


def named_rows(slots_of_both, owner, own):
    low, high = [], []
    for slots in slots_of_both:
        local = slots - owner * own
        lane = lax.broadcasted_iota(jnp.int32, local.shape, 1)
        inside = (local >= 0) & (local < own) & (lane < own)
        low.append(jnp.where(inside, local, own - 1))
        high.append(jnp.where(inside, local, 0))
    return jnp.minimum(*low), jnp.maximum(*high)


def gather_kernel(own, half, peers, density_ref, numbers_ref, rows_ref, *refs):
    outs, sems = refs[:-1], refs[-1]
    me = lax.axis_index("rows")
    copies = []
    for position, out in enumerate(outs):
        reader = lax.rem(me - OFFSETS[position] + peers, peers)
        both = [numbers_ref[2 * reader + layer][0:half] for layer in range(2)]
        low, high = named_rows(both, me, own)
        for k, row in enumerate((jnp.min(low), jnp.max(high))):
            n = position * CAP + k
            rows_ref[n] = row
            copies.append(pltpu.make_async_copy(density_ref.at[row], out.at[k], sems.at[n]))
            copies[-1].start()
    for copy in copies:
        copy.wait()


def gather(density, numbers, half):
    own, edge, wide = density.shape
    piece = jax.ShapeDtypeStruct((CAP, edge, wide), density.dtype)
    return pl.pallas_call(
        functools.partial(gather_kernel, own, half, lax.axis_size("rows")),
        out_shape=[jax.ShapeDtypeStruct((FAR,), jnp.int32)] + [piece] * len(OFFSETS),
        in_specs=[pl.BlockSpec(memory_space=pltpu.HBM), VMEM],
        out_specs=[SMEM] + [VMEM] * len(OFFSETS),
        scratch_shapes=[pltpu.SemaphoreType.DMA((FAR,))],
        compiler_params=PARAMS,
        cost_estimate=cost(0, 2 * FAR * edge * wide * 2),
        name="gather_rows",
    )(density, numbers)


def stack(table, own_ref, other_ref, sems):
    own = own_ref.shape[0]
    copies = [
        pltpu.make_async_copy(own_ref, table.at[pl.ds(0, own)], sems.at[0]),
        pltpu.make_async_copy(other_ref, table.at[pl.ds(own, own)], sems.at[1]),
    ]
    for copy in copies:
        copy.start()
    table[table.shape[0] - 1] = jnp.zeros(table.shape[1:], table.dtype)
    return copies


def tables_kernel(half, peers, numbers_ref, own_ref, other_ref, *refs):
    square_ref, cube_ref, table_ref, sems = refs
    own, edge, wide = own_ref.shape
    copies = stack(table_ref, own_ref, other_ref, sems)
    me, layer = lax.axis_index("rows"), lax.axis_index("layers")
    shape = (SUBLANES, LANES)
    lane = lax.broadcasted_iota(jnp.int32, shape, 1)
    pad = jnp.zeros((SUBLANES - 2 * half, LANES), jnp.int32)

    def slots_of(device):
        first, second = numbers_ref[2 * device + layer], numbers_ref[2 * device + 1 - layer]
        return [
            jnp.concatenate([first[k : k + half], second[k : k + half], pad], axis=0)
            for k in (0, half)
        ]

    columns, kept = slots_of(me)
    named = (columns[0:half], columns[half : 2 * half])
    column_table, kept_table = columns, kept
    slots = columns - me * own
    for position, step in enumerate(OFFSETS):
        owner = lax.rem(me + step + peers, peers)
        low, high = named_rows(named, owner, own)
        low = jnp.min(jnp.min(low, axis=0, keepdims=True), axis=1, keepdims=True)
        high = jnp.max(jnp.max(high, axis=0, keepdims=True), axis=1, keepdims=True)
        local = columns - owner * own
        first = own + position * CAP
        slots = jnp.where(
            (local >= 0) & (local < own), first + (local != low).astype(jnp.int32), slots
        )
        far_columns, far_kept = slots_of(owner)
        source = jnp.where(lane == first, low, high)
        here = (lane == first) | (lane == first + 1)
        column_table = jnp.where(
            here, jnp.take_along_axis(far_columns, source, axis=1), column_table
        )
        kept_table = jnp.where(here, jnp.take_along_axis(far_kept, source, axis=1), kept_table)
    slots = jnp.where(lane < own, jnp.clip(slots, 0, LANES - 1), 0)
    stride = table_stride(half, edge)
    base = jnp.where(slots < own, slots, slots + own)
    shift = jnp.where(slots < own, own, FAR)
    empty = (table_ref.shape[0] - 1) * stride
    for out, table in ((square_ref, column_table), (cube_ref, kept_table)):
        met = [
            jnp.take_along_axis(jnp.broadcast_to(table[b : b + 1], shape), slots, axis=1)
            for b in range(2 * half)
        ]
        for s in range(half):
            index = jnp.full(shape, empty, jnp.int32)
            for b in range(2 * half):
                entry = base + shift if b >= half else base
                place = entry * stride + (b % half) * edge
                index = jnp.where(met[b] == kept[s : s + 1], place, index)
            out[s * SUBLANES : (s + 1) * SUBLANES] = index
    for copy in copies:
        copy.wait()


def table_stride(half, edge):
    return edge << (half - 1).bit_length()


def table_like(own):
    return jax.ShapeDtypeStruct((2 * own.shape[0] + 2 * FAR + 1,) + own.shape[1:], own.dtype)


def tables(numbers, own, other, half):
    shape = jax.ShapeDtypeStruct((half * SUBLANES, LANES), jnp.int32)
    return pl.pallas_call(
        functools.partial(tables_kernel, half, lax.axis_size("rows")),
        out_shape=[shape, shape, table_like(own)],
        in_specs=[VMEM] * 3,
        out_specs=[VMEM] * 3,
        scratch_shapes=[pltpu.SemaphoreType.DMA((2,))],
        compiler_params=PARAMS,
        cost_estimate=cost(0, 4 * own.size * 2),
        name="block_tables",
    )(numbers, own, other)


def stack_kernel(own_ref, other_ref, table_ref, sems):
    for copy in stack(table_ref, own_ref, other_ref, sems):
        copy.wait()


def stacked(own, other):
    return pl.pallas_call(
        stack_kernel,
        out_shape=table_like(own),
        in_specs=[VMEM] * 2,
        out_specs=VMEM,
        scratch_shapes=[pltpu.SemaphoreType.DMA((2,))],
        compiler_params=PARAMS,
        cost_estimate=cost(0, 4 * own.size * 2),
        name="stack_squares",
    )(own, other)


def add_far(table, pieces, own):
    for position, piece in enumerate(pieces):
        for k in range(CAP):
            table[2 * own + position * CAP + k] = piece[k]


def row_product(table, index_ref, row, own_ref, other_ref, half, edge):
    stride = table_stride(half, edge)

    def left(k):
        ref = own_ref if k < half else other_ref
        return ref[row, :, (k % half) * edge : (k % half + 1) * edge]

    def right(k, s):
        place = index_ref[s * SUBLANES + k, row]
        begin = pl.multiple_of(lax.bitwise_and(place, stride - 1), edge)
        return table[lax.div(place, stride), :, pl.ds(begin, edge)]

    total = None
    for a in range(0, 2 * half, 2):
        pair = range(a, min(a + 2, 2 * half))
        lhs = jnp.concatenate([left(k) for k in pair], axis=1)
        rhs = jnp.concatenate(
            [jnp.concatenate([right(k, s) for s in range(half)], axis=1) for k in pair], axis=0
        )
        term = jnp.dot(lhs, rhs, preferred_element_type=jnp.float32)
        total = term if total is None else total + term
    return total


def square_kernel(half, index_ref, rows_ref, own_ref, other_ref, *refs):
    pieces = refs[1 : 1 + 2 * len(OFFSETS)]
    out, *wanted, table = refs[1 + len(pieces) :]
    own, edge, wide = own_ref.shape
    add_far(table, pieces, own)

    def body(i, carry):
        total = row_product(table, index_ref, i, own_ref, other_ref, half, edge)
        out[i] = total.astype(out.dtype)
        return carry

    lax.fori_loop(0, own, body, 0, unroll=2)
    for position, piece in enumerate(wanted):
        for k in range(CAP):
            piece[k] = out[rows_ref[position * CAP + k]]


def square(index, rows, own, other, table, pieces, half):
    size, edge, wide = own.shape
    piece = jax.ShapeDtypeStruct((CAP, edge, wide), own.dtype)
    count = len(OFFSETS)
    out = pl.pallas_call(
        functools.partial(square_kernel, half),
        out_shape=[like(own), *([piece] * count), like(table)],
        in_specs=[SMEM] * 2 + [VMEM] * (3 + len(pieces)),
        out_specs=[VMEM] * (2 + count),
        input_output_aliases={4: 1 + count},
        compiler_params=PARAMS,
        cost_estimate=cost(size * 4 * edge * wide * wide, 8 * own.size * 2),
        name="square_rows",
    )(index, rows, own, other, table, *pieces)
    return out[0], out[1 : 1 + count]


def cube_kernel(half, index_ref, own_ref, other_ref, *refs):
    pieces = refs[1 : 1 + 2 * len(OFFSETS)]
    out, table = refs[1 + len(pieces) :]
    own, edge, wide = own_ref.shape
    add_far(table, pieces, own)

    def body(i, carry):
        total = row_product(table, index_ref, i, own_ref, other_ref, half, edge)
        out[i] = (3.0 * table[i].astype(jnp.float32) - 2.0 * total).astype(out.dtype)
        return carry

    lax.fori_loop(0, own, body, 0, unroll=2)


def cube(index, own, other, table, pieces, half):
    size, edge, wide = own.shape
    return pl.pallas_call(
        functools.partial(cube_kernel, half),
        out_shape=[like(own), like(table)],
        in_specs=[SMEM] + [VMEM] * (3 + len(pieces)),
        out_specs=[VMEM] * 2,
        input_output_aliases={3: 1},
        compiler_params=PARAMS,
        cost_estimate=cost(size * 4 * edge * wide * wide, 8 * own.size * 2),
        name="cube_rows",
    )(index, own, other, table, *pieces)[0]


def local(density, columns, kept):
    half = columns.shape[1]
    numbers = everyones(columns, kept)
    other = from_sibling(density)
    rows, *pieces = gather(density, numbers, half)
    got = [from_ahead(piece, step) for step, piece in zip(OFFSETS, pieces)]
    square_index, cube_index, table = tables(numbers, density, other, half)
    got, square_index, cube_index, table = lax.optimization_barrier(
        (got, square_index, cube_index, table)
    )
    got += [from_sibling(piece) for piece in got]
    squares, wanted = square(square_index, rows, density, other, table, got, half)

    got = [from_ahead(piece, step) for step, piece in zip(OFFSETS, wanted)]
    table = stacked(squares, from_sibling(squares))
    got, table = lax.optimization_barrier((got, table))
    got += [from_sibling(piece) for piece in got]
    return cube(cube_index, density, other, table, got, half)


def solution(mesh):
    in_specs = (
        P(("groups", "rows"), None, "layers"),
        P(("groups", "rows"), "layers"),
        P(("groups", "rows"), "layers"),
    )
    out_specs = P(("groups", "rows"), None, "layers")
    return jax.shard_map(local, mesh=mesh, in_specs=in_specs, out_specs=out_specs, check_vma=False)
```

time: 474 us -> 67.4 us (0.14)
  local copies, waits for them, and re-layouts: 214 us -> 1.43 us
  matrix products: 88.8 us -> 0 us
  loops' own time: 55.9 us -> 0 us
  waiting for transfers between devices: 54.5 us -> 25.7 us
  starting transfers between devices: 29.9 us -> 12.8 us
  between operations: 13.4 us -> 0.06 us
  Pallas kernels: 0 us -> 12.7 us
  other arithmetic: 11 us -> 0.71 us
  blocking collectives: 3.98 us -> 13.7 us
    gather x112 -> x0, local copies, waits for them, and re-layouts: 113 us -> none  [the longest x64 84.9 us: row_terms(): table[index].reshape(groups, half_width, halves, edge, half_width, edge)]
    dot_general x64 -> x0, matrix products: 88.8 us -> none  [the longest x32 64.6 us: row_terms(): jnp.einsum('gxk,gkn->xn', left_half, selected, preferred_element_type=jnp...]
    another operation x2 -> x0, loops' own time: 55.9 us -> none  [product(): terms = lax.map(one_row, row_list)]
    reshape x35 -> x0, local copies, waits for them, and re-layouts: 45.1 us -> none  [the longest x32 44.8 us: row_terms(): selected = selected.reshape(groups, half_width * edge, count_out * edge)]
    another operation x34 -> x0, local copies, waits for them, and re-layouts: 25 us -> none
    reduce_scatter x2 -> x0, waiting for transfers between devices: 22.2 us -> none  [product(): return lax.psum_scatter(terms, 'layers', scatter_dimension=2, tiled=True)]
    dynamic_slice x64 -> x0, local copies, waits for them, and re-layouts: 18.8 us -> none  [the longest x32 18.5 us: product(): terms = lax.map(one_row, row_list)]
    ppermute x20 -> x18, starting transfers between devices: 29.8 us -> 12.8 us  [the longest x8 10 us: from_ahead(): return lax.ppermute(value, 'rows', pairs)]
  transfers between devices with their start and end apart: 23 -> 18, of which waited for: 9 -> 14; matrix products, arithmetic and copies ran while one was open for 4% -> 1% of each run, Pallas kernels for 0% -> 5%
where the time goes in v3:
time: 67.4 us; the launch traced here: 67.1 us
  waiting for transfers between devices  25.7 us (38%)
  blocking collectives  13.7 us (20%)
  starting transfers between devices  12.8 us (19%)
  Pallas kernels  12.7 us (19%)
  local copies, waits for them, and re-layouts  1.43 us (2%)
  other arithmetic  0.71 us (1%)
    ppermute x8, waiting for transfers between devices, from_ahead(): return lax.ppermute(value, 'rows', pairs)  23.2 us
    all_to_all x1, blocking collectives, everyones(): return lax.all_to_all(table, ('rows', 'layers'), 0, 0, tiled=True)  13.7 us
    ppermute x8, starting transfers between devices, from_ahead(): return lax.ppermute(value, 'rows', pairs)  10 us
    pallas_call x1, Pallas kernels, cube(): pl.pallas_call(functools.partial(cube_kernel, half), out_shape=[like(own)...  5.18 us
    pallas_call x1, Pallas kernels, square(): pl.pallas_call(functools.partial(square_kernel, half), out_shape=[like(ow...  4.11 us
    ppermute x10, starting transfers between devices, from_sibling(): return lax.ppermute(value, 'layers', [(0, 1), (1, 0)])  2.78 us
    pallas_call x1, Pallas kernels, gather(): pl.pallas_call(functools.partial(gather_kernel, own, half, lax.axis_size(...  2.55 us
    ppermute x10, waiting for transfers between devices, from_sibling(): return lax.ppermute(value, 'layers', [(0, 1), (1, 0)])  2.53 us
  transfers between devices with their start and end apart: 18, of which 14 were waited for; matrix products, arithmetic and copies ran while one was open for 1% of the time, Pallas kernels for 5%

profile of v3, /device:TPU:0, one launch (start us, length us, event | category | flops | bytes accessed | tf_op | source)
XLA Modules:
  0.0 67.1 jit_solution(7704932363220082320)
XLA Ops:
  0.0 0.5 collective-permute-start.4
  0.5 0.7 %add_bitcast_fusion = s32[6,16]{1,0:T(8,128)S(1)} fusion(s32[16,3]{0,1:T(4,128)} %param.5, s32[16,3]{0,1:T(4,128)} %param.4), kind=kLoop, calls=%fused_computation | loop fusion | flops 96 | bytes 768 | tf_op jit(solution)/shard_map/transpose | solution.py:40
  1.2 13.7 %all_to_all.5.numbers_ref = s32[16,8,128]{2,1,0:T(8,128)S(1)} all-to-all(s32[16,8,128]{2,1,0:T(8,128)S(1)} %broadcast_in_dim.2), channel_id=1, replica_groups=mesh['groups'=2,'rows'=8,'layers'=2] {'rows','layers'}, dimensions={0} | all-to-all | bytes 131072 | tf_op jit(solution)/shard_map/all_to_all | solution.py:44
  14.9 1.4 %copy-done = bf16[16,128,384]{2,1,0:T(8,128)(2,1)S(1)} copy-done((bf16[16,128,384]{2,1,0:T(8,128)(2,1)S(1)}, bf16[16,128,384]{2,1,0:T(8,128)(2,1)}, u32[]{:S(2)}) %copy-start) | copy-done | bytes 1572888
  16.3 2.5 %gather_rows.1 = (s32[8]{0:T(128)S(1)}, bf16[2,128,384]{2,1,0:T(8,128)(2,1)S(1)}, bf16[2,128,384]{2,1,0:T(8,128)(2,1)S(1)}, bf16[2,128,384]{2,1,0:T(8,128)(2,1)S(1)}, bf16[2,128,384]{2,1,0:T(8,128)(2,1)S(1)}) custom-call(bf16[16,128,384]{2,1,0:T(8,128)(2,1)S(1)} %copy-done, s32[16,8,128]{2,1,0:T(8,128)S(1)} %all_to_all.5.numbers_ref), custom_call_target="tpu_custom_call" | custom-call | bytes 1572864 | tf_op jit(solution)/shard_map/gather_rows/pallas_call | solution.py:78
  18.9 0.7 %collective-permute-start = (bf16[2,128,384]{2,1,0:T(8,128)(2,1)S(1)}, bf16[2,128,384]{2,1,0:T(8,128)(2,1)S(1)}, u32[]{:S(2)}, u32[]{:S(2)}) collective-permute-start(bf16[2,128,384]{2,1,0:T(8,128)(2,1)S(1)} %get-tuple-element.31), channel_id=1, source_target_pairs={{0,14},{2,0},{4,2},{6,4},{8,6},{10,8},{12,10},{14,12},{1,15},{3,1}... | collective-permute-start | bytes 589832 | tf_op jit(solution)/shard_map/ppermute | solution.py:32
  19.6 1.4 %collective-permute-start.1 = (bf16[2,128,384]{2,1,0:T(8,128)(2,1)S(1)}, bf16[2,128,384]{2,1,0:T(8,128)(2,1)S(1)}, u32[]{:S(2)}, u32[]{:S(2)}) collective-permute-start(bf16[2,128,384]{2,1,0:T(8,128)(2,1)S(1)} %get-tuple-element.32), channel_id=1, source_target_pairs={{0,2},{2,4},{4,6},{6,8},{8,10},{10,12},{12,14},{14,0},{1,3},{3,5},... | collective-permute-start | bytes 589832 | tf_op jit(solution)/shard_map/ppermute | solution.py:32
  21.0 0.6 collective-permute-start.2
  21.5 1.5 %collective-permute-start.3 = (bf16[2,128,384]{2,1,0:T(8,128)(2,1)S(1)}, bf16[2,128,384]{2,1,0:T(8,128)(2,1)S(1)}, u32[]{:S(2)}, u32[]{:S(2)}) collective-permute-start(bf16[2,128,384]{2,1,0:T(8,128)(2,1)S(1)} %get-tuple-element.34), channel_id=1, source_target_pairs={{0,4},{2,6},{4,8},{6,10},{8,12},{10,14},{12,0},{14,2},{1,5},{3,7},... | collective-permute-start | bytes 589832 | tf_op jit(solution)/shard_map/ppermute | solution.py:32
  23.0 0.6 block_tables.1
  23.6 5.4 %collective-permute-done.refs_1_ = bf16[2,128,384]{2,1,0:T(8,128)(2,1)S(1)} collective-permute-done((bf16[2,128,384]{2,1,0:T(8,128)(2,1)S(1)}, bf16[2,128,384]{2,1,0:T(8,128)(2,1)S(1)}, u32[]{:S(2)}, u32[]{:S(2)}) %collective-permute-start) | collective-permute-done | bytes 196640 | tf_op jit(solution)/shard_map/ppermute | solution.py:32
  29.0 1.1 %collective-permute-done.1.refs_2_ = bf16[2,128,384]{2,1,0:T(8,128)(2,1)S(1)} collective-permute-done((bf16[2,128,384]{2,1,0:T(8,128)(2,1)S(1)}, bf16[2,128,384]{2,1,0:T(8,128)(2,1)S(1)}, u32[]{:S(2)}, u32[]{:S(2)}) %collective-permute-start.1) | collective-permute-done | bytes 196640 | tf_op jit(solution)/shard_map/ppermute | solution.py:32
  30.3 3.7 %collective-permute-done.3.refs_4_ = bf16[2,128,384]{2,1,0:T(8,128)(2,1)S(1)} collective-permute-done((bf16[2,128,384]{2,1,0:T(8,128)(2,1)S(1)}, bf16[2,128,384]{2,1,0:T(8,128)(2,1)S(1)}, u32[]{:S(2)}, u32[]{:S(2)}) %collective-permute-start.3) | collective-permute-done | bytes 196640 | tf_op jit(solution)/shard_map/ppermute | solution.py:32
  34.1 0.5 collective-permute-start.6
  34.6 0.5 collective-permute-start.8
  35.1 0.4 collective-permute-done.5.refs_5_
  35.5 0.3 collective-permute-done.6.refs_6_
  36.1 0.3 collective-permute-done.8.refs_8_
  36.4 4.1 %square_rows.1 = (bf16[16,128,384]{2,1,0:T(8,128)(2,1)S(1)}, bf16[2,128,384]{2,1,0:T(8,128)(2,1)S(1)}, bf16[2,128,384]{2,1,0:T(8,128)(2,1)S(1)}, bf16[2,128,384]...) custom-call(s32[24,128]{1,0:T(8,128)S(1)} %get-tuple-element.39.inde, ...), custom_call_target="tpu_custom_call", output_to_operand_aliasing={{5}: (4, {})} | custom-call | flops 1207959552 | bytes 12582912 | tf_op jit(solution)/shard_map/square_rows/pallas_call | solution.py:251
  40.5 0.3 collective-permute-start.13
  40.8 2.9 %collective-permute-start.9 = (bf16[2,128,384]{2,1,0:T(8,128)(2,1)S(1)}, bf16[2,128,384]{2,1,0:T(8,128)(2,1)S(1)}, u32[]{:S(2)}, u32[]{:S(2)}) collective-permute-start(bf16[2,128,384]{2,1,0:T(8,128)(2,1)S(1)} %get-tuple-element.46), channel_id=1, source_target_pairs={{0,14},{2,0},{4,2},{6,4},{8,6},{10,8},{12,10},{14,12},{1,15},{3,1}... | collective-permute-start | bytes 589832 | tf_op jit(solution)/shard_map/ppermute | solution.py:32
  43.6 1.0 %collective-permute-start.10 = (bf16[2,128,384]{2,1,0:T(8,128)(2,1)S(1)}, bf16[2,128,384]{2,1,0:T(8,128)(2,1)S(1)}, u32[]{:S(2)}, u32[]{:S(2)}) collective-permute-start(bf16[2,128,384]{2,1,0:T(8,128)(2,1)S(1)} %get-tuple-element.47), channel_id=1, source_target_pairs={{0,2},{2,4},{4,6},{6,8},{8,10},{10,12},{12,14},{14,0},{1,3},{3,5},... | collective-permute-start | bytes 589832 | tf_op jit(solution)/shard_map/ppermute | solution.py:32
  44.7 0.8 %collective-permute-start.11 = (bf16[2,128,384]{2,1,0:T(8,128)(2,1)S(1)}, bf16[2,128,384]{2,1,0:T(8,128)(2,1)S(1)}, u32[]{:S(2)}, u32[]{:S(2)}) collective-permute-start(bf16[2,128,384]{2,1,0:T(8,128)(2,1)S(1)} %get-tuple-element.48), channel_id=1, source_target_pairs={{0,12},{2,14},{4,0},{6,2},{8,4},{10,6},{12,8},{14,10},{1,13},{3,15... | collective-permute-start | bytes 589832 | tf_op jit(solution)/shard_map/ppermute | solution.py:32
  45.5 1.2 %collective-permute-start.12 = (bf16[2,128,384]{2,1,0:T(8,128)(2,1)S(1)}, bf16[2,128,384]{2,1,0:T(8,128)(2,1)S(1)}, u32[]{:S(2)}, u32[]{:S(2)}) collective-permute-start(bf16[2,128,384]{2,1,0:T(8,128)(2,1)S(1)} %get-tuple-element.49), channel_id=1, source_target_pairs={{0,4},{2,6},{4,8},{6,10},{8,12},{10,14},{12,0},{14,2},{1,5},{3,7},... | collective-permute-start | bytes 589832 | tf_op jit(solution)/shard_map/ppermute | solution.py:32
  46.9 7.3 %collective-permute-done.9.refs_1_ = bf16[2,128,384]{2,1,0:T(8,128)(2,1)S(1)} collective-permute-done((bf16[2,128,384]{2,1,0:T(8,128)(2,1)S(1)}, bf16[2,128,384]{2,1,0:T(8,128)(2,1)S(1)}, u32[]{:S(2)}, u32[]{:S(2)}) %collective-permute-start.9) | collective-permute-done | bytes 196640 | tf_op jit(solution)/shard_map/ppermute | solution.py:32
  54.2 5.4 %collective-permute-done.11.refs_3_ = bf16[2,128,384]{2,1,0:T(8,128)(2,1)S(1)} collective-permute-done((bf16[2,128,384]{2,1,0:T(8,128)(2,1)S(1)}, bf16[2,128,384]{2,1,0:T(8,128)(2,1)S(1)}, u32[]{:S(2)}, u32[]{:S(2)}) %collective-permute-start.11) | collective-permute-done | bytes 196640 | tf_op jit(solution)/shard_map/ppermute | solution.py:32
  59.7 0.5 collective-permute-start.15
  60.2 0.5 collective-permute-start.17
  60.7 0.4 collective-permute-done.14.refs_5_
  61.4 0.3 collective-permute-done.16.refs_7_
  61.7 0.3 collective-permute-done.17.refs_8_
  61.9 5.2 %cube_rows.1 = (bf16[16,128,384]{2,1,0:T(8,128)(2,1)}, bf16[49,128,384]{2,1,0:T(8,128)(2,1)S(1)}) custom-call(s32[24,128]{1,0:T(8,128)S(1)} %get-tuple-element.38.index_ref, bf16[16,128,384]{2,1,0:T(8,128)(2,1)S(1)} %copy-done.1, bf16[16,128,384]{2,1,0:T(8,128)(2,1)S(1)} %collective-permute-done.4.other_ref, ...), custom_call_target="tpu_custom_call", output_to_operand_aliasing={{1}: (3, {})} | custom-call | flops 1207959552 | bytes 12582912 | tf_op jit(solution)/shard_map/cube_rows/pallas_call | solution.py:280
  (17 shorter events, 1.1 us)
Async XLA Ops:
  0.0 23.0 %collective-permute-start.4 = (bf16[16,128,384]{2,1,0:T(8,128)(2,1)}, bf16[16,128,384]{2,1,0:T(8,128)(2,1)S(1)}, u32[]{:S(2)}, u32[]{:S(2)}) collective-permute-start(bf16[16,128,384]{2,1,0:T(8,128)(2,1)} %own_ref.5), channel_id=1, source_target_pairs={{0,1},{1,0},{2,3},{3,2},{4,5},{5,4},{6,7},{7,6},{8,9},{9,8},{10,11... | collective-permute-start | bytes 4718600 | tf_op jit(solution)/shard_map/ppermute | solution.py:36
  14.9 1.4 %copy-start = (bf16[16,128,384]{2,1,0:T(8,128)(2,1)S(1)}, bf16[16,128,384]{2,1,0:T(8,128)(2,1)}, u32[]{:S(2)}) copy-start(bf16[16,128,384]{2,1,0:T(8,128)(2,1)} %own_ref.5) | copy-start | bytes 4718596
  18.9 10.1 %collective-permute-start = (bf16[2,128,384]{2,1,0:T(8,128)(2,1)S(1)}, bf16[2,128,384]{2,1,0:T(8,128)(2,1)S(1)}, u32[]{:S(2)}, u32[]{:S(2)}) collective-permute-start(bf16[2,128,384]{2,1,0:T(8,128)(2,1)S(1)} %get-tuple-element.31), channel_id=1, source_target_pairs={{0,14},{2,0},{4,2},{6,4},{8,6},{10,8},{12,10},{14,12},{1,15},{3,1}... | collective-permute-start | bytes 589832 | tf_op jit(solution)/shard_map/ppermute | solution.py:32
  19.6 10.5 %collective-permute-start.1 = (bf16[2,128,384]{2,1,0:T(8,128)(2,1)S(1)}, bf16[2,128,384]{2,1,0:T(8,128)(2,1)S(1)}, u32[]{:S(2)}, u32[]{:S(2)}) collective-permute-start(bf16[2,128,384]{2,1,0:T(8,128)(2,1)S(1)} %get-tuple-element.32), channel_id=1, source_target_pairs={{0,2},{2,4},{4,6},{6,8},{8,10},{10,12},{12,14},{14,0},{1,3},{3,5},... | collective-permute-start | bytes 589832 | tf_op jit(solution)/shard_map/ppermute | solution.py:32
  21.0 9.4 %collective-permute-start.2 = (bf16[2,128,384]{2,1,0:T(8,128)(2,1)S(1)}, bf16[2,128,384]{2,1,0:T(8,128)(2,1)S(1)}, u32[]{:S(2)}, u32[]{:S(2)}) collective-permute-start(bf16[2,128,384]{2,1,0:T(8,128)(2,1)S(1)} %get-tuple-element.33), channel_id=1, source_target_pairs={{0,12},{2,14},{4,0},{6,2},{8,4},{10,6},{12,8},{14,10},{1,13},{3,15... | collective-permute-start | bytes 589832 | tf_op jit(solution)/shard_map/ppermute | solution.py:32
  21.5 14.8 %copy-start.1 = (bf16[16,128,384]{2,1,0:T(8,128)(2,1)S(1)}, bf16[16,128,384]{2,1,0:T(8,128)(2,1)}, u32[]{:S(2)}) copy-start(bf16[16,128,384]{2,1,0:T(8,128)(2,1)} %own_ref.5) | copy-start | bytes 4718596
  21.5 12.5 %collective-permute-start.3 = (bf16[2,128,384]{2,1,0:T(8,128)(2,1)S(1)}, bf16[2,128,384]{2,1,0:T(8,128)(2,1)S(1)}, u32[]{:S(2)}, u32[]{:S(2)}) collective-permute-start(bf16[2,128,384]{2,1,0:T(8,128)(2,1)S(1)} %get-tuple-element.34), channel_id=1, source_target_pairs={{0,4},{2,6},{4,8},{6,10},{8,12},{10,14},{12,0},{14,2},{1,5},{3,7},... | collective-permute-start | bytes 589832 | tf_op jit(solution)/shard_map/ppermute | solution.py:32
  34.1 1.4 %collective-permute-start.5 = (bf16[2,128,384]{2,1,0:T(8,128)(2,1)S(1)}, bf16[2,128,384]{2,1,0:T(8,128)(2,1)S(1)}, u32[]{:S(2)}, u32[]{:S(2)}) collective-permute-start(bf16[2,128,384]{2,1,0:T(8,128)(2,1)S(1)} %collective-permute-done.refs_1_), channel_id=1, source_target_pairs={{0,1},{1,0},{2,3},{3,2},{4,5},{5,4},{6,7},{7,6},{8,9},{9,8},{10,11... | collective-permute-start | bytes 589832 | tf_op jit(solution)/shard_map/ppermute | solution.py:36
  34.1 1.7 %collective-permute-start.6 = (bf16[2,128,384]{2,1,0:T(8,128)(2,1)S(1)}, bf16[2,128,384]{2,1,0:T(8,128)(2,1)S(1)}, u32[]{:S(2)}, u32[]{:S(2)}) collective-permute-start(bf16[2,128,384]{2,1,0:T(8,128)(2,1)S(1)} %collective-permute-done.1.refs_2_), channel_id=1, source_target_pairs={{0,1},{1,0},{2,3},{3,2},{4,5},{5,4},{6,7},{7,6},{8,9},{9,8},{10,11... | collective-permute-start | bytes 589832 | tf_op jit(solution)/shard_map/ppermute | solution.py:36
  34.6 1.5 %collective-permute-start.7 = (bf16[2,128,384]{2,1,0:T(8,128)(2,1)S(1)}, bf16[2,128,384]{2,1,0:T(8,128)(2,1)S(1)}, u32[]{:S(2)}, u32[]{:S(2)}) collective-permute-start(bf16[2,128,384]{2,1,0:T(8,128)(2,1)S(1)} %collective-permute-done.2.refs_3_), channel_id=1, source_target_pairs={{0,1},{1,0},{2,3},{3,2},{4,5},{5,4},{6,7},{7,6},{8,9},{9,8},{10,11... | collective-permute-start | bytes 589832 | tf_op jit(solution)/shard_map/ppermute | solution.py:36
  34.6 1.8 %collective-permute-start.8 = (bf16[2,128,384]{2,1,0:T(8,128)(2,1)S(1)}, bf16[2,128,384]{2,1,0:T(8,128)(2,1)S(1)}, u32[]{:S(2)}, u32[]{:S(2)}) collective-permute-start(bf16[2,128,384]{2,1,0:T(8,128)(2,1)S(1)} %collective-permute-done.3.refs_4_), channel_id=1, source_target_pairs={{0,1},{1,0},{2,3},{3,2},{4,5},{5,4},{6,7},{7,6},{8,9},{9,8},{10,11... | collective-permute-start | bytes 589832 | tf_op jit(solution)/shard_map/ppermute | solution.py:36
  40.5 6.2 %collective-permute-start.13 = (bf16[16,128,384]{2,1,0:T(8,128)(2,1)S(1)}, bf16[16,128,384]{2,1,0:T(8,128)(2,1)S(1)}, u32[]{:S(2)}, u32[]{:S(2)}) collective-permute-start(bf16[16,128,384]{2,1,0:T(8,128)(2,1)S(1)} %get-tuple-element.50.own_ref), channel_id=1, source_target_pairs={{0,1},{1,0},{2,3},{3,2},{4,5},{5,4},{6,7},{7,6},{8,9},{9,8},{10,11... | collective-permute-start | bytes 4718600 | tf_op jit(solution)/shard_map/ppermute | solution.py:36
  40.8 13.4 %collective-permute-start.9 = (bf16[2,128,384]{2,1,0:T(8,128)(2,1)S(1)}, bf16[2,128,384]{2,1,0:T(8,128)(2,1)S(1)}, u32[]{:S(2)}, u32[]{:S(2)}) collective-permute-start(bf16[2,128,384]{2,1,0:T(8,128)(2,1)S(1)} %get-tuple-element.46), channel_id=1, source_target_pairs={{0,14},{2,0},{4,2},{6,4},{8,6},{10,8},{12,10},{14,12},{1,15},{3,1}... | collective-permute-start | bytes 589832 | tf_op jit(solution)/shard_map/ppermute | solution.py:32
  43.6 10.6 %collective-permute-start.10 = (bf16[2,128,384]{2,1,0:T(8,128)(2,1)S(1)}, bf16[2,128,384]{2,1,0:T(8,128)(2,1)S(1)}, u32[]{:S(2)}, u32[]{:S(2)}) collective-permute-start(bf16[2,128,384]{2,1,0:T(8,128)(2,1)S(1)} %get-tuple-element.47), channel_id=1, source_target_pairs={{0,2},{2,4},{4,6},{6,8},{8,10},{10,12},{12,14},{14,0},{1,3},{3,5},... | collective-permute-start | bytes 589832 | tf_op jit(solution)/shard_map/ppermute | solution.py:32
  44.7 15.0 %collective-permute-start.11 = (bf16[2,128,384]{2,1,0:T(8,128)(2,1)S(1)}, bf16[2,128,384]{2,1,0:T(8,128)(2,1)S(1)}, u32[]{:S(2)}, u32[]{:S(2)}) collective-permute-start(bf16[2,128,384]{2,1,0:T(8,128)(2,1)S(1)} %get-tuple-element.48), channel_id=1, source_target_pairs={{0,12},{2,14},{4,0},{6,2},{8,4},{10,6},{12,8},{14,10},{1,13},{3,15... | collective-permute-start | bytes 589832 | tf_op jit(solution)/shard_map/ppermute | solution.py:32
  45.5 14.2 %collective-permute-start.12 = (bf16[2,128,384]{2,1,0:T(8,128)(2,1)S(1)}, bf16[2,128,384]{2,1,0:T(8,128)(2,1)S(1)}, u32[]{:S(2)}, u32[]{:S(2)}) collective-permute-start(bf16[2,128,384]{2,1,0:T(8,128)(2,1)S(1)} %get-tuple-element.49), channel_id=1, source_target_pairs={{0,4},{2,6},{4,8},{6,10},{8,12},{10,14},{12,0},{14,2},{1,5},{3,7},... | collective-permute-start | bytes 589832 | tf_op jit(solution)/shard_map/ppermute | solution.py:32
  59.7 1.4 %collective-permute-start.14 = (bf16[2,128,384]{2,1,0:T(8,128)(2,1)S(1)}, bf16[2,128,384]{2,1,0:T(8,128)(2,1)S(1)}, u32[]{:S(2)}, u32[]{:S(2)}) collective-permute-start(bf16[2,128,384]{2,1,0:T(8,128)(2,1)S(1)} %collective-permute-done.9.refs_1_), channel_id=1, source_target_pairs={{0,1},{1,0},{2,3},{3,2},{4,5},{5,4},{6,7},{7,6},{8,9},{9,8},{10,11... | collective-permute-start | bytes 589832 | tf_op jit(solution)/shard_map/ppermute | solution.py:36
  59.7 1.7 %collective-permute-start.15 = (bf16[2,128,384]{2,1,0:T(8,128)(2,1)S(1)}, bf16[2,128,384]{2,1,0:T(8,128)(2,1)S(1)}, u32[]{:S(2)}, u32[]{:S(2)}) collective-permute-start(bf16[2,128,384]{2,1,0:T(8,128)(2,1)S(1)} %collective-permute-done.10.refs_2_), channel_id=1, source_target_pairs={{0,1},{1,0},{2,3},{3,2},{4,5},{5,4},{6,7},{7,6},{8,9},{9,8},{10,11... | collective-permute-start | bytes 589832 | tf_op jit(solution)/shard_map/ppermute | solution.py:36
  60.2 1.5 %collective-permute-start.16 = (bf16[2,128,384]{2,1,0:T(8,128)(2,1)S(1)}, bf16[2,128,384]{2,1,0:T(8,128)(2,1)S(1)}, u32[]{:S(2)}, u32[]{:S(2)}) collective-permute-start(bf16[2,128,384]{2,1,0:T(8,128)(2,1)S(1)} %collective-permute-done.11.refs_3_), channel_id=1, source_target_pairs={{0,1},{1,0},{2,3},{3,2},{4,5},{5,4},{6,7},{7,6},{8,9},{9,8},{10,11... | collective-permute-start | bytes 589832 | tf_op jit(solution)/shard_map/ppermute | solution.py:36
  60.2 1.8 %collective-permute-start.17 = (bf16[2,128,384]{2,1,0:T(8,128)(2,1)S(1)}, bf16[2,128,384]{2,1,0:T(8,128)(2,1)S(1)}, u32[]{:S(2)}, u32[]{:S(2)}) collective-permute-start(bf16[2,128,384]{2,1,0:T(8,128)(2,1)S(1)} %collective-permute-done.12.refs_4_), channel_id=1, source_target_pairs={{0,1},{1,0},{2,3},{3,2},{4,5},{5,4},{6,7},{7,6},{8,9},{9,8},{10,11... | collective-permute-start | bytes 589832 | tf_op jit(solution)/shard_map/ppermute | solution.py:36

commit v4 on v3

v4 whole, which is shorter than its diff:
```python
import functools

import jax
import jax.numpy as jnp
from jax import lax
from jax.experimental import pallas as pl
from jax.experimental.pallas import tpu as pltpu
from jax.sharding import PartitionSpec as P

CAP = 2
OFFSETS = (1, -2, -1, 2)
FAR = len(OFFSETS) * CAP
BEHIND = tuple(OFFSETS.index(-step) for step in OFFSETS)
SUBLANES, LANES = 8, 128
VMEM_LIMIT = 40 * 1024 * 1024
PARAMS = pltpu.CompilerParams(vmem_limit_bytes=VMEM_LIMIT)
VMEM = pl.BlockSpec(memory_space=pltpu.VMEM)
SMEM = pl.BlockSpec(memory_space=pltpu.SMEM)


def cost(flops, size):
    return pl.CostEstimate(flops=flops, bytes_accessed=size, transcendentals=0)


def like(value):
    return jax.ShapeDtypeStruct(value.shape, value.dtype)


def from_ahead(value, steps):
    count = lax.axis_size("rows")
    pairs = [(source, (source - steps) % count) for source in range(count)]
    return lax.ppermute(value, "rows", pairs)


def from_sibling(value):
    return lax.ppermute(value, "layers", [(0, 1), (1, 0)])


def stage_kernel(density_ref, staged_ref, sem):
    copy = pltpu.make_async_copy(density_ref, staged_ref, sem)
    copy.start()
    copy.wait()


def stage(density):
    return pl.pallas_call(
        stage_kernel,
        out_shape=like(density),
        in_specs=[pl.BlockSpec(memory_space=pl.ANY)],
        out_specs=VMEM,
        scratch_shapes=[pltpu.SemaphoreType.DMA],
        compiler_params=PARAMS,
        cost_estimate=cost(0, 4 * density.size),
        name="stage_density",
    )(density)


def spread(columns, kept):
    table = jnp.concatenate([columns, kept], axis=1).T
    return jnp.pad(table, ((0, SUBLANES - table.shape[0]), (0, LANES - table.shape[1])))


def named_rows(slots_of_both, owner, own):
    low, high = [], []
    for slots in slots_of_both:
        local = slots - owner * own
        lane = lax.broadcasted_iota(jnp.int32, local.shape, 1)
        inside = (local >= 0) & (local < own) & (lane < own)
        low.append(jnp.where(inside, local, own - 1))
        high.append(jnp.where(inside, local, 0))
    return jnp.minimum(*low), jnp.maximum(*high)


def gather_kernel(half, density_ref, numbers_ref, out):
    both = [numbers_ref[k : k + half] for k in (0, SUBLANES)]
    low, high = named_rows(both, lax.axis_index("rows"), density_ref.shape[0])
    for k, row in enumerate((jnp.min(low), jnp.max(high))):
        out[k] = density_ref[row]


def gather(density, numbers, half):
    own, edge, wide = density.shape
    return pl.pallas_call(
        functools.partial(gather_kernel, half),
        out_shape=jax.ShapeDtypeStruct((CAP, edge, wide), density.dtype),
        in_specs=[VMEM] * 2,
        out_specs=VMEM,
        compiler_params=PARAMS,
        cost_estimate=cost(0, 4 * CAP * edge * wide),
        name="gather_rows",
    )(density, numbers)


def stack(table, own_ref, other_ref, sems):
    own = own_ref.shape[0]
    copies = [
        pltpu.make_async_copy(own_ref, table.at[pl.ds(0, own)], sems.at[0]),
        pltpu.make_async_copy(other_ref, table.at[pl.ds(own, own)], sems.at[1]),
    ]
    for copy in copies:
        copy.start()
    table[table.shape[0] - 1] = jnp.zeros(table.shape[1:], table.dtype)
    return copies


def tables_kernel(half, peers, mine_ref, own_ref, other_ref, *refs):
    near, refs = refs[: len(OFFSETS)], refs[len(OFFSETS) :]
    square_ref, others_ref, cube_ref, table_ref, sems = refs
    own, edge, wide = own_ref.shape
    copies = stack(table_ref, own_ref, other_ref, sems)
    me = lax.axis_index("rows")
    shape = (SUBLANES, LANES)
    lane = lax.broadcasted_iota(jnp.int32, shape, 1)
    pad = jnp.zeros((SUBLANES - 2 * half, LANES), jnp.int32)

    def slots_of(ref):
        return [
            jnp.concatenate(
                [ref[k : k + half], ref[SUBLANES + k : SUBLANES + k + half], pad], axis=0
            )
            for k in (0, half)
        ]

    def bounds(slots_of_both, owner):
        low, high = named_rows(slots_of_both, owner, own)
        low = jnp.min(jnp.min(low, axis=0, keepdims=True), axis=1, keepdims=True)
        high = jnp.max(jnp.max(high, axis=0, keepdims=True), axis=1, keepdims=True)
        return low, high

    columns, kept = slots_of(mine_ref)
    named = (columns[0:half], columns[half : 2 * half])
    column_table, kept_table = columns, kept
    slots = columns - me * own
    for position, step in enumerate(OFFSETS):
        owner = lax.rem(me + step + peers, peers)
        low, high = bounds(named, owner)
        local = columns - owner * own
        first = own + position * CAP
        slots = jnp.where(
            (local >= 0) & (local < own), first + (local != low).astype(jnp.int32), slots
        )
        far_columns, far_kept = slots_of(near[position])
        source = jnp.where(lane == first, low, high)
        here = (lane == first) | (lane == first + 1)
        column_table = jnp.where(
            here, jnp.take_along_axis(far_columns, source, axis=1), column_table
        )
        kept_table = jnp.where(here, jnp.take_along_axis(far_kept, source, axis=1), kept_table)
    asked = jnp.zeros((1, LANES), jnp.int32)
    for position, behind in enumerate(BEHIND):
        numbers = near[behind]
        pair = bounds([numbers[k : k + half] for k in (0, SUBLANES)], me)
        for k in range(CAP):
            asked = jnp.where(lane[0:1] == position * CAP + k, pair[k], asked)
    slots = jnp.where(lane < own, jnp.clip(slots, 0, LANES - 1), 0)
    stride = table_stride(half, edge)
    base = jnp.where(slots < own, slots, slots + own)
    shift = jnp.where(slots < own, own, FAR)
    empty = (table_ref.shape[0] - 1) * stride
    for table, outs in (
        (column_table, ((square_ref, 0), (others_ref, half))),
        (kept_table, ((cube_ref, 0),)),
    ):
        met = [
            jnp.take_along_axis(jnp.broadcast_to(table[b : b + 1], shape), slots, axis=1)
            for b in range(2 * half)
        ]
        for out, first in outs:
            for s in range(half):
                index = jnp.full(shape, empty, jnp.int32)
                for b in range(2 * half):
                    entry = base + shift if b >= half else base
                    place = entry * stride + (b % half) * edge
                    index = jnp.where(met[b] == kept[first + s : first + s + 1], place, index)
                out[s * SUBLANES : (s + 1) * SUBLANES] = index
    square_ref[SUBLANES - 1 : SUBLANES] = asked
    for copy in copies:
        copy.wait()


def table_stride(half, edge):
    return edge << (half - 1).bit_length()


def table_like(own):
    return jax.ShapeDtypeStruct((2 * own.shape[0] + 2 * FAR + 1,) + own.shape[1:], own.dtype)


def tables(mine, near, own, other, half):
    shape = jax.ShapeDtypeStruct((half * SUBLANES, LANES), jnp.int32)
    return pl.pallas_call(
        functools.partial(tables_kernel, half, lax.axis_size("rows")),
        out_shape=[shape, shape, shape, table_like(own)],
        in_specs=[VMEM] * (3 + len(near)),
        out_specs=[VMEM] * 4,
        scratch_shapes=[pltpu.SemaphoreType.DMA((2,))],
        compiler_params=PARAMS,
        cost_estimate=cost(0, 4 * own.size * 2),
        name="block_tables",
    )(mine, own, other, *near)


def others_kernel(half, index_ref, own_ref, other_ref, table_ref, squares_ref, out, sem):
    own, edge, wide = own_ref.shape
    copy = pltpu.make_async_copy(squares_ref, out.at[pl.ds(0, own)], sem)
    copy.start()
    out[out.shape[0] - 1] = jnp.zeros(out.shape[1:], out.dtype)

    def body(i, carry):
        total = row_product(table_ref, index_ref, i, own_ref, other_ref, half, edge)
        out[own + i] = total.astype(out.dtype)
        return carry

    lax.fori_loop(0, own, body, 0, unroll=True)
    copy.wait()


def with_others(index, own, other, table, squares, half):
    size, edge, wide = own.shape
    return pl.pallas_call(
        functools.partial(others_kernel, half),
        out_shape=like(table),
        in_specs=[SMEM] + [VMEM] * 4,
        out_specs=VMEM,
        scratch_shapes=[pltpu.SemaphoreType.DMA],
        compiler_params=PARAMS,
        cost_estimate=cost(size * 4 * edge * wide * wide, 8 * own.size * 2),
        name="square_others",
    )(index, own, other, table, squares)


def add_far(table, pieces, own):
    for position, piece in enumerate(pieces):
        for k in range(CAP):
            table[2 * own + position * CAP + k] = piece[k]


def row_product(table, index_ref, row, own_ref, other_ref, half, edge):
    stride = table_stride(half, edge)

    def left(k):
        ref = own_ref if k < half else other_ref
        return ref[row, :, (k % half) * edge : (k % half + 1) * edge]

    def right(k, s):
        place = index_ref[s * SUBLANES + k, row]
        begin = pl.multiple_of(lax.bitwise_and(place, stride - 1), edge)
        return table[lax.div(place, stride), :, pl.ds(begin, edge)]

    total = None
    for a in range(0, 2 * half, 2):
        pair = range(a, min(a + 2, 2 * half))
        lhs = jnp.concatenate([left(k) for k in pair], axis=1)
        rhs = jnp.concatenate(
            [jnp.concatenate([right(k, s) for s in range(half)], axis=1) for k in pair], axis=0
        )
        term = jnp.dot(lhs, rhs, preferred_element_type=jnp.float32)
        total = term if total is None else total + term
    return total


def square_kernel(half, index_ref, own_ref, other_ref, *refs):
    pieces = refs[1 : 1 + 2 * len(OFFSETS)]
    out, *wanted, table = refs[1 + len(pieces) :]
    own, edge, wide = own_ref.shape
    add_far(table, pieces, own)

    def body(i, carry):
        total = row_product(table, index_ref, i, own_ref, other_ref, half, edge)
        out[i] = total.astype(out.dtype)
        return carry

    lax.fori_loop(0, own, body, 0, unroll=True)
    for position, piece in enumerate(wanted):
        for k in range(CAP):
            piece[k] = out[index_ref[SUBLANES - 1, position * CAP + k]]


def square(index, own, other, table, pieces, half):
    size, edge, wide = own.shape
    piece = jax.ShapeDtypeStruct((CAP, edge, wide), own.dtype)
    count = len(OFFSETS)
    out = pl.pallas_call(
        functools.partial(square_kernel, half),
        out_shape=[like(own), *([piece] * count), like(table)],
        in_specs=[SMEM] + [VMEM] * (3 + len(pieces)),
        out_specs=[VMEM] * (2 + count),
        input_output_aliases={3: 1 + count},
        compiler_params=PARAMS,
        cost_estimate=cost(size * 4 * edge * wide * wide, 8 * own.size * 2),
        name="square_rows",
    )(index, own, other, table, *pieces)
    return out[0], out[1 : 1 + count], out[1 + count]


def cube_kernel(half, index_ref, own_ref, other_ref, *refs):
    pieces = refs[1 : 1 + 2 * len(OFFSETS)]
    result, table, out, sems = refs[1 + len(pieces) :]
    own, edge, wide = own_ref.shape
    add_far(table, pieces, own)

    def written(i):
        return pltpu.make_async_copy(out.at[i], result.at[i], sems.at[i])

    def body(i, carry):
        total = row_product(table, index_ref, i, own_ref, other_ref, half, edge)
        out[i] = (3.0 * table[i].astype(jnp.float32) - 2.0 * total).astype(out.dtype)
        written(i).start()
        return carry

    lax.fori_loop(0, own, body, 0, unroll=True)
    for i in range(own):
        written(i).wait()


def cube(index, own, other, table, pieces, half):
    size, edge, wide = own.shape
    return pl.pallas_call(
        functools.partial(cube_kernel, half),
        out_shape=[like(own), like(table)],
        in_specs=[SMEM] + [VMEM] * (3 + len(pieces)),
        out_specs=[pl.BlockSpec(memory_space=pl.ANY), VMEM],
        input_output_aliases={3: 1},
        scratch_shapes=[pltpu.VMEM(own.shape, own.dtype), pltpu.SemaphoreType.DMA((size,))],
        compiler_params=PARAMS,
        cost_estimate=cost(size * 4 * edge * wide * wide, 8 * own.size * 2),
        name="cube_rows",
    )(index, own, other, table, *pieces)[0]


def local(density, columns, kept):
    half = columns.shape[1]
    other = from_sibling(density)
    numbers = spread(columns, kept)
    mine = jnp.concatenate([numbers, from_sibling(numbers)], axis=0)
    mine, own = lax.optimization_barrier((mine, stage(density)))
    near = [from_ahead(mine, step) for step in OFFSETS]
    pieces = [gather(own, near[behind], half) for behind in BEHIND]
    got = [from_ahead(piece, step) for step, piece in zip(OFFSETS, pieces)]
    *indices, table = tables(mine, near, own, other, half)
    got = [lax.optimization_barrier((piece, table))[0] for piece in got]
    got += [from_sibling(piece) for piece in got]
    square_index, others_index, cube_index = indices
    squares, wanted, table = square(square_index, own, other, table, got, half)

    got = [from_ahead(piece, step) for step, piece in zip(OFFSETS, wanted)]
    table = with_others(others_index, own, other, table, squares, half)
    got = [lax.optimization_barrier((piece, table))[0] for piece in got]
    got += [from_sibling(piece) for piece in got]
    return cube(cube_index, own, other, table, got, half)


def solution(mesh):
    in_specs = (
        P(("groups", "rows"), None, "layers"),
        P(("groups", "rows"), "layers"),
        P(("groups", "rows"), "layers"),
    )
    out_specs = P(("groups", "rows"), None, "layers")
    return jax.shard_map(local, mesh=mesh, in_specs=in_specs, out_specs=out_specs, check_vma=False)
```

time: 67.4 us -> 55.4 us (0.82)
  blocking collectives: 13.7 us -> 0 us
  starting transfers between devices: 12.8 us -> 24.8 us
  waiting for transfers between devices: 25.7 us -> 16.7 us
  Pallas kernels: 12.7 us -> 11.4 us
    all_to_all x1 -> x0, blocking collectives: 13.7 us -> none  [everyones(): return lax.all_to_all(table, ('rows', 'layers'), 0, 0, tiled=True)]
    ppermute x8 -> x12, starting transfers between devices: 10 us -> 23.2 us  [from_ahead(): return lax.ppermute(value, 'rows', pairs)]
    ppermute x8 -> x12, waiting for transfers between devices: 23.2 us -> 13.4 us  [from_ahead(): return lax.ppermute(value, 'rows', pairs)]
    pallas_call x1, Pallas kernels: 5.18 us -> 3.94 us  [cube(): pl.pallas_call(functools.partial(cube_kernel, half), out_shape=[like(own)...]
    pallas_call x1, Pallas kernels: 4.11 us -> 2.95 us  [square(): pl.pallas_call(functools.partial(square_kernel, half), out_shape=[like(ow...]
    ppermute x10, starting transfers between devices: 2.78 us -> 1.67 us  [from_sibling(): return lax.ppermute(value, 'layers', [(0, 1), (1, 0)])]
    pallas_call x2 -> x6, Pallas kernels: 2.79 us -> 3.89 us  [the longest x1 2.88 us: with_others(): pl.pallas_call(functools.partial(others_kernel, half), out_shape=like(tab...]
    ppermute x10, waiting for transfers between devices: 2.53 us -> 3.37 us  [from_sibling(): return lax.ppermute(value, 'layers', [(0, 1), (1, 0)])]
  transfers between devices with their start and end apart: 18 -> 22, of which waited for: 14 -> 13; matrix products, arithmetic and copies ran while one was open for 1% -> 1% of each run, Pallas kernels for 5% -> 8%
where the time goes in v4:
time: 55.4 us; the launch traced here: 55.2 us
  starting transfers between devices  24.8 us (45%)
  waiting for transfers between devices  16.7 us (30%)
  Pallas kernels  11.4 us (21%)
  local copies, waits for them, and re-layouts  1.41 us (3%)
  other arithmetic  0.71 us (1%)
    ppermute x12, starting transfers between devices, from_ahead(): return lax.ppermute(value, 'rows', pairs)  23.2 us
    ppermute x12, waiting for transfers between devices, from_ahead(): return lax.ppermute(value, 'rows', pairs)  13.4 us
    pallas_call x1, Pallas kernels, cube(): pl.pallas_call(functools.partial(cube_kernel, half), out_shape=[like(own)...  3.94 us
    ppermute x10, waiting for transfers between devices, from_sibling(): return lax.ppermute(value, 'layers', [(0, 1), (1, 0)])  3.37 us
    pallas_call x1, Pallas kernels, square(): pl.pallas_call(functools.partial(square_kernel, half), out_shape=[like(ow...  2.95 us
    pallas_call x1, Pallas kernels, with_others(): pl.pallas_call(functools.partial(others_kernel, half), out_shape=like(tab...  2.88 us
    ppermute x10, starting transfers between devices, from_sibling(): return lax.ppermute(value, 'layers', [(0, 1), (1, 0)])  1.67 us
    unnamed x2, local copies, waits for them, and re-layouts  1.41 us
  transfers between devices with their start and end apart: 22, of which 13 were waited for; matrix products, arithmetic and copies ran while one was open for 1% of the time, Pallas kernels for 8%

profile of v4, /device:TPU:0, one launch (start us, length us, event | category | flops | bytes accessed | tf_op | source)
XLA Modules:
  0.0 55.2 jit_solution(5323345363045608474)
XLA Ops:
  0.0 0.5 collective-permute-start.1
  0.5 0.7 %add_bitcast_fusion = s32[6,16]{1,0:T(8,128)S(1)} fusion(s32[16,3]{0,1:T(4,128)} %param.5, s32[16,3]{0,1:T(4,128)} %param.4), kind=kLoop, calls=%fused_computation.1 | loop fusion | flops 96 | bytes 768 | tf_op jit(solution)/shard_map/transpose | solution.py:59
  1.3 1.4 %copy-done = bf16[16,128,384]{2,1,0:T(8,128)(2,1)S(1)} copy-done((bf16[16,128,384]{2,1,0:T(8,128)(2,1)S(1)}, bf16[16,128,384]{2,1,0:T(8,128)(2,1)}, u32[]{:S(2)}) %copy-start) | copy-done | bytes 1572888
  2.8 0.7 %collective-permute-done = s32[8,128]{1,0:T(8,128)S(1)} collective-permute-done((s32[8,128]{1,0:T(8,128)S(1)}, s32[8,128]{1,0:T(8,128)S(1)}, u32[]{:S(2)}, u32[]{:S(2)}) %collective-permute-start) | collective-permute-done | bytes 4128 | tf_op jit(solution)/shard_map/ppermute | solution.py:36
  3.5 2.9 %collective-permute-start.3 = (s32[16,128]{1,0:T(8,128)S(1)}, s32[16,128]{1,0:T(8,128)S(1)}, u32[]{:S(2)}, u32[]{:S(2)}) collective-permute-start(s32[16,128]{1,0:T(8,128)S(1)} %pad_add_fusion.mine_ref), channel_id=1, source_target_pairs={{0,4},{2,6},{4,8},{6,10},{8,12},{10,14},{12,0},{14,2},{1,5},{3,7},... | collective-permute-start | bytes 24584 | tf_op jit(solution)/shard_map/ppermute | solution.py:32
  6.4 3.2 %collective-permute-start.2 = (s32[16,128]{1,0:T(8,128)S(1)}, s32[16,128]{1,0:T(8,128)S(1)}, u32[]{:S(2)}, u32[]{:S(2)}) collective-permute-start(s32[16,128]{1,0:T(8,128)S(1)} %pad_add_fusion.mine_ref), channel_id=1, source_target_pairs={{0,14},{2,0},{4,2},{6,4},{8,6},{10,8},{12,10},{14,12},{1,15},{3,1}... | collective-permute-start | bytes 24584 | tf_op jit(solution)/shard_map/ppermute | solution.py:32
  9.6 1.8 %collective-permute-start.5 = (s32[16,128]{1,0:T(8,128)S(1)}, s32[16,128]{1,0:T(8,128)S(1)}, u32[]{:S(2)}, u32[]{:S(2)}) collective-permute-start(s32[16,128]{1,0:T(8,128)S(1)} %pad_add_fusion.mine_ref), channel_id=1, source_target_pairs={{0,12},{2,14},{4,0},{6,2},{8,4},{10,6},{12,8},{14,10},{1,13},{3,15... | collective-permute-start | bytes 24584 | tf_op jit(solution)/shard_map/ppermute | solution.py:32
  11.7 1.1 %collective-permute-start.9 = (bf16[2,128,384]{2,1,0:T(8,128)(2,1)S(1)}, bf16[2,128,384]{2,1,0:T(8,128)(2,1)S(1)}, u32[]{:S(2)}, u32[]{:S(2)}) collective-permute-start(bf16[2,128,384]{2,1,0:T(8,128)(2,1)S(1)} %gather_rows.7), channel_id=1, source_target_pairs={{0,12},{2,14},{4,0},{6,2},{8,4},{10,6},{12,8},{14,10},{1,13},{3,15... | collective-permute-start | bytes 589832 | tf_op jit(solution)/shard_map/ppermute | solution.py:32
  13.0 4.3 %collective-permute-start.8 = (bf16[2,128,384]{2,1,0:T(8,128)(2,1)S(1)}, bf16[2,128,384]{2,1,0:T(8,128)(2,1)S(1)}, u32[]{:S(2)}, u32[]{:S(2)}) collective-permute-start(bf16[2,128,384]{2,1,0:T(8,128)(2,1)S(1)} %gather_rows.6), channel_id=1, source_target_pairs={{0,2},{2,4},{4,6},{6,8},{8,10},{10,12},{12,14},{14,0},{1,3},{3,5},... | collective-permute-start | bytes 589832 | tf_op jit(solution)/shard_map/ppermute | solution.py:32
  17.6 0.3 collective-permute-done.4.refs_2_.numbers_ref
  18.2 3.0 %collective-permute-start.6 = (bf16[2,128,384]{2,1,0:T(8,128)(2,1)S(1)}, bf16[2,128,384]{2,1,0:T(8,128)(2,1)S(1)}, u32[]{:S(2)}, u32[]{:S(2)}) collective-permute-start(bf16[2,128,384]{2,1,0:T(8,128)(2,1)S(1)} %gather_rows.4), channel_id=1, source_target_pairs={{0,14},{2,0},{4,2},{6,4},{8,6},{10,8},{12,10},{14,12},{1,15},{3,1}... | collective-permute-start | bytes 589832 | tf_op jit(solution)/shard_map/ppermute | solution.py:32
  21.2 0.6 %block_tables.1 = (s32[24,128]{1,0:T(8,128)S(1)}, s32[24,128]{1,0:T(8,128)S(1)}, s32[24,128]{1,0:T(8,128)S(1)}, bf16[49,128,384]{2,1,0:T(8,128)(2,1)S(1)}) custom-call(s32[16,128]{1,0:T(8,128)S(1)} %pad_add_fusion.mine_ref, bf16[16,128,384]{2,1,0:T(8,128)(2,1)S(1)} %stage_density.1.own_ref.density_ref, ...), custom_call_target="tpu_custom_call" | custom-call | bytes 6291456 | tf_op jit(solution)/shard_map/block_tables/pallas_call | solution.py:191
  21.9 4.7 %collective-permute-done.8.refs_3_ = bf16[2,128,384]{2,1,0:T(8,128)(2,1)S(1)} collective-permute-done((bf16[2,128,384]{2,1,0:T(8,128)(2,1)S(1)}, bf16[2,128,384]{2,1,0:T(8,128)(2,1)S(1)}, u32[]{:S(2)}, u32[]{:S(2)}) %collective-permute-start.8) | collective-permute-done | bytes 196640 | tf_op jit(solution)/shard_map/ppermute | solution.py:32
  26.5 0.3 collective-permute-done.7.refs_2_
  26.8 0.6 %collective-permute-done.6.refs_1_ = bf16[2,128,384]{2,1,0:T(8,128)(2,1)S(1)} collective-permute-done((bf16[2,128,384]{2,1,0:T(8,128)(2,1)S(1)}, bf16[2,128,384]{2,1,0:T(8,128)(2,1)S(1)}, u32[]{:S(2)}, u32[]{:S(2)}) %collective-permute-start.6) | collective-permute-done | bytes 196640 | tf_op jit(solution)/shard_map/ppermute | solution.py:32
  27.4 0.5 collective-permute-start.11
  27.9 0.5 collective-permute-start.13
  28.4 0.4 collective-permute-done.10.refs_5_
  28.8 0.3 collective-permute-done.11.refs_6_
  29.1 0.3 collective-permute-done.12.refs_7_
  29.4 0.3 collective-permute-done.13.refs_8_
  29.7 2.9 %square_rows.1 = (bf16[16,128,384]{2,1,0:T(8,128)(2,1)S(1)}, bf16[2,128,384]{2,1,0:T(8,128)(2,1)S(1)}, bf16[2,128,384]{2,1,0:T(8,128)(2,1)S(1)}, bf16[2,128,384]...) custom-call(s32[24,128]{1,0:T(8,128)S(1)} %get-tuple-element.30.inde, ...), custom_call_target="tpu_custom_call", output_to_operand_aliasing={{5}: (3, {})} | custom-call | flops 1207959552 | bytes 12582912 | tf_op jit(solution)/shard_map/square_rows/pallas_call | solution.py:283
  32.6 2.9 %collective-permute-start.14 = (bf16[2,128,384]{2,1,0:T(8,128)(2,1)S(1)}, bf16[2,128,384]{2,1,0:T(8,128)(2,1)S(1)}, u32[]{:S(2)}, u32[]{:S(2)}) collective-permute-start(bf16[2,128,384]{2,1,0:T(8,128)(2,1)S(1)} %get-tuple-element.38), channel_id=1, source_target_pairs={{0,14},{2,0},{4,2},{6,4},{8,6},{10,8},{12,10},{14,12},{1,15},{3,1}... | collective-permute-start | bytes 589832 | tf_op jit(solution)/shard_map/ppermute | solution.py:32
  35.5 0.9 %collective-permute-start.15 = (bf16[2,128,384]{2,1,0:T(8,128)(2,1)S(1)}, bf16[2,128,384]{2,1,0:T(8,128)(2,1)S(1)}, u32[]{:S(2)}, u32[]{:S(2)}) collective-permute-start(bf16[2,128,384]{2,1,0:T(8,128)(2,1)S(1)} %get-tuple-element.40), channel_id=1, source_target_pairs={{0,4},{2,6},{4,8},{6,10},{8,12},{10,14},{12,0},{14,2},{1,5},{3,7},... | collective-permute-start | bytes 589832 | tf_op jit(solution)/shard_map/ppermute | solution.py:32
  36.4 0.3 collective-permute-start.16
  36.7 2.7 %collective-permute-start.17 = (bf16[2,128,384]{2,1,0:T(8,128)(2,1)S(1)}, bf16[2,128,384]{2,1,0:T(8,128)(2,1)S(1)}, u32[]{:S(2)}, u32[]{:S(2)}) collective-permute-start(bf16[2,128,384]{2,1,0:T(8,128)(2,1)S(1)} %get-tuple-element.44), channel_id=1, source_target_pairs={{0,12},{2,14},{4,0},{6,2},{8,4},{10,6},{12,8},{14,10},{1,13},{3,15... | collective-permute-start | bytes 589832 | tf_op jit(solution)/shard_map/ppermute | solution.py:32
  39.4 2.9 %square_others.1.refs_0_ = bf16[49,128,384]{2,1,0:T(8,128)(2,1)S(1)} custom-call(s32[24,128]{1,0:T(8,128)S(1)} %get-tuple-element.29.index_ref, bf16[16,128,384]{2,1,0:T(8,128)(2,1)S(1)} %stage_density.1.own_ref.density_ref, bf16[16,128,384]{2,1,0:T(8,128)(2,1)S(1)} %collective-permute-done.1.other_ref, ...), custom_call_target="tpu_custom_call" | custom-call | flops 1207959552 | bytes 12582912 | tf_op jit(solution)/shard_map/square_others/pallas_call | solution.py:220
  42.3 4.8 %collective-permute-done.15.refs_2_ = bf16[2,128,384]{2,1,0:T(8,128)(2,1)S(1)} collective-permute-done((bf16[2,128,384]{2,1,0:T(8,128)(2,1)S(1)}, bf16[2,128,384]{2,1,0:T(8,128)(2,1)S(1)}, u32[]{:S(2)}, u32[]{:S(2)}) %collective-permute-start.15) | collective-permute-done | bytes 196640 | tf_op jit(solution)/shard_map/ppermute | solution.py:32
  47.1 1.1 %collective-permute-done.16.refs_3_ = bf16[2,128,384]{2,1,0:T(8,128)(2,1)S(1)} collective-permute-done((bf16[2,128,384]{2,1,0:T(8,128)(2,1)S(1)}, bf16[2,128,384]{2,1,0:T(8,128)(2,1)S(1)}, u32[]{:S(2)}, u32[]{:S(2)}) %collective-permute-start.16) | collective-permute-done | bytes 196640 | tf_op jit(solution)/shard_map/ppermute | solution.py:32
  48.2 1.6 %collective-permute-done.17.refs_4_ = bf16[2,128,384]{2,1,0:T(8,128)(2,1)S(1)} collective-permute-done((bf16[2,128,384]{2,1,0:T(8,128)(2,1)S(1)}, bf16[2,128,384]{2,1,0:T(8,128)(2,1)S(1)}, u32[]{:S(2)}, u32[]{:S(2)}) %collective-permute-start.17) | collective-permute-done | bytes 196640 | tf_op jit(solution)/shard_map/ppermute | solution.py:32
  49.9 1.4 %collective-permute-done.21.refs_8_ = bf16[2,128,384]{2,1,0:T(8,128)(2,1)S(1)} collective-permute-done((bf16[2,128,384]{2,1,0:T(8,128)(2,1)S(1)}, bf16[2,128,384]{2,1,0:T(8,128)(2,1)S(1)}, u32[]{:S(2)}, u32[]{:S(2)}) %collective-permute-start.21) | collective-permute-done | bytes 196640 | tf_op jit(solution)/shard_map/ppermute | solution.py:36
  51.3 3.9 %cube_rows.1 = (bf16[16,128,384]{2,1,0:T(8,128)(2,1)}, bf16[49,128,384]{2,1,0:T(8,128)(2,1)S(1)}) custom-call(s32[24,128]{1,0:T(8,128)S(1)} %get-tuple-element.28.index_ref, bf16[16,128,384]{2,1,0:T(8,128)(2,1)S(1)} %stage_density.1.own_ref.density_ref, bf16[16,128,384]{2,1,0:T(8,128)(2,1)S(1)} %collective-permute-done.1.other_ref, ...), custom_call_target="tpu_custom_call", output_to_operand_aliasing={{1}: (3, {})} | custom-call | flops 1207959552 | bytes 12582912 | tf_op jit(solution)/shard_map/cube_rows/pallas_call | solution.py:318
  (26 shorter events, 1.3 us)
Async XLA Ops:
  0.0 21.2 %collective-permute-start.1 = (bf16[16,128,384]{2,1,0:T(8,128)(2,1)}, bf16[16,128,384]{2,1,0:T(8,128)(2,1)S(1)}, u32[]{:S(2)}, u32[]{:S(2)}) collective-permute-start(bf16[16,128,384]{2,1,0:T(8,128)(2,1)} %density_ref.1), channel_id=1, source_target_pairs={{0,1},{1,0},{2,3},{3,2},{4,5},{5,4},{6,7},{7,6},{8,9},{9,8},{10,11... | collective-permute-start | bytes 4718600 | tf_op jit(solution)/shard_map/ppermute | solution.py:36
  1.2 2.3 %collective-permute-start = (s32[8,128]{1,0:T(8,128)S(1)}, s32[8,128]{1,0:T(8,128)S(1)}, u32[]{:S(2)}, u32[]{:S(2)}) collective-permute-start(s32[8,128]{1,0:T(8,128)S(1)} %pad.4), channel_id=1, source_target_pairs={{0,1},{1,0},{2,3},{3,2},{4,5},{5,4},{6,7},{7,6},{8,9},{9,8},{10,11... | collective-permute-start | bytes 12296 | tf_op jit(solution)/shard_map/ppermute | solution.py:36
  1.3 1.4 %copy-start = (bf16[16,128,384]{2,1,0:T(8,128)(2,1)S(1)}, bf16[16,128,384]{2,1,0:T(8,128)(2,1)}, u32[]{:S(2)}) copy-start(bf16[16,128,384]{2,1,0:T(8,128)(2,1)} %density_ref.1) | copy-start | bytes 4718596
  3.5 8.0 %collective-permute-start.3 = (s32[16,128]{1,0:T(8,128)S(1)}, s32[16,128]{1,0:T(8,128)S(1)}, u32[]{:S(2)}, u32[]{:S(2)}) collective-permute-start(s32[16,128]{1,0:T(8,128)S(1)} %pad_add_fusion.mine_ref), channel_id=1, source_target_pairs={{0,4},{2,6},{4,8},{6,10},{8,12},{10,14},{12,0},{14,2},{1,5},{3,7},... | collective-permute-start | bytes 24584 | tf_op jit(solution)/shard_map/ppermute | solution.py:32
  6.4 6.4 %collective-permute-start.2 = (s32[16,128]{1,0:T(8,128)S(1)}, s32[16,128]{1,0:T(8,128)S(1)}, u32[]{:S(2)}, u32[]{:S(2)}) collective-permute-start(s32[16,128]{1,0:T(8,128)S(1)} %pad_add_fusion.mine_ref), channel_id=1, source_target_pairs={{0,14},{2,0},{4,2},{6,4},{8,6},{10,8},{12,10},{14,12},{1,15},{3,1}... | collective-permute-start | bytes 24584 | tf_op jit(solution)/shard_map/ppermute | solution.py:32
  9.6 7.7 %collective-permute-start.5 = (s32[16,128]{1,0:T(8,128)S(1)}, s32[16,128]{1,0:T(8,128)S(1)}, u32[]{:S(2)}, u32[]{:S(2)}) collective-permute-start(s32[16,128]{1,0:T(8,128)S(1)} %pad_add_fusion.mine_ref), channel_id=1, source_target_pairs={{0,12},{2,14},{4,0},{6,2},{8,4},{10,6},{12,8},{14,10},{1,13},{3,15... | collective-permute-start | bytes 24584 | tf_op jit(solution)/shard_map/ppermute | solution.py:32
  11.5 6.5 %collective-permute-start.4 = (s32[16,128]{1,0:T(8,128)S(1)}, s32[16,128]{1,0:T(8,128)S(1)}, u32[]{:S(2)}, u32[]{:S(2)}) collective-permute-start(s32[16,128]{1,0:T(8,128)S(1)} %pad_add_fusion.mine_ref), channel_id=1, source_target_pairs={{0,2},{2,4},{4,6},{6,8},{8,10},{10,12},{12,14},{14,0},{1,3},{3,5},... | collective-permute-start | bytes 24584 | tf_op jit(solution)/shard_map/ppermute | solution.py:32
  11.7 10.2 %collective-permute-start.9 = (bf16[2,128,384]{2,1,0:T(8,128)(2,1)S(1)}, bf16[2,128,384]{2,1,0:T(8,128)(2,1)S(1)}, u32[]{:S(2)}, u32[]{:S(2)}) collective-permute-start(bf16[2,128,384]{2,1,0:T(8,128)(2,1)S(1)} %gather_rows.7), channel_id=1, source_target_pairs={{0,12},{2,14},{4,0},{6,2},{8,4},{10,6},{12,8},{14,10},{1,13},{3,15... | collective-permute-start | bytes 589832 | tf_op jit(solution)/shard_map/ppermute | solution.py:32
  13.0 13.5 %collective-permute-start.8 = (bf16[2,128,384]{2,1,0:T(8,128)(2,1)S(1)}, bf16[2,128,384]{2,1,0:T(8,128)(2,1)S(1)}, u32[]{:S(2)}, u32[]{:S(2)}) collective-permute-start(bf16[2,128,384]{2,1,0:T(8,128)(2,1)S(1)} %gather_rows.6), channel_id=1, source_target_pairs={{0,2},{2,4},{4,6},{6,8},{8,10},{10,12},{12,14},{14,0},{1,3},{3,5},... | collective-permute-start | bytes 589832 | tf_op jit(solution)/shard_map/ppermute | solution.py:32
  17.6 9.2 %collective-permute-start.7 = (bf16[2,128,384]{2,1,0:T(8,128)(2,1)S(1)}, bf16[2,128,384]{2,1,0:T(8,128)(2,1)S(1)}, u32[]{:S(2)}, u32[]{:S(2)}) collective-permute-start(bf16[2,128,384]{2,1,0:T(8,128)(2,1)S(1)} %gather_rows.5), channel_id=1, source_target_pairs={{0,4},{2,6},{4,8},{6,10},{8,12},{10,14},{12,0},{14,2},{1,5},{3,7},... | collective-permute-start | bytes 589832 | tf_op jit(solution)/shard_map/ppermute | solution.py:32
  18.2 9.2 %collective-permute-start.6 = (bf16[2,128,384]{2,1,0:T(8,128)(2,1)S(1)}, bf16[2,128,384]{2,1,0:T(8,128)(2,1)S(1)}, u32[]{:S(2)}, u32[]{:S(2)}) collective-permute-start(bf16[2,128,384]{2,1,0:T(8,128)(2,1)S(1)} %gather_rows.4), channel_id=1, source_target_pairs={{0,14},{2,0},{4,2},{6,4},{8,6},{10,8},{12,10},{14,12},{1,15},{3,1}... | collective-permute-start | bytes 589832 | tf_op jit(solution)/shard_map/ppermute | solution.py:32
  27.4 1.4 %collective-permute-start.10 = (bf16[2,128,384]{2,1,0:T(8,128)(2,1)S(1)}, bf16[2,128,384]{2,1,0:T(8,128)(2,1)S(1)}, u32[]{:S(2)}, u32[]{:S(2)}) collective-permute-start(bf16[2,128,384]{2,1,0:T(8,128)(2,1)S(1)} %collective-permute-done.6.refs_1_), channel_id=1, source_target_pairs={{0,1},{1,0},{2,3},{3,2},{4,5},{5,4},{6,7},{7,6},{8,9},{9,8},{10,11... | collective-permute-start | bytes 589832 | tf_op jit(solution)/shard_map/ppermute | solution.py:36
  27.4 1.7 %collective-permute-start.11 = (bf16[2,128,384]{2,1,0:T(8,128)(2,1)S(1)}, bf16[2,128,384]{2,1,0:T(8,128)(2,1)S(1)}, u32[]{:S(2)}, u32[]{:S(2)}) collective-permute-start(bf16[2,128,384]{2,1,0:T(8,128)(2,1)S(1)} %collective-permute-done.7.refs_2_), channel_id=1, source_target_pairs={{0,1},{1,0},{2,3},{3,2},{4,5},{5,4},{6,7},{7,6},{8,9},{9,8},{10,11... | collective-permute-start | bytes 589832 | tf_op jit(solution)/shard_map/ppermute | solution.py:36
  27.9 1.5 %collective-permute-start.12 = (bf16[2,128,384]{2,1,0:T(8,128)(2,1)S(1)}, bf16[2,128,384]{2,1,0:T(8,128)(2,1)S(1)}, u32[]{:S(2)}, u32[]{:S(2)}) collective-permute-start(bf16[2,128,384]{2,1,0:T(8,128)(2,1)S(1)} %collective-permute-done.8.refs_3_), channel_id=1, source_target_pairs={{0,1},{1,0},{2,3},{3,2},{4,5},{5,4},{6,7},{7,6},{8,9},{9,8},{10,11... | collective-permute-start | bytes 589832 | tf_op jit(solution)/shard_map/ppermute | solution.py:36
  27.9 1.8 %collective-permute-start.13 = (bf16[2,128,384]{2,1,0:T(8,128)(2,1)S(1)}, bf16[2,128,384]{2,1,0:T(8,128)(2,1)S(1)}, u32[]{:S(2)}, u32[]{:S(2)}) collective-permute-start(bf16[2,128,384]{2,1,0:T(8,128)(2,1)S(1)} %collective-permute-done.9.refs_4_), channel_id=1, source_target_pairs={{0,1},{1,0},{2,3},{3,2},{4,5},{5,4},{6,7},{7,6},{8,9},{9,8},{10,11... | collective-permute-start | bytes 589832 | tf_op jit(solution)/shard_map/ppermute | solution.py:36
  32.6 9.6 %collective-permute-start.14 = (bf16[2,128,384]{2,1,0:T(8,128)(2,1)S(1)}, bf16[2,128,384]{2,1,0:T(8,128)(2,1)S(1)}, u32[]{:S(2)}, u32[]{:S(2)}) collective-permute-start(bf16[2,128,384]{2,1,0:T(8,128)(2,1)S(1)} %get-tuple-element.38), channel_id=1, source_target_pairs={{0,14},{2,0},{4,2},{6,4},{8,6},{10,8},{12,10},{14,12},{1,15},{3,1}... | collective-permute-start | bytes 589832 | tf_op jit(solution)/shard_map/ppermute | solution.py:32
  35.5 11.6 %collective-permute-start.15 = (bf16[2,128,384]{2,1,0:T(8,128)(2,1)S(1)}, bf16[2,128,384]{2,1,0:T(8,128)(2,1)S(1)}, u32[]{:S(2)}, u32[]{:S(2)}) collective-permute-start(bf16[2,128,384]{2,1,0:T(8,128)(2,1)S(1)} %get-tuple-element.40), channel_id=1, source_target_pairs={{0,4},{2,6},{4,8},{6,10},{8,12},{10,14},{12,0},{14,2},{1,5},{3,7},... | collective-permute-start | bytes 589832 | tf_op jit(solution)/shard_map/ppermute | solution.py:32
  36.4 11.8 %collective-permute-start.16 = (bf16[2,128,384]{2,1,0:T(8,128)(2,1)S(1)}, bf16[2,128,384]{2,1,0:T(8,128)(2,1)S(1)}, u32[]{:S(2)}, u32[]{:S(2)}) collective-permute-start(bf16[2,128,384]{2,1,0:T(8,128)(2,1)S(1)} %get-tuple-element.42), channel_id=1, source_target_pairs={{0,2},{2,4},{4,6},{6,8},{8,10},{10,12},{12,14},{14,0},{1,3},{3,5},... | collective-permute-start | bytes 589832 | tf_op jit(solution)/shard_map/ppermute | solution.py:32
  36.7 13.2 %collective-permute-start.17 = (bf16[2,128,384]{2,1,0:T(8,128)(2,1)S(1)}, bf16[2,128,384]{2,1,0:T(8,128)(2,1)S(1)}, u32[]{:S(2)}, u32[]{:S(2)}) collective-permute-start(bf16[2,128,384]{2,1,0:T(8,128)(2,1)S(1)} %get-tuple-element.44), channel_id=1, source_target_pairs={{0,12},{2,14},{4,0},{6,2},{8,4},{10,6},{12,8},{14,10},{1,13},{3,15... | collective-permute-start | bytes 589832 | tf_op jit(solution)/shard_map/ppermute | solution.py:32
  42.3 7.6 %collective-permute-start.18 = (bf16[2,128,384]{2,1,0:T(8,128)(2,1)S(1)}, bf16[2,128,384]{2,1,0:T(8,128)(2,1)S(1)}, u32[]{:S(2)}, u32[]{:S(2)}) collective-permute-start(bf16[2,128,384]{2,1,0:T(8,128)(2,1)S(1)} %collective-permute-done.14.refs_1_), channel_id=1, source_target_pairs={{0,1},{1,0},{2,3},{3,2},{4,5},{5,4},{6,7},{7,6},{8,9},{9,8},{10,11... | collective-permute-start | bytes 589832 | tf_op jit(solution)/shard_map/ppermute | solution.py:36
  47.1 2.7 %collective-permute-start.19 = (bf16[2,128,384]{2,1,0:T(8,128)(2,1)S(1)}, bf16[2,128,384]{2,1,0:T(8,128)(2,1)S(1)}, u32[]{:S(2)}, u32[]{:S(2)}) collective-permute-start(bf16[2,128,384]{2,1,0:T(8,128)(2,1)S(1)} %collective-permute-done.15.refs_2_), channel_id=1, source_target_pairs={{0,1},{1,0},{2,3},{3,2},{4,5},{5,4},{6,7},{7,6},{8,9},{9,8},{10,11... | collective-permute-start | bytes 589832 | tf_op jit(solution)/shard_map/ppermute | solution.py:36
  48.2 1.7 %collective-permute-start.20 = (bf16[2,128,384]{2,1,0:T(8,128)(2,1)S(1)}, bf16[2,128,384]{2,1,0:T(8,128)(2,1)S(1)}, u32[]{:S(2)}, u32[]{:S(2)}) collective-permute-start(bf16[2,128,384]{2,1,0:T(8,128)(2,1)S(1)} %collective-permute-done.16.refs_3_), channel_id=1, source_target_pairs={{0,1},{1,0},{2,3},{3,2},{4,5},{5,4},{6,7},{7,6},{8,9},{9,8},{10,11... | collective-permute-start | bytes 589832 | tf_op jit(solution)/shard_map/ppermute | solution.py:36
  49.9 1.4 %collective-permute-start.21 = (bf16[2,128,384]{2,1,0:T(8,128)(2,1)S(1)}, bf16[2,128,384]{2,1,0:T(8,128)(2,1)S(1)}, u32[]{:S(2)}, u32[]{:S(2)}) collective-permute-start(bf16[2,128,384]{2,1,0:T(8,128)(2,1)S(1)} %collective-permute-done.17.refs_4_), channel_id=1, source_target_pairs={{0,1},{1,0},{2,3},{3,2},{4,5},{5,4},{6,7},{7,6},{8,9},{9,8},{10,11... | collective-permute-start | bytes 589832 | tf_op jit(solution)/shard_map/ppermute | solution.py:36

commit v5 on v4

--- a/solution.py
+++ b/solution.py
@@ -8,11 +8,10 @@
 from jax.sharding import PartitionSpec as P
 
 CAP = 2
-OFFSETS = (1, -2, -1, 2)
-FAR = len(OFFSETS) * CAP
-BEHIND = tuple(OFFSETS.index(-step) for step in OFFSETS)
+EXCHANGES = ((1, 1), (2, 1), (1, 0), (2, 0))
+FAR = len(EXCHANGES) * CAP
 SUBLANES, LANES = 8, 128
-VMEM_LIMIT = 40 * 1024 * 1024
+VMEM_LIMIT = 12 * 1024 * 1024
 PARAMS = pltpu.CompilerParams(vmem_limit_bytes=VMEM_LIMIT)
 VMEM = pl.BlockSpec(memory_space=pltpu.VMEM)
 SMEM = pl.BlockSpec(memory_space=pltpu.SMEM)
@@ -26,9 +25,14 @@
     return jax.ShapeDtypeStruct(value.shape, value.dtype)
 
 
-def from_ahead(value, steps):
+def partner(device, exchange, count):
+    reach, phase = exchange
+    return (device + reach * (1 - 2 * ((device // reach + phase) % 2)) + count) % count
+
+
+def swapped(value, exchange):
     count = lax.axis_size("rows")
-    pairs = [(source, (source - steps) % count) for source in range(count)]
+    pairs = [(source, partner(source, exchange, count)) for source in range(count)]
     return lax.ppermute(value, "rows", pairs)
 
 
@@ -104,7 +108,7 @@
 
 
 def tables_kernel(half, peers, mine_ref, own_ref, other_ref, *refs):
-    near, refs = refs[: len(OFFSETS)], refs[len(OFFSETS) :]
+    near, refs = refs[: len(EXCHANGES)], refs[len(EXCHANGES) :]
     square_ref, others_ref, cube_ref, table_ref, sems = refs
     own, edge, wide = own_ref.shape
     copies = stack(table_ref, own_ref, other_ref, sems)
@@ -131,8 +135,8 @@
     named = (columns[0:half], columns[half : 2 * half])
     column_table, kept_table = columns, kept
     slots = columns - me * own
-    for position, step in enumerate(OFFSETS):
-        owner = lax.rem(me + step + peers, peers)
+    for position, exchange in enumerate(EXCHANGES):
+        owner = partner(me, exchange, peers)
         low, high = bounds(named, owner)
         local = columns - owner * own
         first = own + position * CAP
@@ -147,8 +151,7 @@
         )
         kept_table = jnp.where(here, jnp.take_along_axis(far_kept, source, axis=1), kept_table)
     asked = jnp.zeros((1, LANES), jnp.int32)
-    for position, behind in enumerate(BEHIND):
-        numbers = near[behind]
+    for position, numbers in enumerate(near):
         pair = bounds([numbers[k : k + half] for k in (0, SUBLANES)], me)
         for k in range(CAP):
             asked = jnp.where(lane[0:1] == position * CAP + k, pair[k], asked)
@@ -157,22 +160,30 @@
     base = jnp.where(slots < own, slots, slots + own)
     shift = jnp.where(slots < own, own, FAR)
     empty = (table_ref.shape[0] - 1) * stride
-    for table, outs in (
-        (column_table, ((square_ref, 0), (others_ref, half))),
-        (kept_table, ((cube_ref, 0),)),
-    ):
-        met = [
+
+    def met_in(table):
+        return [
             jnp.take_along_axis(jnp.broadcast_to(table[b : b + 1], shape), slots, axis=1)
             for b in range(2 * half)
         ]
-        for out, first in outs:
-            for s in range(half):
-                index = jnp.full(shape, empty, jnp.int32)
-                for b in range(2 * half):
-                    entry = base + shift if b >= half else base
-                    place = entry * stride + (b % half) * edge
-                    index = jnp.where(met[b] == kept[first + s : first + s + 1], place, index)
-                out[s * SUBLANES : (s + 1) * SUBLANES] = index
+
+    def choose(met, target, place, otherwise):
+        index = jnp.full(shape, otherwise, jnp.int32)
+        for b in range(2 * half):
+            index = jnp.where(met[b] == kept[target : target + 1], place(b), index)
+        return index
+
+    def place(b):
+        return (base + shift if b >= half else base) * stride + (b % half) * edge
+
+    met = met_in(column_table)
+    for out, first in ((square_ref, 0), (others_ref, half)):
+        for s in range(half):
+            out[s * SUBLANES : (s + 1) * SUBLANES] = choose(met, first + s, place, empty)
+
+    met = met_in(kept_table)
+    for s in range(half):
+        cube_ref[s * SUBLANES : (s + 1) * SUBLANES] = choose(met, s, place, empty)
     square_ref[SUBLANES - 1 : SUBLANES] = asked
     for copy in copies:
         copy.wait()
@@ -200,56 +211,23 @@
     )(mine, own, other, *near)
 
 
-def others_kernel(half, index_ref, own_ref, other_ref, table_ref, squares_ref, out, sem):
-    own, edge, wide = own_ref.shape
-    copy = pltpu.make_async_copy(squares_ref, out.at[pl.ds(0, own)], sem)
-    copy.start()
-    out[out.shape[0] - 1] = jnp.zeros(out.shape[1:], out.dtype)
-
-    def body(i, carry):
-        total = row_product(table_ref, index_ref, i, own_ref, other_ref, half, edge)
-        out[own + i] = total.astype(out.dtype)
-        return carry
-
-    lax.fori_loop(0, own, body, 0, unroll=True)
-    copy.wait()
-
-
-def with_others(index, own, other, table, squares, half):
-    size, edge, wide = own.shape
-    return pl.pallas_call(
-        functools.partial(others_kernel, half),
-        out_shape=like(table),
-        in_specs=[SMEM] + [VMEM] * 4,
-        out_specs=VMEM,
-        scratch_shapes=[pltpu.SemaphoreType.DMA],
-        compiler_params=PARAMS,
-        cost_estimate=cost(size * 4 * edge * wide * wide, 8 * own.size * 2),
-        name="square_others",
-    )(index, own, other, table, squares)
-
-
-def add_far(table, pieces, own):
-    for position, piece in enumerate(pieces):
-        for k in range(CAP):
-            table[2 * own + position * CAP + k] = piece[k]
-
-
-def row_product(table, index_ref, row, own_ref, other_ref, half, edge):
-    stride = table_stride(half, edge)
-
-    def left(k):
-        ref = own_ref if k < half else other_ref
-        return ref[row, :, (k % half) * edge : (k % half + 1) * edge]
-
-    def right(k, s):
-        place = index_ref[s * SUBLANES + k, row]
-        begin = pl.multiple_of(lax.bitwise_and(place, stride - 1), edge)
-        return table[lax.div(place, stride), :, pl.ds(begin, edge)]
-
+def add_far(table, begin, own_half, other_half):
+    count = len(own_half) * CAP
+    for first, pieces in ((begin, own_half), (begin + count, other_half)):
+        for position, piece in enumerate(pieces):
+            for k in range(CAP):
+                table[first + position * CAP + k] = piece[k]
+
+
+def block_at(table, place, stride, edge):
+    begin = pl.multiple_of(lax.bitwise_and(place, stride - 1), edge)
+    return table[lax.div(place, stride), :, pl.ds(begin, edge)]
+
+
+def product(left, right, count, half):
     total = None
-    for a in range(0, 2 * half, 2):
-        pair = range(a, min(a + 2, 2 * half))
+    for a in range(0, count, 2):
+        pair = range(a, min(a + 2, count))
         lhs = jnp.concatenate([left(k) for k in pair], axis=1)
         rhs = jnp.concatenate(
             [jnp.concatenate([right(k, s) for s in range(half)], axis=1) for k in pair], axis=0
@@ -259,45 +237,79 @@
     return total
 
 
-def square_kernel(half, index_ref, own_ref, other_ref, *refs):
-    pieces = refs[1 : 1 + 2 * len(OFFSETS)]
-    out, *wanted, table = refs[1 + len(pieces) :]
+def row_product(table, index_ref, row, own_ref, other_ref, half, edge):
+    stride = table_stride(half, edge)
+
+    def left(k):
+        ref = own_ref if k < half else other_ref
+        return ref[row, :, (k % half) * edge : (k % half + 1) * edge]
+
+    def right(k, s):
+        return block_at(table, index_ref[s * SUBLANES + k, row], stride, edge)
+
+    return product(left, right, 2 * half, half)
+
+
+def wanted_kernel(half, index_ref, own_ref, other_ref, *refs):
+    pieces = refs[1 : 1 + 2 * len(EXCHANGES)]
+    *wanted, table = refs[1 + len(pieces) :]
     own, edge, wide = own_ref.shape
-    add_far(table, pieces, own)
-
-    def body(i, carry):
-        total = row_product(table, index_ref, i, own_ref, other_ref, half, edge)
-        out[i] = total.astype(out.dtype)
-        return carry
-
-    lax.fori_loop(0, own, body, 0, unroll=True)
+    add_far(table, 2 * own, pieces[: len(EXCHANGES)], pieces[len(EXCHANGES) :])
     for position, piece in enumerate(wanted):
         for k in range(CAP):
-            piece[k] = out[index_ref[SUBLANES - 1, position * CAP + k]]
-
-
-def square(index, own, other, table, pieces, half):
+            row = index_ref[SUBLANES - 1, position * CAP + k]
+            total = row_product(table, index_ref, row, own_ref, other_ref, half, edge)
+            piece[k] = total.astype(piece.dtype)
+
+
+def square_wanted(index, own, other, table, pieces, half):
     size, edge, wide = own.shape
     piece = jax.ShapeDtypeStruct((CAP, edge, wide), own.dtype)
-    count = len(OFFSETS)
-    out = pl.pallas_call(
+    count = len(EXCHANGES)
+    *wanted, table = pl.pallas_call(
+        functools.partial(wanted_kernel, half),
+        out_shape=[*([piece] * count), like(table)],
+        in_specs=[SMEM] + [VMEM] * (3 + len(pieces)),
+        out_specs=[VMEM] * (1 + count),
+        input_output_aliases={3: count},
+        compiler_params=PARAMS,
+        cost_estimate=cost(FAR * 4 * edge * wide * wide, 8 * own.size * 2),
+        name="square_wanted",
+    )(index, own, other, table, *pieces)
+    return wanted, table
+
+
+def square_kernel(half, index_ref, others_ref, own_ref, other_ref, table_ref, out):
+    own, edge, wide = own_ref.shape
+    out[out.shape[0] - 1] = jnp.zeros(out.shape[1:], out.dtype)
+
+    def body(i, carry):
+        for first, index in ((0, index_ref), (own, others_ref)):
+            total = row_product(table_ref, index, i, own_ref, other_ref, half, edge)
+            out[first + i] = total.astype(out.dtype)
+        return carry
+
+    lax.fori_loop(0, own, body, 0, unroll=4)
+
+
+def square(index, others, own, other, table, half):
+    size, edge, wide = own.shape
+    return pl.pallas_call(
         functools.partial(square_kernel, half),
-        out_shape=[like(own), *([piece] * count), like(table)],
-        in_specs=[SMEM] + [VMEM] * (3 + len(pieces)),
-        out_specs=[VMEM] * (2 + count),
-        input_output_aliases={3: 1 + count},
-        compiler_params=PARAMS,
-        cost_estimate=cost(size * 4 * edge * wide * wide, 8 * own.size * 2),
+        out_shape=like(table),
+        in_specs=[SMEM] * 2 + [VMEM] * 3,
+        out_specs=VMEM,
+        compiler_params=PARAMS,
+        cost_estimate=cost(size * 8 * edge * wide * wide, 8 * own.size * 2),
         name="square_rows",
-    )(index, own, other, table, *pieces)
-    return out[0], out[1 : 1 + count], out[1 + count]
+    )(index, others, own, other, table)
 
 
 def cube_kernel(half, index_ref, own_ref, other_ref, *refs):
-    pieces = refs[1 : 1 + 2 * len(OFFSETS)]
+    pieces = refs[1 : 1 + 2 * len(EXCHANGES)]
     result, table, out, sems = refs[1 + len(pieces) :]
     own, edge, wide = own_ref.shape
-    add_far(table, pieces, own)
+    add_far(table, 2 * own, pieces[: len(EXCHANGES)], pieces[len(EXCHANGES) :])
 
     def written(i):
         return pltpu.make_async_copy(out.at[i], result.at[i], sems.at[i])
@@ -334,20 +346,20 @@
     numbers = spread(columns, kept)
     mine = jnp.concatenate([numbers, from_sibling(numbers)], axis=0)
     mine, own = lax.optimization_barrier((mine, stage(density)))
-    near = [from_ahead(mine, step) for step in OFFSETS]
-    pieces = [gather(own, near[behind], half) for behind in BEHIND]
-    got = [from_ahead(piece, step) for step, piece in zip(OFFSETS, pieces)]
+    near = [swapped(mine, exchange) for exchange in EXCHANGES]
+    pieces = [gather(own, numbers, half) for numbers in near]
+    got = [swapped(piece, exchange) for exchange, piece in zip(EXCHANGES, pieces)]
     *indices, table = tables(mine, near, own, other, half)
     got = [lax.optimization_barrier((piece, table))[0] for piece in got]
     got += [from_sibling(piece) for piece in got]
     square_index, others_index, cube_index = indices
-    squares, wanted, table = square(square_index, own, other, table, got, half)
-
-    got = [from_ahead(piece, step) for step, piece in zip(OFFSETS, wanted)]
-    table = with_others(others_index, own, other, table, squares, half)
-    got = [lax.optimization_barrier((piece, table))[0] for piece in got]
+    wanted, table = square_wanted(square_index, own, other, table, got, half)
+
+    got = [swapped(piece, exchange) for exchange, piece in zip(EXCHANGES, wanted)]
+    squares = square(square_index, others_index, own, other, table, half)
+    got = [lax.optimization_barrier((piece, squares))[0] for piece in got]
     got += [from_sibling(piece) for piece in got]
-    return cube(cube_index, own, other, table, got, half)
+    return cube(cube_index, own, other, squares, got, half)
 
 
 def solution(mesh):

time: 55.4 us -> 54.2 us (0.978); the launches traced: 55.2 us -> 53.2 us
  starting transfers between devices: 24.8 us -> 21 us
  Pallas kernels: 11.4 us -> 12.7 us
  waiting for transfers between devices: 16.7 us -> 17.3 us
    ppermute x12, starting transfers between devices: 23.2 us -> 19.3 us  [swapped(): return lax.ppermute(value, 'rows', pairs)]
    pallas_call x2, Pallas kernels: 5.83 us -> 7.17 us  [the longest x1 5.18 us: square(): pl.pallas_call(functools.partial(square_kernel, half), out_shape=like(tab...]
  transfers between devices with their start and end apart: 22 -> 22, of which waited for: 13 -> 16; matrix products, arithmetic and copies ran while one was open for 1% -> 1% of each run, Pallas kernels for 8% -> 13%
where the time goes in v5:
time: 54.2 us; the launch traced here: 53.2 us
  starting transfers between devices  21 us (39%)
  waiting for transfers between devices  17.3 us (32%)
  Pallas kernels  12.7 us (23%)
  local copies, waits for them, and re-layouts  1.41 us (3%)
  other arithmetic  0.71 us (1%)
    ppermute x12, starting transfers between devices, swapped(): return lax.ppermute(value, 'rows', pairs)  19.3 us
    ppermute x12, waiting for transfers between devices, swapped(): return lax.ppermute(value, 'rows', pairs)  13.9 us
    pallas_call x1, Pallas kernels, square(): pl.pallas_call(functools.partial(square_kernel, half), out_shape=like(tab...  5.18 us
    pallas_call x1, Pallas kernels, cube(): pl.pallas_call(functools.partial(cube_kernel, half), out_shape=[like(own)...  3.93 us
    ppermute x10, waiting for transfers between devices, from_sibling(): return lax.ppermute(value, 'layers', [(0, 1), (1, 0)])  3.37 us
    pallas_call x1, Pallas kernels, square_wanted(): pl.pallas_call(functools.partial(wanted_kernel, half), out_shape=[*[piece...  1.99 us
    ppermute x10, starting transfers between devices, from_sibling(): return lax.ppermute(value, 'layers', [(0, 1), (1, 0)])  1.62 us
    unnamed x2, local copies, waits for them, and re-layouts  1.41 us
  transfers between devices with their start and end apart: 22, of which 16 were waited for; matrix products, arithmetic and copies ran while one was open for 1% of the time, Pallas kernels for 13%

profile of v5, /device:TPU:0, one launch (start us, length us, event | category | flops | bytes accessed | tf_op | source)
XLA Modules:
  0.0 53.2 jit_solution(7456425548883798379)
XLA Ops:
  0.0 0.5 collective-permute-start.1
  0.5 0.7 %add_bitcast_fusion = s32[6,16]{1,0:T(8,128)S(1)} fusion(s32[16,3]{0,1:T(4,128)} %param.5, s32[16,3]{0,1:T(4,128)} %param.4), kind=kLoop, calls=%fused_computation.1 | loop fusion | flops 96 | bytes 768 | tf_op jit(solution)/shard_map/transpose | solution.py:63
  1.3 1.4 %copy-done = bf16[16,128,384]{2,1,0:T(8,128)(2,1)S(1)} copy-done((bf16[16,128,384]{2,1,0:T(8,128)(2,1)S(1)}, bf16[16,128,384]{2,1,0:T(8,128)(2,1)}, u32[]{:S(2)}) %copy-start) | copy-done | bytes 1572888
  2.8 0.7 %collective-permute-done = s32[8,128]{1,0:T(8,128)S(1)} collective-permute-done((s32[8,128]{1,0:T(8,128)S(1)}, s32[8,128]{1,0:T(8,128)S(1)}, u32[]{:S(2)}, u32[]{:S(2)}) %collective-permute-start) | collective-permute-done | bytes 4128 | tf_op jit(solution)/shard_map/ppermute | solution.py:40
  3.5 2.9 %collective-permute-start.5 = (s32[16,128]{1,0:T(8,128)S(1)}, s32[16,128]{1,0:T(8,128)S(1)}, u32[]{:S(2)}, u32[]{:S(2)}) collective-permute-start(s32[16,128]{1,0:T(8,128)S(1)} %pad_add_fusion.mine_ref), channel_id=1, source_target_pairs={{0,4},{2,6},{4,0},{6,2},{8,12},{10,14},{12,8},{14,10},{1,5},{3,7},... | collective-permute-start | bytes 24584 | tf_op jit(solution)/shard_map/ppermute | solution.py:36
  6.4 1.5 %collective-permute-start.4 = (s32[16,128]{1,0:T(8,128)S(1)}, s32[16,128]{1,0:T(8,128)S(1)}, u32[]{:S(2)}, u32[]{:S(2)}) collective-permute-start(s32[16,128]{1,0:T(8,128)S(1)} %pad_add_fusion.mine_ref), channel_id=1, source_target_pairs={{0,2},{2,0},{4,6},{6,4},{8,10},{10,8},{12,14},{14,12},{1,3},{3,1},... | collective-permute-start | bytes 24584 | tf_op jit(solution)/shard_map/ppermute | solution.py:36
  8.0 2.5 %collective-permute-start.3 = (s32[16,128]{1,0:T(8,128)S(1)}, s32[16,128]{1,0:T(8,128)S(1)}, u32[]{:S(2)}, u32[]{:S(2)}) collective-permute-start(s32[16,128]{1,0:T(8,128)S(1)} %pad_add_fusion.mine_ref), channel_id=1, source_target_pairs={{0,12},{2,14},{4,8},{6,10},{8,4},{10,6},{12,0},{14,2},{1,13},{3,15... | collective-permute-start | bytes 24584 | tf_op jit(solution)/shard_map/ppermute | solution.py:36
  10.4 1.3 %collective-permute-start.2 = (s32[16,128]{1,0:T(8,128)S(1)}, s32[16,128]{1,0:T(8,128)S(1)}, u32[]{:S(2)}, u32[]{:S(2)}) collective-permute-start(s32[16,128]{1,0:T(8,128)S(1)} %pad_add_fusion.mine_ref), channel_id=1, source_target_pairs={{0,14},{2,4},{4,2},{6,8},{8,6},{10,12},{12,10},{14,0},{1,15},{3,5}... | collective-permute-start | bytes 24584 | tf_op jit(solution)/shard_map/ppermute | solution.py:36
  12.0 0.7 %collective-permute-start.9 = (bf16[2,128,384]{2,1,0:T(8,128)(2,1)S(1)}, bf16[2,128,384]{2,1,0:T(8,128)(2,1)S(1)}, u32[]{:S(2)}, u32[]{:S(2)}) collective-permute-start(bf16[2,128,384]{2,1,0:T(8,128)(2,1)S(1)} %gather_rows.7), channel_id=1, source_target_pairs={{0,4},{2,6},{4,0},{6,2},{8,12},{10,14},{12,8},{14,10},{1,5},{3,7},... | collective-permute-start | bytes 589832 | tf_op jit(solution)/shard_map/ppermute | solution.py:36
  13.6 3.0 %collective-permute-start.7 = (bf16[2,128,384]{2,1,0:T(8,128)(2,1)S(1)}, bf16[2,128,384]{2,1,0:T(8,128)(2,1)S(1)}, u32[]{:S(2)}, u32[]{:S(2)}) collective-permute-start(bf16[2,128,384]{2,1,0:T(8,128)(2,1)S(1)} %gather_rows.5), channel_id=1, source_target_pairs={{0,12},{2,14},{4,8},{6,10},{8,4},{10,6},{12,0},{14,2},{1,13},{3,15... | collective-permute-start | bytes 589832 | tf_op jit(solution)/shard_map/ppermute | solution.py:36
  16.7 0.3 collective-permute-done.2.refs_0_.numbers_ref
  17.2 1.7 %collective-permute-start.6 = (bf16[2,128,384]{2,1,0:T(8,128)(2,1)S(1)}, bf16[2,128,384]{2,1,0:T(8,128)(2,1)S(1)}, u32[]{:S(2)}, u32[]{:S(2)}) collective-permute-start(bf16[2,128,384]{2,1,0:T(8,128)(2,1)S(1)} %gather_rows.4), channel_id=1, source_target_pairs={{0,14},{2,4},{4,2},{6,8},{8,6},{10,12},{12,10},{14,0},{1,15},{3,5}... | collective-permute-start | bytes 589832 | tf_op jit(solution)/shard_map/ppermute | solution.py:36
  18.9 0.6 %block_tables.1 = (s32[24,128]{1,0:T(8,128)S(1)}, s32[24,128]{1,0:T(8,128)S(1)}, s32[24,128]{1,0:T(8,128)S(1)}, bf16[49,128,384]{2,1,0:T(8,128)(2,1)S(1)}) custom-call(s32[16,128]{1,0:T(8,128)S(1)} %pad_add_fusion.mine_ref, bf16[16,128,384]{2,1,0:T(8,128)(2,1)S(1)} %stage_density.1.own_ref.density_ref, ...), custom_call_target="tpu_custom_call" | custom-call | bytes 6291456 | tf_op jit(solution)/shard_map/block_tables/pallas_call | solution.py:202
  19.5 2.4 %collective-permute-done.9.refs_4_ = bf16[2,128,384]{2,1,0:T(8,128)(2,1)S(1)} collective-permute-done((bf16[2,128,384]{2,1,0:T(8,128)(2,1)S(1)}, bf16[2,128,384]{2,1,0:T(8,128)(2,1)S(1)}, u32[]{:S(2)}, u32[]{:S(2)}) %collective-permute-start.9) | collective-permute-done | bytes 196640 | tf_op jit(solution)/shard_map/ppermute | solution.py:36
  21.9 1.9 %collective-permute-done.7.refs_2_ = bf16[2,128,384]{2,1,0:T(8,128)(2,1)S(1)} collective-permute-done((bf16[2,128,384]{2,1,0:T(8,128)(2,1)S(1)}, bf16[2,128,384]{2,1,0:T(8,128)(2,1)S(1)}, u32[]{:S(2)}, u32[]{:S(2)}) %collective-permute-start.7) | collective-permute-done | bytes 196640 | tf_op jit(solution)/shard_map/ppermute | solution.py:36
  23.8 4.4 %collective-permute-done.6.refs_1_ = bf16[2,128,384]{2,1,0:T(8,128)(2,1)S(1)} collective-permute-done((bf16[2,128,384]{2,1,0:T(8,128)(2,1)S(1)}, bf16[2,128,384]{2,1,0:T(8,128)(2,1)S(1)}, u32[]{:S(2)}, u32[]{:S(2)}) %collective-permute-start.6) | collective-permute-done | bytes 196640 | tf_op jit(solution)/shard_map/ppermute | solution.py:36
  28.2 0.5 collective-permute-start.11
  28.7 0.5 collective-permute-start.13
  29.2 0.4 collective-permute-done.10.refs_5_
  29.6 0.3 collective-permute-done.11.refs_6_
  29.9 0.3 collective-permute-done.12.refs_7_
  30.2 0.3 collective-permute-done.13.refs_8_
  30.5 2.0 %square_wanted.1 = (bf16[2,128,384]{2,1,0:T(8,128)(2,1)S(1)}, bf16[2,128,384]{2,1,0:T(8,128)(2,1)S(1)}, bf16[2,128,384]{2,1,0:T(8,128)(2,1)S(1)}, bf16[2,128,384...) custom-call(s32[24,128]{1,0:T(8,128)S(1)} %get-tuple-element.28.index_ref, ...), custom_call_target="tpu_custom_call", output_to_operand_aliasing={{4}: (3, {})} | custom-call | flops 603979776 | bytes 12582912 | tf_op jit(solution)/shard_map/square_wanted/pallas_call | solution.py:269
  32.4 1.8 %collective-permute-start.14 = (bf16[2,128,384]{2,1,0:T(8,128)(2,1)S(1)}, bf16[2,128,384]{2,1,0:T(8,128)(2,1)S(1)}, u32[]{:S(2)}, u32[]{:S(2)}) collective-permute-start(bf16[2,128,384]{2,1,0:T(8,128)(2,1)S(1)} %get-tuple-element.36), channel_id=1, source_target_pairs={{0,14},{2,4},{4,2},{6,8},{8,6},{10,12},{12,10},{14,0},{1,15},{3,5}... | collective-permute-start | bytes 589832 | tf_op jit(solution)/shard_map/ppermute | solution.py:36
  34.2 0.5 collective-permute-start.15
  34.7 3.1 %collective-permute-start.16 = (bf16[2,128,384]{2,1,0:T(8,128)(2,1)S(1)}, bf16[2,128,384]{2,1,0:T(8,128)(2,1)S(1)}, u32[]{:S(2)}, u32[]{:S(2)}) collective-permute-start(bf16[2,128,384]{2,1,0:T(8,128)(2,1)S(1)} %get-tuple-element.40), channel_id=1, source_target_pairs={{0,2},{2,0},{4,6},{6,4},{8,10},{10,8},{12,14},{14,12},{1,3},{3,1},... | collective-permute-start | bytes 589832 | tf_op jit(solution)/shard_map/ppermute | solution.py:36
  37.8 5.2 %square_rows.1.refs_0_ = bf16[49,128,384]{2,1,0:T(8,128)(2,1)S(1)} custom-call(s32[24,128]{1,0:T(8,128)S(1)} %get-tuple-element.28.index_ref, s32[24,128]{1,0:T(8,128)S(1)} %get-tuple-element.29.others_ref, bf16[16,128,384]{2,1,0:T(8,128)(2,1)S(1)} %stage_density.1.own_ref.density_ref, bf16[16,128,384]{2,1,0:T(8,128)(2,1)S(1)} %collective-permute-done.1.other_ref, ...), custom_call_target="tpu_custom_call" | custom-call | flops 2415919104 | bytes 12582912 | tf_op jit(solution)/shard_map/square_rows/pallas_call | solution.py:297
  43.1 1.5 %collective-permute-done.15.refs_2_ = bf16[2,128,384]{2,1,0:T(8,128)(2,1)S(1)} collective-permute-done((bf16[2,128,384]{2,1,0:T(8,128)(2,1)S(1)}, bf16[2,128,384]{2,1,0:T(8,128)(2,1)S(1)}, u32[]{:S(2)}, u32[]{:S(2)}) %collective-permute-start.15) | collective-permute-done | bytes 196640 | tf_op jit(solution)/shard_map/ppermute | solution.py:36
  44.7 1.8 %collective-permute-done.16.refs_3_ = bf16[2,128,384]{2,1,0:T(8,128)(2,1)S(1)} collective-permute-done((bf16[2,128,384]{2,1,0:T(8,128)(2,1)S(1)}, bf16[2,128,384]{2,1,0:T(8,128)(2,1)S(1)}, u32[]{:S(2)}, u32[]{:S(2)}) %collective-permute-start.16) | collective-permute-done | bytes 196640 | tf_op jit(solution)/shard_map/ppermute | solution.py:36
  46.5 1.3 %collective-permute-done.17.refs_4_ = bf16[2,128,384]{2,1,0:T(8,128)(2,1)S(1)} collective-permute-done((bf16[2,128,384]{2,1,0:T(8,128)(2,1)S(1)}, bf16[2,128,384]{2,1,0:T(8,128)(2,1)S(1)}, u32[]{:S(2)}, u32[]{:S(2)}) %collective-permute-start.17) | collective-permute-done | bytes 196640 | tf_op jit(solution)/shard_map/ppermute | solution.py:36
  47.9 1.4 %collective-permute-done.21.refs_8_ = bf16[2,128,384]{2,1,0:T(8,128)(2,1)S(1)} collective-permute-done((bf16[2,128,384]{2,1,0:T(8,128)(2,1)S(1)}, bf16[2,128,384]{2,1,0:T(8,128)(2,1)S(1)}, u32[]{:S(2)}, u32[]{:S(2)}) %collective-permute-start.21) | collective-permute-done | bytes 196640 | tf_op jit(solution)/shard_map/ppermute | solution.py:40
  49.2 3.9 %cube_rows.1 = (bf16[16,128,384]{2,1,0:T(8,128)(2,1)}, bf16[49,128,384]{2,1,0:T(8,128)(2,1)S(1)}) custom-call(s32[24,128]{1,0:T(8,128)S(1)} %get-tuple-element.27.index_ref, bf16[16,128,384]{2,1,0:T(8,128)(2,1)S(1)} %stage_density.1.own_ref.density_ref, bf16[16,128,384]{2,1,0:T(8,128)(2,1)S(1)} %collective-permute-done.1.other_ref, ...), custom_call_target="tpu_custom_call", output_to_operand_aliasing={{1}: (3, {})} | custom-call | flops 1207959552 | bytes 12582912 | tf_op jit(solution)/shard_map/cube_rows/pallas_call | solution.py:330
  (26 shorter events, 1.9 us)
Async XLA Ops:
  0.0 18.9 %collective-permute-start.1 = (bf16[16,128,384]{2,1,0:T(8,128)(2,1)}, bf16[16,128,384]{2,1,0:T(8,128)(2,1)S(1)}, u32[]{:S(2)}, u32[]{:S(2)}) collective-permute-start(bf16[16,128,384]{2,1,0:T(8,128)(2,1)} %density_ref.1), channel_id=1, source_target_pairs={{0,1},{1,0},{2,3},{3,2},{4,5},{5,4},{6,7},{7,6},{8,9},{9,8},{10,11... | collective-permute-start | bytes 4718600 | tf_op jit(solution)/shard_map/ppermute | solution.py:40
  1.2 2.3 %collective-permute-start = (s32[8,128]{1,0:T(8,128)S(1)}, s32[8,128]{1,0:T(8,128)S(1)}, u32[]{:S(2)}, u32[]{:S(2)}) collective-permute-start(s32[8,128]{1,0:T(8,128)S(1)} %pad.4), channel_id=1, source_target_pairs={{0,1},{1,0},{2,3},{3,2},{4,5},{5,4},{6,7},{7,6},{8,9},{9,8},{10,11... | collective-permute-start | bytes 12296 | tf_op jit(solution)/shard_map/ppermute | solution.py:40
  1.3 1.4 %copy-start = (bf16[16,128,384]{2,1,0:T(8,128)(2,1)S(1)}, bf16[16,128,384]{2,1,0:T(8,128)(2,1)}, u32[]{:S(2)}) copy-start(bf16[16,128,384]{2,1,0:T(8,128)(2,1)} %density_ref.1) | copy-start | bytes 4718596
  3.5 8.2 %collective-permute-start.5 = (s32[16,128]{1,0:T(8,128)S(1)}, s32[16,128]{1,0:T(8,128)S(1)}, u32[]{:S(2)}, u32[]{:S(2)}) collective-permute-start(s32[16,128]{1,0:T(8,128)S(1)} %pad_add_fusion.mine_ref), channel_id=1, source_target_pairs={{0,4},{2,6},{4,0},{6,2},{8,12},{10,14},{12,8},{14,10},{1,5},{3,7},... | collective-permute-start | bytes 24584 | tf_op jit(solution)/shard_map/ppermute | solution.py:36
  6.4 6.3 %collective-permute-start.4 = (s32[16,128]{1,0:T(8,128)S(1)}, s32[16,128]{1,0:T(8,128)S(1)}, u32[]{:S(2)}, u32[]{:S(2)}) collective-permute-start(s32[16,128]{1,0:T(8,128)S(1)} %pad_add_fusion.mine_ref), channel_id=1, source_target_pairs={{0,2},{2,0},{4,6},{6,4},{8,10},{10,8},{12,14},{14,12},{1,3},{3,1},... | collective-permute-start | bytes 24584 | tf_op jit(solution)/shard_map/ppermute | solution.py:36
  8.0 5.4 %collective-permute-start.3 = (s32[16,128]{1,0:T(8,128)S(1)}, s32[16,128]{1,0:T(8,128)S(1)}, u32[]{:S(2)}, u32[]{:S(2)}) collective-permute-start(s32[16,128]{1,0:T(8,128)S(1)} %pad_add_fusion.mine_ref), channel_id=1, source_target_pairs={{0,12},{2,14},{4,8},{6,10},{8,4},{10,6},{12,0},{14,2},{1,13},{3,15... | collective-permute-start | bytes 24584 | tf_op jit(solution)/shard_map/ppermute | solution.py:36
  10.4 6.5 %collective-permute-start.2 = (s32[16,128]{1,0:T(8,128)S(1)}, s32[16,128]{1,0:T(8,128)S(1)}, u32[]{:S(2)}, u32[]{:S(2)}) collective-permute-start(s32[16,128]{1,0:T(8,128)S(1)} %pad_add_fusion.mine_ref), channel_id=1, source_target_pairs={{0,14},{2,4},{4,2},{6,8},{8,6},{10,12},{12,10},{14,0},{1,15},{3,5}... | collective-permute-start | bytes 24584 | tf_op jit(solution)/shard_map/ppermute | solution.py:36
  12.0 9.9 %collective-permute-start.9 = (bf16[2,128,384]{2,1,0:T(8,128)(2,1)S(1)}, bf16[2,128,384]{2,1,0:T(8,128)(2,1)S(1)}, u32[]{:S(2)}, u32[]{:S(2)}) collective-permute-start(bf16[2,128,384]{2,1,0:T(8,128)(2,1)S(1)} %gather_rows.7), channel_id=1, source_target_pairs={{0,4},{2,6},{4,0},{6,2},{8,12},{10,14},{12,8},{14,10},{1,5},{3,7},... | collective-permute-start | bytes 589832 | tf_op jit(solution)/shard_map/ppermute | solution.py:36
  12.9 9.0 %collective-permute-start.8 = (bf16[2,128,384]{2,1,0:T(8,128)(2,1)S(1)}, bf16[2,128,384]{2,1,0:T(8,128)(2,1)S(1)}, u32[]{:S(2)}, u32[]{:S(2)}) collective-permute-start(bf16[2,128,384]{2,1,0:T(8,128)(2,1)S(1)} %gather_rows.6), channel_id=1, source_target_pairs={{0,2},{2,0},{4,6},{6,4},{8,10},{10,8},{12,14},{14,12},{1,3},{3,1},... | collective-permute-start | bytes 589832 | tf_op jit(solution)/shard_map/ppermute | solution.py:36
  13.6 10.1 %collective-permute-start.7 = (bf16[2,128,384]{2,1,0:T(8,128)(2,1)S(1)}, bf16[2,128,384]{2,1,0:T(8,128)(2,1)S(1)}, u32[]{:S(2)}, u32[]{:S(2)}) collective-permute-start(bf16[2,128,384]{2,1,0:T(8,128)(2,1)S(1)} %gather_rows.5), channel_id=1, source_target_pairs={{0,12},{2,14},{4,8},{6,10},{8,4},{10,6},{12,0},{14,2},{1,13},{3,15... | collective-permute-start | bytes 589832 | tf_op jit(solution)/shard_map/ppermute | solution.py:36
  17.2 11.0 %collective-permute-start.6 = (bf16[2,128,384]{2,1,0:T(8,128)(2,1)S(1)}, bf16[2,128,384]{2,1,0:T(8,128)(2,1)S(1)}, u32[]{:S(2)}, u32[]{:S(2)}) collective-permute-start(bf16[2,128,384]{2,1,0:T(8,128)(2,1)S(1)} %gather_rows.4), channel_id=1, source_target_pairs={{0,14},{2,4},{4,2},{6,8},{8,6},{10,12},{12,10},{14,0},{1,15},{3,5}... | collective-permute-start | bytes 589832 | tf_op jit(solution)/shard_map/ppermute | solution.py:36
  28.2 1.4 %collective-permute-start.10 = (bf16[2,128,384]{2,1,0:T(8,128)(2,1)S(1)}, bf16[2,128,384]{2,1,0:T(8,128)(2,1)S(1)}, u32[]{:S(2)}, u32[]{:S(2)}) collective-permute-start(bf16[2,128,384]{2,1,0:T(8,128)(2,1)S(1)} %collective-permute-done.6.refs_1_), channel_id=1, source_target_pairs={{0,1},{1,0},{2,3},{3,2},{4,5},{5,4},{6,7},{7,6},{8,9},{9,8},{10,11... | collective-permute-start | bytes 589832 | tf_op jit(solution)/shard_map/ppermute | solution.py:40
  28.2 1.7 %collective-permute-start.11 = (bf16[2,128,384]{2,1,0:T(8,128)(2,1)S(1)}, bf16[2,128,384]{2,1,0:T(8,128)(2,1)S(1)}, u32[]{:S(2)}, u32[]{:S(2)}) collective-permute-start(bf16[2,128,384]{2,1,0:T(8,128)(2,1)S(1)} %collective-permute-done.7.refs_2_), channel_id=1, source_target_pairs={{0,1},{1,0},{2,3},{3,2},{4,5},{5,4},{6,7},{7,6},{8,9},{9,8},{10,11... | collective-permute-start | bytes 589832 | tf_op jit(solution)/shard_map/ppermute | solution.py:40
  28.7 1.5 %collective-permute-start.12 = (bf16[2,128,384]{2,1,0:T(8,128)(2,1)S(1)}, bf16[2,128,384]{2,1,0:T(8,128)(2,1)S(1)}, u32[]{:S(2)}, u32[]{:S(2)}) collective-permute-start(bf16[2,128,384]{2,1,0:T(8,128)(2,1)S(1)} %collective-permute-done.8.refs_3_), channel_id=1, source_target_pairs={{0,1},{1,0},{2,3},{3,2},{4,5},{5,4},{6,7},{7,6},{8,9},{9,8},{10,11... | collective-permute-start | bytes 589832 | tf_op jit(solution)/shard_map/ppermute | solution.py:40
  28.7 1.8 %collective-permute-start.13 = (bf16[2,128,384]{2,1,0:T(8,128)(2,1)S(1)}, bf16[2,128,384]{2,1,0:T(8,128)(2,1)S(1)}, u32[]{:S(2)}, u32[]{:S(2)}) collective-permute-start(bf16[2,128,384]{2,1,0:T(8,128)(2,1)S(1)} %collective-permute-done.9.refs_4_), channel_id=1, source_target_pairs={{0,1},{1,0},{2,3},{3,2},{4,5},{5,4},{6,7},{7,6},{8,9},{9,8},{10,11... | collective-permute-start | bytes 589832 | tf_op jit(solution)/shard_map/ppermute | solution.py:40
  32.4 10.7 %collective-permute-start.14 = (bf16[2,128,384]{2,1,0:T(8,128)(2,1)S(1)}, bf16[2,128,384]{2,1,0:T(8,128)(2,1)S(1)}, u32[]{:S(2)}, u32[]{:S(2)}) collective-permute-start(bf16[2,128,384]{2,1,0:T(8,128)(2,1)S(1)} %get-tuple-element.36), channel_id=1, source_target_pairs={{0,14},{2,4},{4,2},{6,8},{8,6},{10,12},{12,10},{14,0},{1,15},{3,5}... | collective-permute-start | bytes 589832 | tf_op jit(solution)/shard_map/ppermute | solution.py:36
  34.2 10.4 %collective-permute-start.15 = (bf16[2,128,384]{2,1,0:T(8,128)(2,1)S(1)}, bf16[2,128,384]{2,1,0:T(8,128)(2,1)S(1)}, u32[]{:S(2)}, u32[]{:S(2)}) collective-permute-start(bf16[2,128,384]{2,1,0:T(8,128)(2,1)S(1)} %get-tuple-element.38), channel_id=1, source_target_pairs={{0,12},{2,14},{4,8},{6,10},{8,4},{10,6},{12,0},{14,2},{1,13},{3,15... | collective-permute-start | bytes 589832 | tf_op jit(solution)/shard_map/ppermute | solution.py:36
  34.7 11.8 %collective-permute-start.16 = (bf16[2,128,384]{2,1,0:T(8,128)(2,1)S(1)}, bf16[2,128,384]{2,1,0:T(8,128)(2,1)S(1)}, u32[]{:S(2)}, u32[]{:S(2)}) collective-permute-start(bf16[2,128,384]{2,1,0:T(8,128)(2,1)S(1)} %get-tuple-element.40), channel_id=1, source_target_pairs={{0,2},{2,0},{4,6},{6,4},{8,10},{10,8},{12,14},{14,12},{1,3},{3,1},... | collective-permute-start | bytes 589832 | tf_op jit(solution)/shard_map/ppermute | solution.py:36
  37.8 10.0 %collective-permute-start.17 = (bf16[2,128,384]{2,1,0:T(8,128)(2,1)S(1)}, bf16[2,128,384]{2,1,0:T(8,128)(2,1)S(1)}, u32[]{:S(2)}, u32[]{:S(2)}) collective-permute-start(bf16[2,128,384]{2,1,0:T(8,128)(2,1)S(1)} %get-tuple-element.42), channel_id=1, source_target_pairs={{0,4},{2,6},{4,0},{6,2},{8,12},{10,14},{12,8},{14,10},{1,5},{3,7},... | collective-permute-start | bytes 589832 | tf_op jit(solution)/shard_map/ppermute | solution.py:36
  43.1 4.7 %collective-permute-start.18 = (bf16[2,128,384]{2,1,0:T(8,128)(2,1)S(1)}, bf16[2,128,384]{2,1,0:T(8,128)(2,1)S(1)}, u32[]{:S(2)}, u32[]{:S(2)}) collective-permute-start(bf16[2,128,384]{2,1,0:T(8,128)(2,1)S(1)} %collective-permute-done.14.refs_1_), channel_id=1, source_target_pairs={{0,1},{1,0},{2,3},{3,2},{4,5},{5,4},{6,7},{7,6},{8,9},{9,8},{10,11... | collective-permute-start | bytes 589832 | tf_op jit(solution)/shard_map/ppermute | solution.py:40
  44.7 3.2 %collective-permute-start.19 = (bf16[2,128,384]{2,1,0:T(8,128)(2,1)S(1)}, bf16[2,128,384]{2,1,0:T(8,128)(2,1)S(1)}, u32[]{:S(2)}, u32[]{:S(2)}) collective-permute-start(bf16[2,128,384]{2,1,0:T(8,128)(2,1)S(1)} %collective-permute-done.15.refs_2_), channel_id=1, source_target_pairs={{0,1},{1,0},{2,3},{3,2},{4,5},{5,4},{6,7},{7,6},{8,9},{9,8},{10,11... | collective-permute-start | bytes 589832 | tf_op jit(solution)/shard_map/ppermute | solution.py:40
  46.4 1.4 %collective-permute-start.20 = (bf16[2,128,384]{2,1,0:T(8,128)(2,1)S(1)}, bf16[2,128,384]{2,1,0:T(8,128)(2,1)S(1)}, u32[]{:S(2)}, u32[]{:S(2)}) collective-permute-start(bf16[2,128,384]{2,1,0:T(8,128)(2,1)S(1)} %collective-permute-done.16.refs_3_), channel_id=1, source_target_pairs={{0,1},{1,0},{2,3},{3,2},{4,5},{5,4},{6,7},{7,6},{8,9},{9,8},{10,11... | collective-permute-start | bytes 589832 | tf_op jit(solution)/shard_map/ppermute | solution.py:40
  47.8 1.4 %collective-permute-start.21 = (bf16[2,128,384]{2,1,0:T(8,128)(2,1)S(1)}, bf16[2,128,384]{2,1,0:T(8,128)(2,1)S(1)}, u32[]{:S(2)}, u32[]{:S(2)}) collective-permute-start(bf16[2,128,384]{2,1,0:T(8,128)(2,1)S(1)} %collective-permute-done.17.refs_4_), channel_id=1, source_target_pairs={{0,1},{1,0},{2,3},{3,2},{4,5},{5,4},{6,7},{7,6},{8,9},{9,8},{10,11... | collective-permute-start | bytes 589832 | tf_op jit(solution)/shard_map/ppermute | solution.py:40

commit v6 on v5

--- a/solution.py
+++ b/solution.py
@@ -109,7 +109,7 @@
 
 def tables_kernel(half, peers, mine_ref, own_ref, other_ref, *refs):
     near, refs = refs[: len(EXCHANGES)], refs[len(EXCHANGES) :]
-    square_ref, others_ref, cube_ref, table_ref, sems = refs
+    wanted_ref, square_ref, others_ref, cube_ref, table_ref, sems = refs
     own, edge, wide = own_ref.shape
     copies = stack(table_ref, own_ref, other_ref, sems)
     me = lax.axis_index("rows")
@@ -184,7 +184,11 @@
     met = met_in(kept_table)
     for s in range(half):
         cube_ref[s * SUBLANES : (s + 1) * SUBLANES] = choose(met, s, place, empty)
-    square_ref[SUBLANES - 1 : SUBLANES] = asked
+    asked_all = jnp.broadcast_to(asked, shape)
+    for s in range(half):
+        rows = slice(s * SUBLANES, (s + 1) * SUBLANES)
+        wanted_ref[rows] = jnp.take_along_axis(square_ref[rows], asked_all, axis=1)
+    wanted_ref[SUBLANES - 1 : SUBLANES] = asked
     for copy in copies:
         copy.wait()
 
@@ -201,9 +205,9 @@
     shape = jax.ShapeDtypeStruct((half * SUBLANES, LANES), jnp.int32)
     return pl.pallas_call(
         functools.partial(tables_kernel, half, lax.axis_size("rows")),
-        out_shape=[shape, shape, shape, table_like(own)],
+        out_shape=[shape, shape, shape, shape, table_like(own)],
         in_specs=[VMEM] * (3 + len(near)),
-        out_specs=[VMEM] * 4,
+        out_specs=[VMEM] * 5,
         scratch_shapes=[pltpu.SemaphoreType.DMA((2,))],
         compiler_params=PARAMS,
         cost_estimate=cost(0, 4 * own.size * 2),
@@ -237,46 +241,48 @@
     return total
 
 
-def row_product(table, index_ref, row, own_ref, other_ref, half, edge):
+def row_product(table, index_ref, entry, own_ref, other_ref, half, edge, row=None):
     stride = table_stride(half, edge)
+    row = entry if row is None else row
 
     def left(k):
         ref = own_ref if k < half else other_ref
         return ref[row, :, (k % half) * edge : (k % half + 1) * edge]
 
     def right(k, s):
-        return block_at(table, index_ref[s * SUBLANES + k, row], stride, edge)
+        return block_at(table, index_ref[s * SUBLANES + k, entry], stride, edge)
 
     return product(left, right, 2 * half, half)
 
 
-def wanted_kernel(half, index_ref, own_ref, other_ref, *refs):
-    pieces = refs[1 : 1 + 2 * len(EXCHANGES)]
-    *wanted, table = refs[1 + len(pieces) :]
+def wanted_kernel(half, first, far, index_ref, own_ref, other_ref, table_in, *refs):
+    pieces, (*wanted, table) = refs[:far], refs[far:] if far else (*refs, table_in)
     own, edge, wide = own_ref.shape
-    add_far(table, 2 * own, pieces[: len(EXCHANGES)], pieces[len(EXCHANGES) :])
+    if far:
+        add_far(table, 2 * own, pieces[: far // 2], pieces[far // 2 :])
     for position, piece in enumerate(wanted):
         for k in range(CAP):
-            row = index_ref[SUBLANES - 1, position * CAP + k]
-            total = row_product(table, index_ref, row, own_ref, other_ref, half, edge)
+            n = (first + position) * CAP + k
+            row = index_ref[SUBLANES - 1, n]
+            total = row_product(table, index_ref, n, own_ref, other_ref, half, edge, row)
             piece[k] = total.astype(piece.dtype)
 
 
-def square_wanted(index, own, other, table, pieces, half):
+def square_wanted(index, own, other, table, pieces, half, first, count):
     size, edge, wide = own.shape
     piece = jax.ShapeDtypeStruct((CAP, edge, wide), own.dtype)
-    count = len(EXCHANGES)
-    *wanted, table = pl.pallas_call(
-        functools.partial(wanted_kernel, half),
-        out_shape=[*([piece] * count), like(table)],
-        in_specs=[SMEM] + [VMEM] * (3 + len(pieces)),
-        out_specs=[VMEM] * (1 + count),
-        input_output_aliases={3: count},
-        compiler_params=PARAMS,
-        cost_estimate=cost(FAR * 4 * edge * wide * wide, 8 * own.size * 2),
+    changed = [like(table)] if pieces else []
+    out = pl.pallas_call(
+        functools.partial(wanted_kernel, half, first, len(pieces)),
+        out_shape=[piece] * count + changed,
+        in_specs=[VMEM] * (4 + len(pieces)),
+        out_specs=[VMEM] * (count + len(changed)),
+        input_output_aliases={3: count} if pieces else {},
+        compiler_params=PARAMS,
+        cost_estimate=cost(count * CAP * 4 * edge * wide * wide, 8 * own.size * 2),
         name="square_wanted",
     )(index, own, other, table, *pieces)
-    return wanted, table
+    return out[:count], out[count] if pieces else table
 
 
 def square_kernel(half, index_ref, others_ref, own_ref, other_ref, table_ref, out):
@@ -314,13 +320,10 @@
     def written(i):
         return pltpu.make_async_copy(out.at[i], result.at[i], sems.at[i])
 
-    def body(i, carry):
+    for i in range(own):
         total = row_product(table, index_ref, i, own_ref, other_ref, half, edge)
         out[i] = (3.0 * table[i].astype(jnp.float32) - 2.0 * total).astype(out.dtype)
         written(i).start()
-        return carry
-
-    lax.fori_loop(0, own, body, 0, unroll=True)
     for i in range(own):
         written(i).wait()
 
@@ -330,10 +333,13 @@
     return pl.pallas_call(
         functools.partial(cube_kernel, half),
         out_shape=[like(own), like(table)],
-        in_specs=[SMEM] + [VMEM] * (3 + len(pieces)),
+        in_specs=[VMEM] * (4 + len(pieces)),
         out_specs=[pl.BlockSpec(memory_space=pl.ANY), VMEM],
         input_output_aliases={3: 1},
-        scratch_shapes=[pltpu.VMEM(own.shape, own.dtype), pltpu.SemaphoreType.DMA((size,))],
+        scratch_shapes=[
+            pltpu.VMEM(own.shape, own.dtype),
+            pltpu.SemaphoreType.DMA((size,)),
+        ],
         compiler_params=PARAMS,
         cost_estimate=cost(size * 4 * edge * wide * wide, 8 * own.size * 2),
         name="cube_rows",
@@ -342,18 +348,23 @@
 
 def local(density, columns, kept):
     half = columns.shape[1]
-    other = from_sibling(density)
     numbers = spread(columns, kept)
     mine = jnp.concatenate([numbers, from_sibling(numbers)], axis=0)
     mine, own = lax.optimization_barrier((mine, stage(density)))
+    other = from_sibling(own)
     near = [swapped(mine, exchange) for exchange in EXCHANGES]
     pieces = [gather(own, numbers, half) for numbers in near]
     got = [swapped(piece, exchange) for exchange, piece in zip(EXCHANGES, pieces)]
     *indices, table = tables(mine, near, own, other, half)
     got = [lax.optimization_barrier((piece, table))[0] for piece in got]
     got += [from_sibling(piece) for piece in got]
-    square_index, others_index, cube_index = indices
-    wanted, table = square_wanted(square_index, own, other, table, got, half)
+    wanted_index, square_index, others_index, cube_index = indices
+    wanted, part = [], len(EXCHANGES) // 2
+    for first in range(0, len(EXCHANGES), part):
+        more, table = square_wanted(
+            wanted_index, own, other, table, [] if first else got, half, first, part
+        )
+        wanted += more
 
     got = [swapped(piece, exchange) for exchange, piece in zip(EXCHANGES, wanted)]
     squares = square(square_index, others_index, own, other, table, half)

time: 54.2 us -> 51.8 us (0.956)
  waiting for transfers between devices: 17.3 us -> 15.5 us
  Pallas kernels: 12.7 us -> 11.8 us
  starting transfers between devices: 21 us -> 21.7 us
    ppermute x12, waiting for transfers between devices: 13.9 us -> 12.8 us  [swapped(): return lax.ppermute(value, 'rows', pairs)]
    ppermute x10, waiting for transfers between devices: 3.37 us -> 2.69 us  [from_sibling(): return lax.ppermute(value, 'layers', [(0, 1), (1, 0)])]
    pallas_call x1, Pallas kernels: 3.93 us -> 3.27 us  [cube(): pl.pallas_call(functools.partial(cube_kernel, half), out_shape=[like(own)...]
    ppermute x10, starting transfers between devices: 1.62 us -> 2.2 us  [from_sibling(): return lax.ppermute(value, 'layers', [(0, 1), (1, 0)])]
    pallas_call x1 -> x2, Pallas kernels: 1.99 us -> 1.58 us  [square_wanted(): pl.pallas_call(functools.partial(wanted_kernel, half, first, len(pieces))...]
  transfers between devices with their start and end apart: 22 -> 22, of which waited for: 16 -> 13; matrix products, arithmetic and copies ran while one was open for 1% -> 0% of each run, Pallas kernels for 13% -> 15%
where the time goes in v6:
time: 51.8 us; the launch traced here: 51.2 us
  starting transfers between devices  21.7 us (42%)
  waiting for transfers between devices  15.5 us (30%)
  Pallas kernels  11.8 us (23%)
  local copies, waits for them, and re-layouts  1.41 us (3%)
  other arithmetic  0.71 us (1%)
    ppermute x12, starting transfers between devices, swapped(): return lax.ppermute(value, 'rows', pairs)  19.5 us
    ppermute x12, waiting for transfers between devices, swapped(): return lax.ppermute(value, 'rows', pairs)  12.8 us
    pallas_call x1, Pallas kernels, square(): pl.pallas_call(functools.partial(square_kernel, half), out_shape=like(tab...  5.23 us
    pallas_call x1, Pallas kernels, cube(): pl.pallas_call(functools.partial(cube_kernel, half), out_shape=[like(own)...  3.27 us
    ppermute x10, waiting for transfers between devices, from_sibling(): return lax.ppermute(value, 'layers', [(0, 1), (1, 0)])  2.69 us
    ppermute x10, starting transfers between devices, from_sibling(): return lax.ppermute(value, 'layers', [(0, 1), (1, 0)])  2.2 us
    pallas_call x2, Pallas kernels, square_wanted(): pl.pallas_call(functools.partial(wanted_kernel, half, first, len(pieces))...  1.58 us
    unnamed x2, local copies, waits for them, and re-layouts  1.41 us
  transfers between devices with their start and end apart: 22, of which 13 were waited for; matrix products, arithmetic and copies ran while one was open for 0% of the time, Pallas kernels for 15%

profile of v6, /device:TPU:0, one launch (start us, length us, event | category | flops | bytes accessed | tf_op | source)
XLA Modules:
  0.0 51.2 jit_solution(3663387422105771090)
XLA Ops:
  0.0 0.7 %add_bitcast_fusion = s32[6,16]{1,0:T(8,128)S(1)} fusion(s32[16,3]{0,1:T(4,128)} %param.5, s32[16,3]{0,1:T(4,128)} %param.4), kind=kLoop, calls=%fused_computation.1 | loop fusion | flops 96 | bytes 768 | tf_op jit(solution)/shard_map/transpose | solution.py:63
  0.7 0.5 %collective-permute-start = (s32[8,128]{1,0:T(8,128)S(1)}, s32[8,128]{1,0:T(8,128)S(1)}, u32[]{:S(2)}, u32[]{:S(2)}) collective-permute-start(s32[8,128]{1,0:T(8,128)S(1)} %pad.4), channel_id=1, source_target_pairs={{0,1},{1,0},{2,3},{3,2},{4,5},{5,4},{6,7},{7,6},{8,9},{9,8},{10,11... | collective-permute-start | bytes 12296 | tf_op jit(solution)/shard_map/ppermute | solution.py:40
  1.2 1.4 %copy-done = bf16[16,128,384]{2,1,0:T(8,128)(2,1)S(1)} copy-done((bf16[16,128,384]{2,1,0:T(8,128)(2,1)S(1)}, bf16[16,128,384]{2,1,0:T(8,128)(2,1)}, u32[]{:S(2)}) %copy-start) | copy-done | bytes 1572888
  2.9 3.0 %collective-permute-start.5 = (s32[16,128]{1,0:T(8,128)S(1)}, s32[16,128]{1,0:T(8,128)S(1)}, u32[]{:S(2)}, u32[]{:S(2)}) collective-permute-start(s32[16,128]{1,0:T(8,128)S(1)} %pad_add_fusion.mine_ref), channel_id=1, source_target_pairs={{0,4},{2,6},{4,0},{6,2},{8,12},{10,14},{12,8},{14,10},{1,5},{3,7},... | collective-permute-start | bytes 24584 | tf_op jit(solution)/shard_map/ppermute | solution.py:36
  5.9 1.5 %collective-permute-start.4 = (s32[16,128]{1,0:T(8,128)S(1)}, s32[16,128]{1,0:T(8,128)S(1)}, u32[]{:S(2)}, u32[]{:S(2)}) collective-permute-start(s32[16,128]{1,0:T(8,128)S(1)} %pad_add_fusion.mine_ref), channel_id=1, source_target_pairs={{0,2},{2,0},{4,6},{6,4},{8,10},{10,8},{12,14},{14,12},{1,3},{3,1},... | collective-permute-start | bytes 24584 | tf_op jit(solution)/shard_map/ppermute | solution.py:36
  7.5 2.5 %collective-permute-start.3 = (s32[16,128]{1,0:T(8,128)S(1)}, s32[16,128]{1,0:T(8,128)S(1)}, u32[]{:S(2)}, u32[]{:S(2)}) collective-permute-start(s32[16,128]{1,0:T(8,128)S(1)} %pad_add_fusion.mine_ref), channel_id=1, source_target_pairs={{0,12},{2,14},{4,8},{6,10},{8,4},{10,6},{12,0},{14,2},{1,13},{3,15... | collective-permute-start | bytes 24584 | tf_op jit(solution)/shard_map/ppermute | solution.py:36
  9.9 1.3 %collective-permute-start.2 = (s32[16,128]{1,0:T(8,128)S(1)}, s32[16,128]{1,0:T(8,128)S(1)}, u32[]{:S(2)}, u32[]{:S(2)}) collective-permute-start(s32[16,128]{1,0:T(8,128)S(1)} %pad_add_fusion.mine_ref), channel_id=1, source_target_pairs={{0,14},{2,4},{4,2},{6,8},{8,6},{10,12},{12,10},{14,0},{1,15},{3,5}... | collective-permute-start | bytes 24584 | tf_op jit(solution)/shard_map/ppermute | solution.py:36
  11.5 0.7 %collective-permute-start.9 = (bf16[2,128,384]{2,1,0:T(8,128)(2,1)S(1)}, bf16[2,128,384]{2,1,0:T(8,128)(2,1)S(1)}, u32[]{:S(2)}, u32[]{:S(2)}) collective-permute-start(bf16[2,128,384]{2,1,0:T(8,128)(2,1)S(1)} %gather_rows.7), channel_id=1, source_target_pairs={{0,4},{2,6},{4,0},{6,2},{8,12},{10,14},{12,8},{14,10},{1,5},{3,7},... | collective-permute-start | bytes 589832 | tf_op jit(solution)/shard_map/ppermute | solution.py:36
  13.1 3.0 %collective-permute-start.7 = (bf16[2,128,384]{2,1,0:T(8,128)(2,1)S(1)}, bf16[2,128,384]{2,1,0:T(8,128)(2,1)S(1)}, u32[]{:S(2)}, u32[]{:S(2)}) collective-permute-start(bf16[2,128,384]{2,1,0:T(8,128)(2,1)S(1)} %gather_rows.5), channel_id=1, source_target_pairs={{0,12},{2,14},{4,8},{6,10},{8,4},{10,6},{12,0},{14,2},{1,13},{3,15... | collective-permute-start | bytes 589832 | tf_op jit(solution)/shard_map/ppermute | solution.py:36
  16.7 1.7 %collective-permute-start.6 = (bf16[2,128,384]{2,1,0:T(8,128)(2,1)S(1)}, bf16[2,128,384]{2,1,0:T(8,128)(2,1)S(1)}, u32[]{:S(2)}, u32[]{:S(2)}) collective-permute-start(bf16[2,128,384]{2,1,0:T(8,128)(2,1)S(1)} %gather_rows.4), channel_id=1, source_target_pairs={{0,14},{2,4},{4,2},{6,8},{8,6},{10,12},{12,10},{14,0},{1,15},{3,5}... | collective-permute-start | bytes 589832 | tf_op jit(solution)/shard_map/ppermute | solution.py:36
  18.4 0.7 %block_tables.1 = (s32[24,128]{1,0:T(8,128)S(1)}, s32[24,128]{1,0:T(8,128)S(1)}, s32[24,128]{1,0:T(8,128)S(1)}, s32[24,128]{1,0:T(8,128)S(1)}, bf16[49,128,384]{2,1,0:T(8,128)(2,1)S(1)}) custom-call(s32[16,128]{1,0:T(8,128)S(1)} %pad_add_fusion.mine_ref, bf16[16,128,384]{2,1,0:T(8,128)(2,1)S(1)} %stage_density.1.own_ref.density_ref, ...), custom_call_target="tpu_custom_call" | custom-call | bytes 6291456 | tf_op jit(solution)/shard_map/block_tables/pallas_call | solution.py:206
  19.1 2.3 %collective-permute-done.9.refs_3_ = bf16[2,128,384]{2,1,0:T(8,128)(2,1)S(1)} collective-permute-done((bf16[2,128,384]{2,1,0:T(8,128)(2,1)S(1)}, bf16[2,128,384]{2,1,0:T(8,128)(2,1)S(1)}, u32[]{:S(2)}, u32[]{:S(2)}) %collective-permute-start.9) | collective-permute-done | bytes 196640 | tf_op jit(solution)/shard_map/ppermute | solution.py:36
  21.3 1.9 %collective-permute-done.7.refs_1_ = bf16[2,128,384]{2,1,0:T(8,128)(2,1)S(1)} collective-permute-done((bf16[2,128,384]{2,1,0:T(8,128)(2,1)S(1)}, bf16[2,128,384]{2,1,0:T(8,128)(2,1)S(1)}, u32[]{:S(2)}, u32[]{:S(2)}) %collective-permute-start.7) | collective-permute-done | bytes 196640 | tf_op jit(solution)/shard_map/ppermute | solution.py:36
  23.2 4.4 %collective-permute-done.6.refs_0_ = bf16[2,128,384]{2,1,0:T(8,128)(2,1)S(1)} collective-permute-done((bf16[2,128,384]{2,1,0:T(8,128)(2,1)S(1)}, bf16[2,128,384]{2,1,0:T(8,128)(2,1)S(1)}, u32[]{:S(2)}, u32[]{:S(2)}) %collective-permute-start.6) | collective-permute-done | bytes 196640 | tf_op jit(solution)/shard_map/ppermute | solution.py:36
  27.6 0.5 collective-permute-start.11
  28.1 0.5 collective-permute-start.13
  28.6 0.4 collective-permute-done.10.refs_4_
  29.0 0.3 collective-permute-done.11.refs_5_
  29.3 0.3 collective-permute-done.12.refs_6_
  29.6 0.3 collective-permute-done.13.refs_7_
  29.9 0.8 %square_wanted.2 = (bf16[2,128,384]{2,1,0:T(8,128)(2,1)S(1)}, bf16[2,128,384]{2,1,0:T(8,128)(2,1)S(1)}, bf16[49,128,384]{2,1,0:T(8,128)(2,1)S(1)}) custom-call(s32[24,128]{1,0:T(8,128)S(1)} %get-tuple-element.31.index_ref, bf16[16,128,384]{2,1,0:T(8,128)(2,1)S(1)} %stage_density.1.own_ref.density_ref, ...), custom_call_target="tpu_custom_call", output_to_operand_aliasing={{2}: (3, {})} | custom-call | flops 301989888 | bytes 12582912 | tf_op jit(solution)/shard_map/square_wanted/pallas_call | solution.py:275
  30.7 1.8 %collective-permute-start.14 = (bf16[2,128,384]{2,1,0:T(8,128)(2,1)S(1)}, bf16[2,128,384]{2,1,0:T(8,128)(2,1)S(1)}, u32[]{:S(2)}, u32[]{:S(2)}) collective-permute-start(bf16[2,128,384]{2,1,0:T(8,128)(2,1)S(1)} %get-tuple-element.38), channel_id=1, source_target_pairs={{0,14},{2,4},{4,2},{6,8},{8,6},{10,12},{12,10},{14,0},{1,15},{3,5}... | collective-permute-start | bytes 589832 | tf_op jit(solution)/shard_map/ppermute | solution.py:36
  32.4 0.5 collective-permute-start.15
  32.9 0.8 %square_wanted.3 = (bf16[2,128,384]{2,1,0:T(8,128)(2,1)S(1)}, bf16[2,128,384]{2,1,0:T(8,128)(2,1)S(1)}) custom-call(s32[24,128]{1,0:T(8,128)S(1)} %get-tuple-element.31.index_ref, bf16[16,128,384]{2,1,0:T(8,128)(2,1)S(1)} %stage_density.1.own_ref.density_ref, bf16[16,128,384]{2,1,0:T(8,128)(2,1)S(1)} %collective-permute-done.1.other_ref, ...), custom_call_target="tpu_custom_call" | custom-call | flops 301989888 | bytes 12582912 | tf_op jit(solution)/shard_map/square_wanted/pallas_call | solution.py:275
  33.7 3.2 %collective-permute-start.16 = (bf16[2,128,384]{2,1,0:T(8,128)(2,1)S(1)}, bf16[2,128,384]{2,1,0:T(8,128)(2,1)S(1)}, u32[]{:S(2)}, u32[]{:S(2)}) collective-permute-start(bf16[2,128,384]{2,1,0:T(8,128)(2,1)S(1)} %get-tuple-element.42), channel_id=1, source_target_pairs={{0,2},{2,0},{4,6},{6,4},{8,10},{10,8},{12,14},{14,12},{1,3},{3,1},... | collective-permute-start | bytes 589832 | tf_op jit(solution)/shard_map/ppermute | solution.py:36
  36.9 5.2 %square_rows.1.refs_0_ = bf16[49,128,384]{2,1,0:T(8,128)(2,1)S(1)} custom-call(s32[24,128]{1,0:T(8,128)S(1)} %get-tuple-element.29.index_ref, s32[24,128]{1,0:T(8,128)S(1)} %get-tuple-element.30.others_ref, bf16[16,128,384]{2,1,0:T(8,128)(2,1)S(1)} %stage_density.1.own_ref.density_ref, bf16[16,128,384]{2,1,0:T(8,128)(2,1)S(1)} %collective-permute-done.1.other_ref, ...), custom_call_target="tpu_custom_call" | custom-call | flops 2415919104 | bytes 12582912 | tf_op jit(solution)/shard_map/square_rows/pallas_call | solution.py:303
  42.1 0.8 %collective-permute-done.15.refs_2_ = bf16[2,128,384]{2,1,0:T(8,128)(2,1)S(1)} collective-permute-done((bf16[2,128,384]{2,1,0:T(8,128)(2,1)S(1)}, bf16[2,128,384]{2,1,0:T(8,128)(2,1)S(1)}, u32[]{:S(2)}, u32[]{:S(2)}) %collective-permute-start.15) | collective-permute-done | bytes 196640 | tf_op jit(solution)/shard_map/ppermute | solution.py:36
  42.9 0.5 collective-permute-start.19
  43.4 1.3 %collective-permute-done.16.refs_3_ = bf16[2,128,384]{2,1,0:T(8,128)(2,1)S(1)} collective-permute-done((bf16[2,128,384]{2,1,0:T(8,128)(2,1)S(1)}, bf16[2,128,384]{2,1,0:T(8,128)(2,1)S(1)}, u32[]{:S(2)}, u32[]{:S(2)}) %collective-permute-start.16) | collective-permute-done | bytes 196640 | tf_op jit(solution)/shard_map/ppermute | solution.py:36
  44.8 1.7 %collective-permute-done.17.refs_4_ = bf16[2,128,384]{2,1,0:T(8,128)(2,1)S(1)} collective-permute-done((bf16[2,128,384]{2,1,0:T(8,128)(2,1)S(1)}, bf16[2,128,384]{2,1,0:T(8,128)(2,1)S(1)}, u32[]{:S(2)}, u32[]{:S(2)}) %collective-permute-start.17) | collective-permute-done | bytes 196640 | tf_op jit(solution)/shard_map/ppermute | solution.py:36
  46.5 1.4 %collective-permute-done.21.refs_8_ = bf16[2,128,384]{2,1,0:T(8,128)(2,1)S(1)} collective-permute-done((bf16[2,128,384]{2,1,0:T(8,128)(2,1)S(1)}, bf16[2,128,384]{2,1,0:T(8,128)(2,1)S(1)}, u32[]{:S(2)}, u32[]{:S(2)}) %collective-permute-start.21) | collective-permute-done | bytes 196640 | tf_op jit(solution)/shard_map/ppermute | solution.py:40
  47.9 3.3 %cube_rows.1 = (bf16[16,128,384]{2,1,0:T(8,128)(2,1)}, bf16[49,128,384]{2,1,0:T(8,128)(2,1)S(1)}) custom-call(s32[24,128]{1,0:T(8,128)S(1)} %get-tuple-element.28.index_ref, bf16[16,128,384]{2,1,0:T(8,128)(2,1)S(1)} %stage_density.1.own_ref.density_ref, bf16[16,128,384]{2,1,0:T(8,128)(2,1)S(1)} %collective-permute-done.1.other_ref, ...), custom_call_target="tpu_custom_call", output_to_operand_aliasing={{1}: (3, {})} | custom-call | flops 1207959552 | bytes 12582912 | tf_op jit(solution)/shard_map/cube_rows/pallas_call | solution.py:333
  (27 shorter events, 2.0 us)
Async XLA Ops:
  0.7 2.1 %collective-permute-start = (s32[8,128]{1,0:T(8,128)S(1)}, s32[8,128]{1,0:T(8,128)S(1)}, u32[]{:S(2)}, u32[]{:S(2)}) collective-permute-start(s32[8,128]{1,0:T(8,128)S(1)} %pad.4), channel_id=1, source_target_pairs={{0,1},{1,0},{2,3},{3,2},{4,5},{5,4},{6,7},{7,6},{8,9},{9,8},{10,11... | collective-permute-start | bytes 12296 | tf_op jit(solution)/shard_map/ppermute | solution.py:40
  1.2 1.4 %copy-start = (bf16[16,128,384]{2,1,0:T(8,128)(2,1)S(1)}, bf16[16,128,384]{2,1,0:T(8,128)(2,1)}, u32[]{:S(2)}) copy-start(bf16[16,128,384]{2,1,0:T(8,128)(2,1)} %density_ref.1) | copy-start | bytes 4718596
  2.8 15.6 %collective-permute-start.1 = (bf16[16,128,384]{2,1,0:T(8,128)(2,1)S(1)}, bf16[16,128,384]{2,1,0:T(8,128)(2,1)S(1)}, u32[]{:S(2)}, u32[]{:S(2)}) collective-permute-start(bf16[16,128,384]{2,1,0:T(8,128)(2,1)S(1)} %stage_density.1.own_ref.density_ref), channel_id=1, source_target_pairs={{0,1},{1,0},{2,3},{3,2},{4,5},{5,4},{6,7},{7,6},{8,9},{9,8},{10,11... | collective-permute-start | bytes 4718600 | tf_op jit(solution)/shard_map/ppermute | solution.py:40
  2.9 8.3 %collective-permute-start.5 = (s32[16,128]{1,0:T(8,128)S(1)}, s32[16,128]{1,0:T(8,128)S(1)}, u32[]{:S(2)}, u32[]{:S(2)}) collective-permute-start(s32[16,128]{1,0:T(8,128)S(1)} %pad_add_fusion.mine_ref), channel_id=1, source_target_pairs={{0,4},{2,6},{4,0},{6,2},{8,12},{10,14},{12,8},{14,10},{1,5},{3,7},... | collective-permute-start | bytes 24584 | tf_op jit(solution)/shard_map/ppermute | solution.py:36
  5.9 6.3 %collective-permute-start.4 = (s32[16,128]{1,0:T(8,128)S(1)}, s32[16,128]{1,0:T(8,128)S(1)}, u32[]{:S(2)}, u32[]{:S(2)}) collective-permute-start(s32[16,128]{1,0:T(8,128)S(1)} %pad_add_fusion.mine_ref), channel_id=1, source_target_pairs={{0,2},{2,0},{4,6},{6,4},{8,10},{10,8},{12,14},{14,12},{1,3},{3,1},... | collective-permute-start | bytes 24584 | tf_op jit(solution)/shard_map/ppermute | solution.py:36
  7.5 5.4 %collective-permute-start.3 = (s32[16,128]{1,0:T(8,128)S(1)}, s32[16,128]{1,0:T(8,128)S(1)}, u32[]{:S(2)}, u32[]{:S(2)}) collective-permute-start(s32[16,128]{1,0:T(8,128)S(1)} %pad_add_fusion.mine_ref), channel_id=1, source_target_pairs={{0,12},{2,14},{4,8},{6,10},{8,4},{10,6},{12,0},{14,2},{1,13},{3,15... | collective-permute-start | bytes 24584 | tf_op jit(solution)/shard_map/ppermute | solution.py:36
  9.9 6.5 %collective-permute-start.2 = (s32[16,128]{1,0:T(8,128)S(1)}, s32[16,128]{1,0:T(8,128)S(1)}, u32[]{:S(2)}, u32[]{:S(2)}) collective-permute-start(s32[16,128]{1,0:T(8,128)S(1)} %pad_add_fusion.mine_ref), channel_id=1, source_target_pairs={{0,14},{2,4},{4,2},{6,8},{8,6},{10,12},{12,10},{14,0},{1,15},{3,5}... | collective-permute-start | bytes 24584 | tf_op jit(solution)/shard_map/ppermute | solution.py:36
  11.5 9.9 %collective-permute-start.9 = (bf16[2,128,384]{2,1,0:T(8,128)(2,1)S(1)}, bf16[2,128,384]{2,1,0:T(8,128)(2,1)S(1)}, u32[]{:S(2)}, u32[]{:S(2)}) collective-permute-start(bf16[2,128,384]{2,1,0:T(8,128)(2,1)S(1)} %gather_rows.7), channel_id=1, source_target_pairs={{0,4},{2,6},{4,0},{6,2},{8,12},{10,14},{12,8},{14,10},{1,5},{3,7},... | collective-permute-start | bytes 589832 | tf_op jit(solution)/shard_map/ppermute | solution.py:36
  12.4 8.9 %collective-permute-start.8 = (bf16[2,128,384]{2,1,0:T(8,128)(2,1)S(1)}, bf16[2,128,384]{2,1,0:T(8,128)(2,1)S(1)}, u32[]{:S(2)}, u32[]{:S(2)}) collective-permute-start(bf16[2,128,384]{2,1,0:T(8,128)(2,1)S(1)} %gather_rows.6), channel_id=1, source_target_pairs={{0,2},{2,0},{4,6},{6,4},{8,10},{10,8},{12,14},{14,12},{1,3},{3,1},... | collective-permute-start | bytes 589832 | tf_op jit(solution)/shard_map/ppermute | solution.py:36
  13.1 10.1 %collective-permute-start.7 = (bf16[2,128,384]{2,1,0:T(8,128)(2,1)S(1)}, bf16[2,128,384]{2,1,0:T(8,128)(2,1)S(1)}, u32[]{:S(2)}, u32[]{:S(2)}) collective-permute-start(bf16[2,128,384]{2,1,0:T(8,128)(2,1)S(1)} %gather_rows.5), channel_id=1, source_target_pairs={{0,12},{2,14},{4,8},{6,10},{8,4},{10,6},{12,0},{14,2},{1,13},{3,15... | collective-permute-start | bytes 589832 | tf_op jit(solution)/shard_map/ppermute | solution.py:36
  16.7 10.9 %collective-permute-start.6 = (bf16[2,128,384]{2,1,0:T(8,128)(2,1)S(1)}, bf16[2,128,384]{2,1,0:T(8,128)(2,1)S(1)}, u32[]{:S(2)}, u32[]{:S(2)}) collective-permute-start(bf16[2,128,384]{2,1,0:T(8,128)(2,1)S(1)} %gather_rows.4), channel_id=1, source_target_pairs={{0,14},{2,4},{4,2},{6,8},{8,6},{10,12},{12,10},{14,0},{1,15},{3,5}... | collective-permute-start | bytes 589832 | tf_op jit(solution)/shard_map/ppermute | solution.py:36
  27.6 1.4 %collective-permute-start.10 = (bf16[2,128,384]{2,1,0:T(8,128)(2,1)S(1)}, bf16[2,128,384]{2,1,0:T(8,128)(2,1)S(1)}, u32[]{:S(2)}, u32[]{:S(2)}) collective-permute-start(bf16[2,128,384]{2,1,0:T(8,128)(2,1)S(1)} %collective-permute-done.6.refs_0_), channel_id=1, source_target_pairs={{0,1},{1,0},{2,3},{3,2},{4,5},{5,4},{6,7},{7,6},{8,9},{9,8},{10,11... | collective-permute-start | bytes 589832 | tf_op jit(solution)/shard_map/ppermute | solution.py:40
  27.6 1.7 %collective-permute-start.11 = (bf16[2,128,384]{2,1,0:T(8,128)(2,1)S(1)}, bf16[2,128,384]{2,1,0:T(8,128)(2,1)S(1)}, u32[]{:S(2)}, u32[]{:S(2)}) collective-permute-start(bf16[2,128,384]{2,1,0:T(8,128)(2,1)S(1)} %collective-permute-done.7.refs_1_), channel_id=1, source_target_pairs={{0,1},{1,0},{2,3},{3,2},{4,5},{5,4},{6,7},{7,6},{8,9},{9,8},{10,11... | collective-permute-start | bytes 589832 | tf_op jit(solution)/shard_map/ppermute | solution.py:40
  28.1 1.5 %collective-permute-start.12 = (bf16[2,128,384]{2,1,0:T(8,128)(2,1)S(1)}, bf16[2,128,384]{2,1,0:T(8,128)(2,1)S(1)}, u32[]{:S(2)}, u32[]{:S(2)}) collective-permute-start(bf16[2,128,384]{2,1,0:T(8,128)(2,1)S(1)} %collective-permute-done.8.refs_2_), channel_id=1, source_target_pairs={{0,1},{1,0},{2,3},{3,2},{4,5},{5,4},{6,7},{7,6},{8,9},{9,8},{10,11... | collective-permute-start | bytes 589832 | tf_op jit(solution)/shard_map/ppermute | solution.py:40
  28.1 1.8 %collective-permute-start.13 = (bf16[2,128,384]{2,1,0:T(8,128)(2,1)S(1)}, bf16[2,128,384]{2,1,0:T(8,128)(2,1)S(1)}, u32[]{:S(2)}, u32[]{:S(2)}) collective-permute-start(bf16[2,128,384]{2,1,0:T(8,128)(2,1)S(1)} %collective-permute-done.9.refs_3_), channel_id=1, source_target_pairs={{0,1},{1,0},{2,3},{3,2},{4,5},{5,4},{6,7},{7,6},{8,9},{9,8},{10,11... | collective-permute-start | bytes 589832 | tf_op jit(solution)/shard_map/ppermute | solution.py:40
  30.7 12.2 %collective-permute-start.14 = (bf16[2,128,384]{2,1,0:T(8,128)(2,1)S(1)}, bf16[2,128,384]{2,1,0:T(8,128)(2,1)S(1)}, u32[]{:S(2)}, u32[]{:S(2)}) collective-permute-start(bf16[2,128,384]{2,1,0:T(8,128)(2,1)S(1)} %get-tuple-element.38), channel_id=1, source_target_pairs={{0,14},{2,4},{4,2},{6,8},{8,6},{10,12},{12,10},{14,0},{1,15},{3,5}... | collective-permute-start | bytes 589832 | tf_op jit(solution)/shard_map/ppermute | solution.py:36
  32.4 10.5 %collective-permute-start.15 = (bf16[2,128,384]{2,1,0:T(8,128)(2,1)S(1)}, bf16[2,128,384]{2,1,0:T(8,128)(2,1)S(1)}, u32[]{:S(2)}, u32[]{:S(2)}) collective-permute-start(bf16[2,128,384]{2,1,0:T(8,128)(2,1)S(1)} %get-tuple-element.40), channel_id=1, source_target_pairs={{0,12},{2,14},{4,8},{6,10},{8,4},{10,6},{12,0},{14,2},{1,13},{3,15... | collective-permute-start | bytes 589832 | tf_op jit(solution)/shard_map/ppermute | solution.py:36
  33.7 11.0 %collective-permute-start.16 = (bf16[2,128,384]{2,1,0:T(8,128)(2,1)S(1)}, bf16[2,128,384]{2,1,0:T(8,128)(2,1)S(1)}, u32[]{:S(2)}, u32[]{:S(2)}) collective-permute-start(bf16[2,128,384]{2,1,0:T(8,128)(2,1)S(1)} %get-tuple-element.42), channel_id=1, source_target_pairs={{0,2},{2,0},{4,6},{6,4},{8,10},{10,8},{12,14},{14,12},{1,3},{3,1},... | collective-permute-start | bytes 589832 | tf_op jit(solution)/shard_map/ppermute | solution.py:36
  36.9 9.6 %collective-permute-start.17 = (bf16[2,128,384]{2,1,0:T(8,128)(2,1)S(1)}, bf16[2,128,384]{2,1,0:T(8,128)(2,1)S(1)}, u32[]{:S(2)}, u32[]{:S(2)}) collective-permute-start(bf16[2,128,384]{2,1,0:T(8,128)(2,1)S(1)} %get-tuple-element.44), channel_id=1, source_target_pairs={{0,4},{2,6},{4,0},{6,2},{8,12},{10,14},{12,8},{14,10},{1,5},{3,7},... | collective-permute-start | bytes 589832 | tf_op jit(solution)/shard_map/ppermute | solution.py:36
  42.9 3.6 %collective-permute-start.18 = (bf16[2,128,384]{2,1,0:T(8,128)(2,1)S(1)}, bf16[2,128,384]{2,1,0:T(8,128)(2,1)S(1)}, u32[]{:S(2)}, u32[]{:S(2)}) collective-permute-start(bf16[2,128,384]{2,1,0:T(8,128)(2,1)S(1)} %collective-permute-done.14.refs_1_), channel_id=1, source_target_pairs={{0,1},{1,0},{2,3},{3,2},{4,5},{5,4},{6,7},{7,6},{8,9},{9,8},{10,11... | collective-permute-start | bytes 589832 | tf_op jit(solution)/shard_map/ppermute | solution.py:40
  42.9 3.6 %collective-permute-start.19 = (bf16[2,128,384]{2,1,0:T(8,128)(2,1)S(1)}, bf16[2,128,384]{2,1,0:T(8,128)(2,1)S(1)}, u32[]{:S(2)}, u32[]{:S(2)}) collective-permute-start(bf16[2,128,384]{2,1,0:T(8,128)(2,1)S(1)} %collective-permute-done.15.refs_2_), channel_id=1, source_target_pairs={{0,1},{1,0},{2,3},{3,2},{4,5},{5,4},{6,7},{7,6},{8,9},{9,8},{10,11... | collective-permute-start | bytes 589832 | tf_op jit(solution)/shard_map/ppermute | solution.py:40
  44.7 1.7 %collective-permute-start.20 = (bf16[2,128,384]{2,1,0:T(8,128)(2,1)S(1)}, bf16[2,128,384]{2,1,0:T(8,128)(2,1)S(1)}, u32[]{:S(2)}, u32[]{:S(2)}) collective-permute-start(bf16[2,128,384]{2,1,0:T(8,128)(2,1)S(1)} %collective-permute-done.16.refs_3_), channel_id=1, source_target_pairs={{0,1},{1,0},{2,3},{3,2},{4,5},{5,4},{6,7},{7,6},{8,9},{9,8},{10,11... | collective-permute-start | bytes 589832 | tf_op jit(solution)/shard_map/ppermute | solution.py:40
  46.5 1.4 %collective-permute-start.21 = (bf16[2,128,384]{2,1,0:T(8,128)(2,1)S(1)}, bf16[2,128,384]{2,1,0:T(8,128)(2,1)S(1)}, u32[]{:S(2)}, u32[]{:S(2)}) collective-permute-start(bf16[2,128,384]{2,1,0:T(8,128)(2,1)S(1)} %collective-permute-done.17.refs_4_), channel_id=1, source_target_pairs={{0,1},{1,0},{2,3},{3,2},{4,5},{5,4},{6,7},{7,6},{8,9},{9,8},{10,11... | collective-permute-start | bytes 589832 | tf_op jit(solution)/shard_map/ppermute | solution.py:40

commit v7 on v6

--- a/solution.py
+++ b/solution.py
@@ -356,7 +356,7 @@
     pieces = [gather(own, numbers, half) for numbers in near]
     got = [swapped(piece, exchange) for exchange, piece in zip(EXCHANGES, pieces)]
     *indices, table = tables(mine, near, own, other, half)
-    got = [lax.optimization_barrier((piece, table))[0] for piece in got]
+    got[0] = lax.optimization_barrier((got[0], table))[0]
     got += [from_sibling(piece) for piece in got]
     wanted_index, square_index, others_index, cube_index = indices
     wanted, part = [], len(EXCHANGES) // 2

time: 51.8 us -> 51.3 us (level)
  transfers between devices with their start and end apart: 22 -> 22, of which waited for: 13 -> 10; matrix products, arithmetic and copies ran while one was open for 0% -> 0% of each run, Pallas kernels for 15% -> 15%
where the time goes in v7:
time: 51.3 us; the launch traced here: 50.9 us
  starting transfers between devices  21.6 us (42%)
  waiting for transfers between devices  15.3 us (30%)
  Pallas kernels  11.8 us (23%)
  local copies, waits for them, and re-layouts  1.41 us (3%)
  other arithmetic  0.71 us (1%)
    ppermute x12, starting transfers between devices, swapped(): return lax.ppermute(value, 'rows', pairs)  19.9 us
    ppermute x12, waiting for transfers between devices, swapped(): return lax.ppermute(value, 'rows', pairs)  12.4 us
    pallas_call x1, Pallas kernels, square(): pl.pallas_call(functools.partial(square_kernel, half), out_shape=like(tab...  5.25 us
    pallas_call x1, Pallas kernels, cube(): pl.pallas_call(functools.partial(cube_kernel, half), out_shape=[like(own)...  3.26 us
    ppermute x10, waiting for transfers between devices, from_sibling(): return lax.ppermute(value, 'layers', [(0, 1), (1, 0)])  2.86 us
    ppermute x10, starting transfers between devices, from_sibling(): return lax.ppermute(value, 'layers', [(0, 1), (1, 0)])  1.69 us
    pallas_call x2, Pallas kernels, square_wanted(): pl.pallas_call(functools.partial(wanted_kernel, half, first, len(pieces))...  1.58 us
    unnamed x2, local copies, waits for them, and re-layouts  1.41 us
  transfers between devices with their start and end apart: 22, of which 10 were waited for; matrix products, arithmetic and copies ran while one was open for 0% of the time, Pallas kernels for 15%

profile of v7, /device:TPU:0, one launch (start us, length us, event | category | flops | bytes accessed | tf_op | source)
XLA Modules:
  0.0 50.9 jit_solution(3367171751530691838)
XLA Ops:
  0.0 0.7 %add_bitcast_fusion = s32[6,16]{1,0:T(8,128)S(1)} fusion(s32[16,3]{0,1:T(4,128)} %param.5, s32[16,3]{0,1:T(4,128)} %param.4), kind=kLoop, calls=%fused_computation.1 | loop fusion | flops 96 | bytes 768 | tf_op jit(solution)/shard_map/transpose | solution.py:63
  0.7 0.5 %collective-permute-start = (s32[8,128]{1,0:T(8,128)S(1)}, s32[8,128]{1,0:T(8,128)S(1)}, u32[]{:S(2)}, u32[]{:S(2)}) collective-permute-start(s32[8,128]{1,0:T(8,128)S(1)} %pad.4), channel_id=1, source_target_pairs={{0,1},{1,0},{2,3},{3,2},{4,5},{5,4},{6,7},{7,6},{8,9},{9,8},{10,11... | collective-permute-start | bytes 12296 | tf_op jit(solution)/shard_map/ppermute | solution.py:40
  1.2 1.4 %copy-done = bf16[16,128,384]{2,1,0:T(8,128)(2,1)S(1)} copy-done((bf16[16,128,384]{2,1,0:T(8,128)(2,1)S(1)}, bf16[16,128,384]{2,1,0:T(8,128)(2,1)}, u32[]{:S(2)}) %copy-start) | copy-done | bytes 1572888
  2.9 3.0 %collective-permute-start.5 = (s32[16,128]{1,0:T(8,128)S(1)}, s32[16,128]{1,0:T(8,128)S(1)}, u32[]{:S(2)}, u32[]{:S(2)}) collective-permute-start(s32[16,128]{1,0:T(8,128)S(1)} %pad_add_fusion.mine_ref), channel_id=1, source_target_pairs={{0,4},{2,6},{4,0},{6,2},{8,12},{10,14},{12,8},{14,10},{1,5},{3,7},... | collective-permute-start | bytes 24584 | tf_op jit(solution)/shard_map/ppermute | solution.py:36
  5.9 1.5 %collective-permute-start.4 = (s32[16,128]{1,0:T(8,128)S(1)}, s32[16,128]{1,0:T(8,128)S(1)}, u32[]{:S(2)}, u32[]{:S(2)}) collective-permute-start(s32[16,128]{1,0:T(8,128)S(1)} %pad_add_fusion.mine_ref), channel_id=1, source_target_pairs={{0,2},{2,0},{4,6},{6,4},{8,10},{10,8},{12,14},{14,12},{1,3},{3,1},... | collective-permute-start | bytes 24584 | tf_op jit(solution)/shard_map/ppermute | solution.py:36
  7.5 2.5 %collective-permute-start.3 = (s32[16,128]{1,0:T(8,128)S(1)}, s32[16,128]{1,0:T(8,128)S(1)}, u32[]{:S(2)}, u32[]{:S(2)}) collective-permute-start(s32[16,128]{1,0:T(8,128)S(1)} %pad_add_fusion.mine_ref), channel_id=1, source_target_pairs={{0,12},{2,14},{4,8},{6,10},{8,4},{10,6},{12,0},{14,2},{1,13},{3,15... | collective-permute-start | bytes 24584 | tf_op jit(solution)/shard_map/ppermute | solution.py:36
  9.9 1.3 %collective-permute-start.2 = (s32[16,128]{1,0:T(8,128)S(1)}, s32[16,128]{1,0:T(8,128)S(1)}, u32[]{:S(2)}, u32[]{:S(2)}) collective-permute-start(s32[16,128]{1,0:T(8,128)S(1)} %pad_add_fusion.mine_ref), channel_id=1, source_target_pairs={{0,14},{2,4},{4,2},{6,8},{8,6},{10,12},{12,10},{14,0},{1,15},{3,5}... | collective-permute-start | bytes 24584 | tf_op jit(solution)/shard_map/ppermute | solution.py:36
  11.2 0.2 gather_rows.7
  11.5 0.7 %collective-permute-start.9 = (bf16[2,128,384]{2,1,0:T(8,128)(2,1)S(1)}, bf16[2,128,384]{2,1,0:T(8,128)(2,1)S(1)}, u32[]{:S(2)}, u32[]{:S(2)}) collective-permute-start(bf16[2,128,384]{2,1,0:T(8,128)(2,1)S(1)} %gather_rows.7), channel_id=1, source_target_pairs={{0,4},{2,6},{4,0},{6,2},{8,12},{10,14},{12,8},{14,10},{1,5},{3,7},... | collective-permute-start | bytes 589832 | tf_op jit(solution)/shard_map/ppermute | solution.py:36
  12.4 0.3 collective-permute-start.8
  13.1 3.0 %collective-permute-start.7 = (bf16[2,128,384]{2,1,0:T(8,128)(2,1)S(1)}, bf16[2,128,384]{2,1,0:T(8,128)(2,1)S(1)}, u32[]{:S(2)}, u32[]{:S(2)}) collective-permute-start(bf16[2,128,384]{2,1,0:T(8,128)(2,1)S(1)} %gather_rows.5), channel_id=1, source_target_pairs={{0,12},{2,14},{4,8},{6,10},{8,4},{10,6},{12,0},{14,2},{1,13},{3,15... | collective-permute-start | bytes 589832 | tf_op jit(solution)/shard_map/ppermute | solution.py:36
  16.1 0.3 collective-permute-done.2.refs_0_.numbers_ref
  16.7 1.7 %collective-permute-start.6 = (bf16[2,128,384]{2,1,0:T(8,128)(2,1)S(1)}, bf16[2,128,384]{2,1,0:T(8,128)(2,1)S(1)}, u32[]{:S(2)}, u32[]{:S(2)}) collective-permute-start(bf16[2,128,384]{2,1,0:T(8,128)(2,1)S(1)} %gather_rows.4), channel_id=1, source_target_pairs={{0,14},{2,4},{4,2},{6,8},{8,6},{10,12},{12,10},{14,0},{1,15},{3,5}... | collective-permute-start | bytes 589832 | tf_op jit(solution)/shard_map/ppermute | solution.py:36
  18.4 3.0 %collective-permute-done.9.refs_3_ = bf16[2,128,384]{2,1,0:T(8,128)(2,1)S(1)} collective-permute-done((bf16[2,128,384]{2,1,0:T(8,128)(2,1)S(1)}, bf16[2,128,384]{2,1,0:T(8,128)(2,1)S(1)}, u32[]{:S(2)}, u32[]{:S(2)}) %collective-permute-start.9) | collective-permute-done | bytes 196640 | tf_op jit(solution)/shard_map/ppermute | solution.py:36
  21.4 0.5 collective-permute-start.12
  21.9 1.4 %collective-permute-done.7.refs_1_ = bf16[2,128,384]{2,1,0:T(8,128)(2,1)S(1)} collective-permute-done((bf16[2,128,384]{2,1,0:T(8,128)(2,1)S(1)}, bf16[2,128,384]{2,1,0:T(8,128)(2,1)S(1)}, u32[]{:S(2)}, u32[]{:S(2)}) %collective-permute-start.7) | collective-permute-done | bytes 196640 | tf_op jit(solution)/shard_map/ppermute | solution.py:36
  23.2 0.7 %block_tables.1 = (s32[24,128]{1,0:T(8,128)S(1)}, s32[24,128]{1,0:T(8,128)S(1)}, s32[24,128]{1,0:T(8,128)S(1)}, s32[24,128]{1,0:T(8,128)S(1)}, bf16[49,128,384]{2,1,0:T(8,128)(2,1)S(1)}) custom-call(s32[16,128]{1,0:T(8,128)S(1)} %pad_add_fusion.mine_ref, bf16[16,128,384]{2,1,0:T(8,128)(2,1)S(1)} %stage_density.1.own_ref.density_ref, ...), custom_call_target="tpu_custom_call" | custom-call | bytes 6291456 | tf_op jit(solution)/shard_map/block_tables/pallas_call | solution.py:206
  23.9 3.7 %collective-permute-done.6.refs_0_ = bf16[2,128,384]{2,1,0:T(8,128)(2,1)S(1)} collective-permute-done((bf16[2,128,384]{2,1,0:T(8,128)(2,1)S(1)}, bf16[2,128,384]{2,1,0:T(8,128)(2,1)S(1)}, u32[]{:S(2)}, u32[]{:S(2)}) %collective-permute-start.6) | collective-permute-done | bytes 196640 | tf_op jit(solution)/shard_map/ppermute | solution.py:36
  27.6 1.4 %collective-permute-done.10.refs_4_ = bf16[2,128,384]{2,1,0:T(8,128)(2,1)S(1)} collective-permute-done((bf16[2,128,384]{2,1,0:T(8,128)(2,1)S(1)}, bf16[2,128,384]{2,1,0:T(8,128)(2,1)S(1)}, u32[]{:S(2)}, u32[]{:S(2)}) %collective-permute-start.10) | collective-permute-done | bytes 196640 | tf_op jit(solution)/shard_map/ppermute | solution.py:40
  29.0 0.8 %square_wanted.2 = (bf16[2,128,384]{2,1,0:T(8,128)(2,1)S(1)}, bf16[2,128,384]{2,1,0:T(8,128)(2,1)S(1)}, bf16[49,128,384]{2,1,0:T(8,128)(2,1)S(1)}) custom-call(s32[24,128]{1,0:T(8,128)S(1)} %get-tuple-element.28.index_ref, bf16[16,128,384]{2,1,0:T(8,128)(2,1)S(1)} %stage_density.1.own_ref.density_ref, ...), custom_call_target="tpu_custom_call", output_to_operand_aliasing={{2}: (3, {})} | custom-call | flops 301989888 | bytes 12582912 | tf_op jit(solution)/shard_map/square_wanted/pallas_call | solution.py:275
  29.8 1.7 %collective-permute-start.14 = (bf16[2,128,384]{2,1,0:T(8,128)(2,1)S(1)}, bf16[2,128,384]{2,1,0:T(8,128)(2,1)S(1)}, u32[]{:S(2)}, u32[]{:S(2)}) collective-permute-start(bf16[2,128,384]{2,1,0:T(8,128)(2,1)S(1)} %get-tuple-element.32), channel_id=1, source_target_pairs={{0,14},{2,4},{4,2},{6,8},{8,6},{10,12},{12,10},{14,0},{1,15},{3,5}... | collective-permute-start | bytes 589832 | tf_op jit(solution)/shard_map/ppermute | solution.py:36
  31.6 1.4 %collective-permute-start.15 = (bf16[2,128,384]{2,1,0:T(8,128)(2,1)S(1)}, bf16[2,128,384]{2,1,0:T(8,128)(2,1)S(1)}, u32[]{:S(2)}, u32[]{:S(2)}) collective-permute-start(bf16[2,128,384]{2,1,0:T(8,128)(2,1)S(1)} %get-tuple-element.34), channel_id=1, source_target_pairs={{0,12},{2,14},{4,8},{6,10},{8,4},{10,6},{12,0},{14,2},{1,13},{3,15... | collective-permute-start | bytes 589832 | tf_op jit(solution)/shard_map/ppermute | solution.py:36
  33.0 0.8 %square_wanted.3 = (bf16[2,128,384]{2,1,0:T(8,128)(2,1)S(1)}, bf16[2,128,384]{2,1,0:T(8,128)(2,1)S(1)}) custom-call(s32[24,128]{1,0:T(8,128)S(1)} %get-tuple-element.28.index_ref, bf16[16,128,384]{2,1,0:T(8,128)(2,1)S(1)} %stage_density.1.own_ref.density_ref, bf16[16,128,384]{2,1,0:T(8,128)(2,1)S(1)} %collective-permute-done.1.other_ref, ...), custom_call_target="tpu_custom_call" | custom-call | flops 301989888 | bytes 12582912 | tf_op jit(solution)/shard_map/square_wanted/pallas_call | solution.py:275
  33.8 2.3 %collective-permute-start.16 = (bf16[2,128,384]{2,1,0:T(8,128)(2,1)S(1)}, bf16[2,128,384]{2,1,0:T(8,128)(2,1)S(1)}, u32[]{:S(2)}, u32[]{:S(2)}) collective-permute-start(bf16[2,128,384]{2,1,0:T(8,128)(2,1)S(1)} %get-tuple-element.36), channel_id=1, source_target_pairs={{0,2},{2,0},{4,6},{6,4},{8,10},{10,8},{12,14},{14,12},{1,3},{3,1},... | collective-permute-start | bytes 589832 | tf_op jit(solution)/shard_map/ppermute | solution.py:36
  36.1 0.4 collective-permute-start.17
  36.4 5.2 %square_rows.1.refs_0_ = bf16[49,128,384]{2,1,0:T(8,128)(2,1)S(1)} custom-call(s32[24,128]{1,0:T(8,128)S(1)} %get-tuple-element.26.index_ref, s32[24,128]{1,0:T(8,128)S(1)} %get-tuple-element.27.others_ref, bf16[16,128,384]{2,1,0:T(8,128)(2,1)S(1)} %stage_density.1.own_ref.density_ref, bf16[16,128,384]{2,1,0:T(8,128)(2,1)S(1)} %collective-permute-done.1.other_ref, ...), custom_call_target="tpu_custom_call" | custom-call | flops 2415919104 | bytes 12582912 | tf_op jit(solution)/shard_map/square_rows/pallas_call | solution.py:303
  41.7 1.3 %collective-permute-done.15.refs_2_ = bf16[2,128,384]{2,1,0:T(8,128)(2,1)S(1)} collective-permute-done((bf16[2,128,384]{2,1,0:T(8,128)(2,1)S(1)}, bf16[2,128,384]{2,1,0:T(8,128)(2,1)S(1)}, u32[]{:S(2)}, u32[]{:S(2)}) %collective-permute-start.15) | collective-permute-done | bytes 196640 | tf_op jit(solution)/shard_map/ppermute | solution.py:36
  43.0 0.5 collective-permute-start.19
  43.5 0.3 collective-permute-done.16.refs_3_
  43.8 2.4 %collective-permute-done.17.refs_4_ = bf16[2,128,384]{2,1,0:T(8,128)(2,1)S(1)} collective-permute-done((bf16[2,128,384]{2,1,0:T(8,128)(2,1)S(1)}, bf16[2,128,384]{2,1,0:T(8,128)(2,1)S(1)}, u32[]{:S(2)}, u32[]{:S(2)}) %collective-permute-start.17) | collective-permute-done | bytes 196640 | tf_op jit(solution)/shard_map/ppermute | solution.py:36
  46.2 1.4 %collective-permute-done.21.refs_8_ = bf16[2,128,384]{2,1,0:T(8,128)(2,1)S(1)} collective-permute-done((bf16[2,128,384]{2,1,0:T(8,128)(2,1)S(1)}, bf16[2,128,384]{2,1,0:T(8,128)(2,1)S(1)}, u32[]{:S(2)}, u32[]{:S(2)}) %collective-permute-start.21) | collective-permute-done | bytes 196640 | tf_op jit(solution)/shard_map/ppermute | solution.py:40
  47.6 3.3 %cube_rows.1 = (bf16[16,128,384]{2,1,0:T(8,128)(2,1)}, bf16[49,128,384]{2,1,0:T(8,128)(2,1)S(1)}) custom-call(s32[24,128]{1,0:T(8,128)S(1)} %get-tuple-element.25.index_ref, bf16[16,128,384]{2,1,0:T(8,128)(2,1)S(1)} %stage_density.1.own_ref.density_ref, bf16[16,128,384]{2,1,0:T(8,128)(2,1)S(1)} %collective-permute-done.1.other_ref, ...), custom_call_target="tpu_custom_call", output_to_operand_aliasing={{1}: (3, {})} | custom-call | flops 1207959552 | bytes 12582912 | tf_op jit(solution)/shard_map/cube_rows/pallas_call | solution.py:333
  (27 shorter events, 1.2 us)
Async XLA Ops:
  0.7 2.1 %collective-permute-start = (s32[8,128]{1,0:T(8,128)S(1)}, s32[8,128]{1,0:T(8,128)S(1)}, u32[]{:S(2)}, u32[]{:S(2)}) collective-permute-start(s32[8,128]{1,0:T(8,128)S(1)} %pad.4), channel_id=1, source_target_pairs={{0,1},{1,0},{2,3},{3,2},{4,5},{5,4},{6,7},{7,6},{8,9},{9,8},{10,11... | collective-permute-start | bytes 12296 | tf_op jit(solution)/shard_map/ppermute | solution.py:40
  1.2 1.4 %copy-start = (bf16[16,128,384]{2,1,0:T(8,128)(2,1)S(1)}, bf16[16,128,384]{2,1,0:T(8,128)(2,1)}, u32[]{:S(2)}) copy-start(bf16[16,128,384]{2,1,0:T(8,128)(2,1)} %density_ref.1) | copy-start | bytes 4718596
  2.8 20.4 %collective-permute-start.1 = (bf16[16,128,384]{2,1,0:T(8,128)(2,1)S(1)}, bf16[16,128,384]{2,1,0:T(8,128)(2,1)S(1)}, u32[]{:S(2)}, u32[]{:S(2)}) collective-permute-start(bf16[16,128,384]{2,1,0:T(8,128)(2,1)S(1)} %stage_density.1.own_ref.density_ref), channel_id=1, source_target_pairs={{0,1},{1,0},{2,3},{3,2},{4,5},{5,4},{6,7},{7,6},{8,9},{9,8},{10,11... | collective-permute-start | bytes 4718600 | tf_op jit(solution)/shard_map/ppermute | solution.py:40
  2.9 8.3 %collective-permute-start.5 = (s32[16,128]{1,0:T(8,128)S(1)}, s32[16,128]{1,0:T(8,128)S(1)}, u32[]{:S(2)}, u32[]{:S(2)}) collective-permute-start(s32[16,128]{1,0:T(8,128)S(1)} %pad_add_fusion.mine_ref), channel_id=1, source_target_pairs={{0,4},{2,6},{4,0},{6,2},{8,12},{10,14},{12,8},{14,10},{1,5},{3,7},... | collective-permute-start | bytes 24584 | tf_op jit(solution)/shard_map/ppermute | solution.py:36
  5.9 6.3 %collective-permute-start.4 = (s32[16,128]{1,0:T(8,128)S(1)}, s32[16,128]{1,0:T(8,128)S(1)}, u32[]{:S(2)}, u32[]{:S(2)}) collective-permute-start(s32[16,128]{1,0:T(8,128)S(1)} %pad_add_fusion.mine_ref), channel_id=1, source_target_pairs={{0,2},{2,0},{4,6},{6,4},{8,10},{10,8},{12,14},{14,12},{1,3},{3,1},... | collective-permute-start | bytes 24584 | tf_op jit(solution)/shard_map/ppermute | solution.py:36
  7.5 5.4 %collective-permute-start.3 = (s32[16,128]{1,0:T(8,128)S(1)}, s32[16,128]{1,0:T(8,128)S(1)}, u32[]{:S(2)}, u32[]{:S(2)}) collective-permute-start(s32[16,128]{1,0:T(8,128)S(1)} %pad_add_fusion.mine_ref), channel_id=1, source_target_pairs={{0,12},{2,14},{4,8},{6,10},{8,4},{10,6},{12,0},{14,2},{1,13},{3,15... | collective-permute-start | bytes 24584 | tf_op jit(solution)/shard_map/ppermute | solution.py:36
  9.9 6.5 %collective-permute-start.2 = (s32[16,128]{1,0:T(8,128)S(1)}, s32[16,128]{1,0:T(8,128)S(1)}, u32[]{:S(2)}, u32[]{:S(2)}) collective-permute-start(s32[16,128]{1,0:T(8,128)S(1)} %pad_add_fusion.mine_ref), channel_id=1, source_target_pairs={{0,14},{2,4},{4,2},{6,8},{8,6},{10,12},{12,10},{14,0},{1,15},{3,5}... | collective-permute-start | bytes 24584 | tf_op jit(solution)/shard_map/ppermute | solution.py:36
  11.5 9.9 %collective-permute-start.9 = (bf16[2,128,384]{2,1,0:T(8,128)(2,1)S(1)}, bf16[2,128,384]{2,1,0:T(8,128)(2,1)S(1)}, u32[]{:S(2)}, u32[]{:S(2)}) collective-permute-start(bf16[2,128,384]{2,1,0:T(8,128)(2,1)S(1)} %gather_rows.7), channel_id=1, source_target_pairs={{0,4},{2,6},{4,0},{6,2},{8,12},{10,14},{12,8},{14,10},{1,5},{3,7},... | collective-permute-start | bytes 589832 | tf_op jit(solution)/shard_map/ppermute | solution.py:36
  12.4 8.9 %collective-permute-start.8 = (bf16[2,128,384]{2,1,0:T(8,128)(2,1)S(1)}, bf16[2,128,384]{2,1,0:T(8,128)(2,1)S(1)}, u32[]{:S(2)}, u32[]{:S(2)}) collective-permute-start(bf16[2,128,384]{2,1,0:T(8,128)(2,1)S(1)} %gather_rows.6), channel_id=1, source_target_pairs={{0,2},{2,0},{4,6},{6,4},{8,10},{10,8},{12,14},{14,12},{1,3},{3,1},... | collective-permute-start | bytes 589832 | tf_op jit(solution)/shard_map/ppermute | solution.py:36
  13.1 10.1 %collective-permute-start.7 = (bf16[2,128,384]{2,1,0:T(8,128)(2,1)S(1)}, bf16[2,128,384]{2,1,0:T(8,128)(2,1)S(1)}, u32[]{:S(2)}, u32[]{:S(2)}) collective-permute-start(bf16[2,128,384]{2,1,0:T(8,128)(2,1)S(1)} %gather_rows.5), channel_id=1, source_target_pairs={{0,12},{2,14},{4,8},{6,10},{8,4},{10,6},{12,0},{14,2},{1,13},{3,15... | collective-permute-start | bytes 589832 | tf_op jit(solution)/shard_map/ppermute | solution.py:36
  16.7 10.9 %collective-permute-start.6 = (bf16[2,128,384]{2,1,0:T(8,128)(2,1)S(1)}, bf16[2,128,384]{2,1,0:T(8,128)(2,1)S(1)}, u32[]{:S(2)}, u32[]{:S(2)}) collective-permute-start(bf16[2,128,384]{2,1,0:T(8,128)(2,1)S(1)} %gather_rows.4), channel_id=1, source_target_pairs={{0,14},{2,4},{4,2},{6,8},{8,6},{10,12},{12,10},{14,0},{1,15},{3,5}... | collective-permute-start | bytes 589832 | tf_op jit(solution)/shard_map/ppermute | solution.py:36
  21.3 6.3 %collective-permute-start.13 = (bf16[2,128,384]{2,1,0:T(8,128)(2,1)S(1)}, bf16[2,128,384]{2,1,0:T(8,128)(2,1)S(1)}, u32[]{:S(2)}, u32[]{:S(2)}) collective-permute-start(bf16[2,128,384]{2,1,0:T(8,128)(2,1)S(1)} %collective-permute-done.9.refs_3_), channel_id=1, source_target_pairs={{0,1},{1,0},{2,3},{3,2},{4,5},{5,4},{6,7},{7,6},{8,9},{9,8},{10,11... | collective-permute-start | bytes 589832 | tf_op jit(solution)/shard_map/ppermute | solution.py:40
  21.4 6.3 %collective-permute-start.12 = (bf16[2,128,384]{2,1,0:T(8,128)(2,1)S(1)}, bf16[2,128,384]{2,1,0:T(8,128)(2,1)S(1)}, u32[]{:S(2)}, u32[]{:S(2)}) collective-permute-start(bf16[2,128,384]{2,1,0:T(8,128)(2,1)S(1)} %collective-permute-done.8.refs_2_), channel_id=1, source_target_pairs={{0,1},{1,0},{2,3},{3,2},{4,5},{5,4},{6,7},{7,6},{8,9},{9,8},{10,11... | collective-permute-start | bytes 589832 | tf_op jit(solution)/shard_map/ppermute | solution.py:40
  23.2 4.4 %collective-permute-start.11 = (bf16[2,128,384]{2,1,0:T(8,128)(2,1)S(1)}, bf16[2,128,384]{2,1,0:T(8,128)(2,1)S(1)}, u32[]{:S(2)}, u32[]{:S(2)}) collective-permute-start(bf16[2,128,384]{2,1,0:T(8,128)(2,1)S(1)} %collective-permute-done.7.refs_1_), channel_id=1, source_target_pairs={{0,1},{1,0},{2,3},{3,2},{4,5},{5,4},{6,7},{7,6},{8,9},{9,8},{10,11... | collective-permute-start | bytes 589832 | tf_op jit(solution)/shard_map/ppermute | solution.py:40
  27.6 1.4 %collective-permute-start.10 = (bf16[2,128,384]{2,1,0:T(8,128)(2,1)S(1)}, bf16[2,128,384]{2,1,0:T(8,128)(2,1)S(1)}, u32[]{:S(2)}, u32[]{:S(2)}) collective-permute-start(bf16[2,128,384]{2,1,0:T(8,128)(2,1)S(1)} %collective-permute-done.6.refs_0_), channel_id=1, source_target_pairs={{0,1},{1,0},{2,3},{3,2},{4,5},{5,4},{6,7},{7,6},{8,9},{9,8},{10,11... | collective-permute-start | bytes 589832 | tf_op jit(solution)/shard_map/ppermute | solution.py:40
  29.8 13.1 %collective-permute-start.14 = (bf16[2,128,384]{2,1,0:T(8,128)(2,1)S(1)}, bf16[2,128,384]{2,1,0:T(8,128)(2,1)S(1)}, u32[]{:S(2)}, u32[]{:S(2)}) collective-permute-start(bf16[2,128,384]{2,1,0:T(8,128)(2,1)S(1)} %get-tuple-element.32), channel_id=1, source_target_pairs={{0,14},{2,4},{4,2},{6,8},{8,6},{10,12},{12,10},{14,0},{1,15},{3,5}... | collective-permute-start | bytes 589832 | tf_op jit(solution)/shard_map/ppermute | solution.py:36
  31.6 11.4 %collective-permute-start.15 = (bf16[2,128,384]{2,1,0:T(8,128)(2,1)S(1)}, bf16[2,128,384]{2,1,0:T(8,128)(2,1)S(1)}, u32[]{:S(2)}, u32[]{:S(2)}) collective-permute-start(bf16[2,128,384]{2,1,0:T(8,128)(2,1)S(1)} %get-tuple-element.34), channel_id=1, source_target_pairs={{0,12},{2,14},{4,8},{6,10},{8,4},{10,6},{12,0},{14,2},{1,13},{3,15... | collective-permute-start | bytes 589832 | tf_op jit(solution)/shard_map/ppermute | solution.py:36
  33.8 10.0 %collective-permute-start.16 = (bf16[2,128,384]{2,1,0:T(8,128)(2,1)S(1)}, bf16[2,128,384]{2,1,0:T(8,128)(2,1)S(1)}, u32[]{:S(2)}, u32[]{:S(2)}) collective-permute-start(bf16[2,128,384]{2,1,0:T(8,128)(2,1)S(1)} %get-tuple-element.36), channel_id=1, source_target_pairs={{0,2},{2,0},{4,6},{6,4},{8,10},{10,8},{12,14},{14,12},{1,3},{3,1},... | collective-permute-start | bytes 589832 | tf_op jit(solution)/shard_map/ppermute | solution.py:36
  36.1 10.1 %collective-permute-start.17 = (bf16[2,128,384]{2,1,0:T(8,128)(2,1)S(1)}, bf16[2,128,384]{2,1,0:T(8,128)(2,1)S(1)}, u32[]{:S(2)}, u32[]{:S(2)}) collective-permute-start(bf16[2,128,384]{2,1,0:T(8,128)(2,1)S(1)} %get-tuple-element.38), channel_id=1, source_target_pairs={{0,4},{2,6},{4,0},{6,2},{8,12},{10,14},{12,8},{14,10},{1,5},{3,7},... | collective-permute-start | bytes 589832 | tf_op jit(solution)/shard_map/ppermute | solution.py:36
  43.0 3.2 %collective-permute-start.18 = (bf16[2,128,384]{2,1,0:T(8,128)(2,1)S(1)}, bf16[2,128,384]{2,1,0:T(8,128)(2,1)S(1)}, u32[]{:S(2)}, u32[]{:S(2)}) collective-permute-start(bf16[2,128,384]{2,1,0:T(8,128)(2,1)S(1)} %collective-permute-done.14.refs_1_), channel_id=1, source_target_pairs={{0,1},{1,0},{2,3},{3,2},{4,5},{5,4},{6,7},{7,6},{8,9},{9,8},{10,11... | collective-permute-start | bytes 589832 | tf_op jit(solution)/shard_map/ppermute | solution.py:40
  43.0 3.2 %collective-permute-start.19 = (bf16[2,128,384]{2,1,0:T(8,128)(2,1)S(1)}, bf16[2,128,384]{2,1,0:T(8,128)(2,1)S(1)}, u32[]{:S(2)}, u32[]{:S(2)}) collective-permute-start(bf16[2,128,384]{2,1,0:T(8,128)(2,1)S(1)} %collective-permute-done.15.refs_2_), channel_id=1, source_target_pairs={{0,1},{1,0},{2,3},{3,2},{4,5},{5,4},{6,7},{7,6},{8,9},{9,8},{10,11... | collective-permute-start | bytes 589832 | tf_op jit(solution)/shard_map/ppermute | solution.py:40
  43.8 2.4 %collective-permute-start.20 = (bf16[2,128,384]{2,1,0:T(8,128)(2,1)S(1)}, bf16[2,128,384]{2,1,0:T(8,128)(2,1)S(1)}, u32[]{:S(2)}, u32[]{:S(2)}) collective-permute-start(bf16[2,128,384]{2,1,0:T(8,128)(2,1)S(1)} %collective-permute-done.16.refs_3_), channel_id=1, source_target_pairs={{0,1},{1,0},{2,3},{3,2},{4,5},{5,4},{6,7},{7,6},{8,9},{9,8},{10,11... | collective-permute-start | bytes 589832 | tf_op jit(solution)/shard_map/ppermute | solution.py:40
  46.2 1.4 %collective-permute-start.21 = (bf16[2,128,384]{2,1,0:T(8,128)(2,1)S(1)}, bf16[2,128,384]{2,1,0:T(8,128)(2,1)S(1)}, u32[]{:S(2)}, u32[]{:S(2)}) collective-permute-start(bf16[2,128,384]{2,1,0:T(8,128)(2,1)S(1)} %collective-permute-done.17.refs_4_), channel_id=1, source_target_pairs={{0,1},{1,0},{2,3},{3,2},{4,5},{5,4},{6,7},{7,6},{8,9},{9,8},{10,11... | collective-permute-start | bytes 589832 | tf_op jit(solution)/shard_map/ppermute | solution.py:40

commit v8 on v7

--- a/solution.py
+++ b/solution.py
@@ -359,8 +359,8 @@
     got[0] = lax.optimization_barrier((got[0], table))[0]
     got += [from_sibling(piece) for piece in got]
     wanted_index, square_index, others_index, cube_index = indices
-    wanted, part = [], len(EXCHANGES) // 2
-    for first in range(0, len(EXCHANGES), part):
+    wanted = []
+    for first, part in ((0, 1), (1, len(EXCHANGES) - 1)):
         more, table = square_wanted(
             wanted_index, own, other, table, [] if first else got, half, first, part
         )

time: 51.3 us -> 51 us (level)
  transfers between devices with their start and end apart: 22 -> 22, of which waited for: 10 -> 10; matrix products, arithmetic and copies ran while one was open for 0% -> 0% of each run, Pallas kernels for 15% -> 16%
where the time goes in v8:
time: 51 us; the launch traced here: 50.8 us
  starting transfers between devices  21.2 us (42%)
  waiting for transfers between devices  15.6 us (31%)
  Pallas kernels  11.8 us (23%)
  local copies, waits for them, and re-layouts  1.41 us (3%)
  other arithmetic  0.71 us (1%)
    ppermute x12, starting transfers between devices, swapped(): return lax.ppermute(value, 'rows', pairs)  19.9 us
    ppermute x12, waiting for transfers between devices, swapped(): return lax.ppermute(value, 'rows', pairs)  12.7 us
    pallas_call x1, Pallas kernels, square(): pl.pallas_call(functools.partial(square_kernel, half), out_shape=like(tab...  5.23 us
    pallas_call x1, Pallas kernels, cube(): pl.pallas_call(functools.partial(cube_kernel, half), out_shape=[like(own)...  3.26 us
    ppermute x10, waiting for transfers between devices, from_sibling(): return lax.ppermute(value, 'layers', [(0, 1), (1, 0)])  2.86 us
    pallas_call x2, Pallas kernels, square_wanted(): pl.pallas_call(functools.partial(wanted_kernel, half, first, len(pieces))...  1.58 us
    unnamed x2, local copies, waits for them, and re-layouts  1.41 us
    ppermute x10, starting transfers between devices, from_sibling(): return lax.ppermute(value, 'layers', [(0, 1), (1, 0)])  1.25 us
  transfers between devices with their start and end apart: 22, of which 10 were waited for; matrix products, arithmetic and copies ran while one was open for 0% of the time, Pallas kernels for 16%

profile of v8, /device:TPU:0, one launch (start us, length us, event | category | flops | bytes accessed | tf_op | source)
XLA Modules:
  0.0 50.8 jit_solution(7811218808833476728)
XLA Ops:
  0.0 0.7 %add_bitcast_fusion = s32[6,16]{1,0:T(8,128)S(1)} fusion(s32[16,3]{0,1:T(4,128)} %param.5, s32[16,3]{0,1:T(4,128)} %param.4), kind=kLoop, calls=%fused_computation.1 | loop fusion | flops 96 | bytes 768 | tf_op jit(solution)/shard_map/transpose | solution.py:63
  0.7 0.5 %collective-permute-start = (s32[8,128]{1,0:T(8,128)S(1)}, s32[8,128]{1,0:T(8,128)S(1)}, u32[]{:S(2)}, u32[]{:S(2)}) collective-permute-start(s32[8,128]{1,0:T(8,128)S(1)} %pad.4), channel_id=1, source_target_pairs={{0,1},{1,0},{2,3},{3,2},{4,5},{5,4},{6,7},{7,6},{8,9},{9,8},{10,11... | collective-permute-start | bytes 12296 | tf_op jit(solution)/shard_map/ppermute | solution.py:40
  1.2 1.4 %copy-done = bf16[16,128,384]{2,1,0:T(8,128)(2,1)S(1)} copy-done((bf16[16,128,384]{2,1,0:T(8,128)(2,1)S(1)}, bf16[16,128,384]{2,1,0:T(8,128)(2,1)}, u32[]{:S(2)}) %copy-start) | copy-done | bytes 1572888
  2.9 3.0 %collective-permute-start.5 = (s32[16,128]{1,0:T(8,128)S(1)}, s32[16,128]{1,0:T(8,128)S(1)}, u32[]{:S(2)}, u32[]{:S(2)}) collective-permute-start(s32[16,128]{1,0:T(8,128)S(1)} %pad_add_fusion.mine_ref), channel_id=1, source_target_pairs={{0,4},{2,6},{4,0},{6,2},{8,12},{10,14},{12,8},{14,10},{1,5},{3,7},... | collective-permute-start | bytes 24584 | tf_op jit(solution)/shard_map/ppermute | solution.py:36
  5.9 1.5 %collective-permute-start.4 = (s32[16,128]{1,0:T(8,128)S(1)}, s32[16,128]{1,0:T(8,128)S(1)}, u32[]{:S(2)}, u32[]{:S(2)}) collective-permute-start(s32[16,128]{1,0:T(8,128)S(1)} %pad_add_fusion.mine_ref), channel_id=1, source_target_pairs={{0,2},{2,0},{4,6},{6,4},{8,10},{10,8},{12,14},{14,12},{1,3},{3,1},... | collective-permute-start | bytes 24584 | tf_op jit(solution)/shard_map/ppermute | solution.py:36
  7.5 2.5 %collective-permute-start.3 = (s32[16,128]{1,0:T(8,128)S(1)}, s32[16,128]{1,0:T(8,128)S(1)}, u32[]{:S(2)}, u32[]{:S(2)}) collective-permute-start(s32[16,128]{1,0:T(8,128)S(1)} %pad_add_fusion.mine_ref), channel_id=1, source_target_pairs={{0,12},{2,14},{4,8},{6,10},{8,4},{10,6},{12,0},{14,2},{1,13},{3,15... | collective-permute-start | bytes 24584 | tf_op jit(solution)/shard_map/ppermute | solution.py:36
  9.9 1.3 %collective-permute-start.2 = (s32[16,128]{1,0:T(8,128)S(1)}, s32[16,128]{1,0:T(8,128)S(1)}, u32[]{:S(2)}, u32[]{:S(2)}) collective-permute-start(s32[16,128]{1,0:T(8,128)S(1)} %pad_add_fusion.mine_ref), channel_id=1, source_target_pairs={{0,14},{2,4},{4,2},{6,8},{8,6},{10,12},{12,10},{14,0},{1,15},{3,5}... | collective-permute-start | bytes 24584 | tf_op jit(solution)/shard_map/ppermute | solution.py:36
  11.2 0.2 gather_rows.7
  11.5 0.7 %collective-permute-start.9 = (bf16[2,128,384]{2,1,0:T(8,128)(2,1)S(1)}, bf16[2,128,384]{2,1,0:T(8,128)(2,1)S(1)}, u32[]{:S(2)}, u32[]{:S(2)}) collective-permute-start(bf16[2,128,384]{2,1,0:T(8,128)(2,1)S(1)} %gather_rows.7), channel_id=1, source_target_pairs={{0,4},{2,6},{4,0},{6,2},{8,12},{10,14},{12,8},{14,10},{1,5},{3,7},... | collective-permute-start | bytes 589832 | tf_op jit(solution)/shard_map/ppermute | solution.py:36
  12.2 0.2 gather_rows.6
  12.4 0.3 collective-permute-start.8
  13.1 3.0 %collective-permute-start.7 = (bf16[2,128,384]{2,1,0:T(8,128)(2,1)S(1)}, bf16[2,128,384]{2,1,0:T(8,128)(2,1)S(1)}, u32[]{:S(2)}, u32[]{:S(2)}) collective-permute-start(bf16[2,128,384]{2,1,0:T(8,128)(2,1)S(1)} %gather_rows.5), channel_id=1, source_target_pairs={{0,12},{2,14},{4,8},{6,10},{8,4},{10,6},{12,0},{14,2},{1,13},{3,15... | collective-permute-start | bytes 589832 | tf_op jit(solution)/shard_map/ppermute | solution.py:36
  16.1 0.3 collective-permute-done.2.refs_0_.numbers_ref
  16.7 1.7 %collective-permute-start.6 = (bf16[2,128,384]{2,1,0:T(8,128)(2,1)S(1)}, bf16[2,128,384]{2,1,0:T(8,128)(2,1)S(1)}, u32[]{:S(2)}, u32[]{:S(2)}) collective-permute-start(bf16[2,128,384]{2,1,0:T(8,128)(2,1)S(1)} %gather_rows.4), channel_id=1, source_target_pairs={{0,14},{2,4},{4,2},{6,8},{8,6},{10,12},{12,10},{14,0},{1,15},{3,5}... | collective-permute-start | bytes 589832 | tf_op jit(solution)/shard_map/ppermute | solution.py:36
  18.4 3.0 %collective-permute-done.9.refs_3_ = bf16[2,128,384]{2,1,0:T(8,128)(2,1)S(1)} collective-permute-done((bf16[2,128,384]{2,1,0:T(8,128)(2,1)S(1)}, bf16[2,128,384]{2,1,0:T(8,128)(2,1)S(1)}, u32[]{:S(2)}, u32[]{:S(2)}) %collective-permute-start.9) | collective-permute-done | bytes 196640 | tf_op jit(solution)/shard_map/ppermute | solution.py:36
  21.4 0.5 %collective-permute-start.12 = (bf16[2,128,384]{2,1,0:T(8,128)(2,1)S(1)}, bf16[2,128,384]{2,1,0:T(8,128)(2,1)S(1)}, u32[]{:S(2)}, u32[]{:S(2)}) collective-permute-start(bf16[2,128,384]{2,1,0:T(8,128)(2,1)S(1)} %collective-permute-done.8.refs_2_), channel_id=1, source_target_pairs={{0,1},{1,0},{2,3},{3,2},{4,5},{5,4},{6,7},{7,6},{8,9},{9,8},{10,11... | collective-permute-start | bytes 589832 | tf_op jit(solution)/shard_map/ppermute | solution.py:40
  21.9 1.4 %collective-permute-done.7.refs_1_ = bf16[2,128,384]{2,1,0:T(8,128)(2,1)S(1)} collective-permute-done((bf16[2,128,384]{2,1,0:T(8,128)(2,1)S(1)}, bf16[2,128,384]{2,1,0:T(8,128)(2,1)S(1)}, u32[]{:S(2)}, u32[]{:S(2)}) %collective-permute-start.7) | collective-permute-done | bytes 196640 | tf_op jit(solution)/shard_map/ppermute | solution.py:36
  23.2 0.7 %block_tables.1 = (s32[24,128]{1,0:T(8,128)S(1)}, s32[24,128]{1,0:T(8,128)S(1)}, s32[24,128]{1,0:T(8,128)S(1)}, s32[24,128]{1,0:T(8,128)S(1)}, bf16[49,128,384]{2,1,0:T(8,128)(2,1)S(1)}) custom-call(s32[16,128]{1,0:T(8,128)S(1)} %pad_add_fusion.mine_ref, bf16[16,128,384]{2,1,0:T(8,128)(2,1)S(1)} %stage_density.1.own_ref.density_ref, ...), custom_call_target="tpu_custom_call" | custom-call | bytes 6291456 | tf_op jit(solution)/shard_map/block_tables/pallas_call | solution.py:206
  23.9 3.7 %collective-permute-done.6.refs_0_ = bf16[2,128,384]{2,1,0:T(8,128)(2,1)S(1)} collective-permute-done((bf16[2,128,384]{2,1,0:T(8,128)(2,1)S(1)}, bf16[2,128,384]{2,1,0:T(8,128)(2,1)S(1)}, u32[]{:S(2)}, u32[]{:S(2)}) %collective-permute-start.6) | collective-permute-done | bytes 196640 | tf_op jit(solution)/shard_map/ppermute | solution.py:36
  27.6 1.4 %collective-permute-done.10.refs_4_ = bf16[2,128,384]{2,1,0:T(8,128)(2,1)S(1)} collective-permute-done((bf16[2,128,384]{2,1,0:T(8,128)(2,1)S(1)}, bf16[2,128,384]{2,1,0:T(8,128)(2,1)S(1)}, u32[]{:S(2)}, u32[]{:S(2)}) %collective-permute-start.10) | collective-permute-done | bytes 196640 | tf_op jit(solution)/shard_map/ppermute | solution.py:40
  29.0 0.5 %square_wanted.2 = (bf16[2,128,384]{2,1,0:T(8,128)(2,1)S(1)}, bf16[49,128,384]{2,1,0:T(8,128)(2,1)S(1)}) custom-call(s32[24,128]{1,0:T(8,128)S(1)} %get-tuple-element.28.index_ref, bf16[16,128,384]{2,1,0:T(8,128)(2,1)S(1)} %stage_density.1.own_ref.density_ref, ...), custom_call_target="tpu_custom_call", output_to_operand_aliasing={{1}: (3, {})} | custom-call | flops 150994944 | bytes 12582912 | tf_op jit(solution)/shard_map/square_wanted/pallas_call | solution.py:275
  29.6 1.7 %collective-permute-start.14 = (bf16[2,128,384]{2,1,0:T(8,128)(2,1)S(1)}, bf16[2,128,384]{2,1,0:T(8,128)(2,1)S(1)}, u32[]{:S(2)}, u32[]{:S(2)}) collective-permute-start(bf16[2,128,384]{2,1,0:T(8,128)(2,1)S(1)} %get-tuple-element.32), channel_id=1, source_target_pairs={{0,14},{2,4},{4,2},{6,8},{8,6},{10,12},{12,10},{14,0},{1,15},{3,5}... | collective-permute-start | bytes 589832 | tf_op jit(solution)/shard_map/ppermute | solution.py:36
  31.3 1.0 %square_wanted.3 = (bf16[2,128,384]{2,1,0:T(8,128)(2,1)S(1)}, bf16[2,128,384]{2,1,0:T(8,128)(2,1)S(1)}, bf16[2,128,384]{2,1,0:T(8,128)(2,1)S(1)}) custom-call(s32[24,128]{1,0:T(8,128)S(1)} %get-tuple-element.28.index_ref, bf16[16,128,384]{2,1,0:T(8,128)(2,1)S(1)} %stage_density.1.own_ref.density_ref, ...), custom_call_target="tpu_custom_call" | custom-call | flops 452984832 | bytes 12582912 | tf_op jit(solution)/shard_map/square_wanted/pallas_call | solution.py:275
  32.4 1.5 %collective-permute-start.15 = (bf16[2,128,384]{2,1,0:T(8,128)(2,1)S(1)}, bf16[2,128,384]{2,1,0:T(8,128)(2,1)S(1)}, u32[]{:S(2)}, u32[]{:S(2)}) collective-permute-start(bf16[2,128,384]{2,1,0:T(8,128)(2,1)S(1)} %get-tuple-element.34), channel_id=1, source_target_pairs={{0,12},{2,14},{4,8},{6,10},{8,4},{10,6},{12,0},{14,2},{1,13},{3,15... | collective-permute-start | bytes 589832 | tf_op jit(solution)/shard_map/ppermute | solution.py:36
  33.9 2.2 %collective-permute-start.16 = (bf16[2,128,384]{2,1,0:T(8,128)(2,1)S(1)}, bf16[2,128,384]{2,1,0:T(8,128)(2,1)S(1)}, u32[]{:S(2)}, u32[]{:S(2)}) collective-permute-start(bf16[2,128,384]{2,1,0:T(8,128)(2,1)S(1)} %get-tuple-element.36), channel_id=1, source_target_pairs={{0,2},{2,0},{4,6},{6,4},{8,10},{10,8},{12,14},{14,12},{1,3},{3,1},... | collective-permute-start | bytes 589832 | tf_op jit(solution)/shard_map/ppermute | solution.py:36
  36.0 0.5 collective-permute-start.17
  36.5 5.2 %square_rows.1.refs_0_ = bf16[49,128,384]{2,1,0:T(8,128)(2,1)S(1)} custom-call(s32[24,128]{1,0:T(8,128)S(1)} %get-tuple-element.26.index_ref, s32[24,128]{1,0:T(8,128)S(1)} %get-tuple-element.27.others_ref, bf16[16,128,384]{2,1,0:T(8,128)(2,1)S(1)} %stage_density.1.own_ref.density_ref, bf16[16,128,384]{2,1,0:T(8,128)(2,1)S(1)} %collective-permute-done.1.other_ref, ...), custom_call_target="tpu_custom_call" | custom-call | flops 2415919104 | bytes 12582912 | tf_op jit(solution)/shard_map/square_rows/pallas_call | solution.py:303
  41.8 0.9 %collective-permute-done.15.refs_2_ = bf16[2,128,384]{2,1,0:T(8,128)(2,1)S(1)} collective-permute-done((bf16[2,128,384]{2,1,0:T(8,128)(2,1)S(1)}, bf16[2,128,384]{2,1,0:T(8,128)(2,1)S(1)}, u32[]{:S(2)}, u32[]{:S(2)}) %collective-permute-start.15) | collective-permute-done | bytes 196640 | tf_op jit(solution)/shard_map/ppermute | solution.py:36
  42.7 0.8 %collective-permute-done.16.refs_3_ = bf16[2,128,384]{2,1,0:T(8,128)(2,1)S(1)} collective-permute-done((bf16[2,128,384]{2,1,0:T(8,128)(2,1)S(1)}, bf16[2,128,384]{2,1,0:T(8,128)(2,1)S(1)}, u32[]{:S(2)}, u32[]{:S(2)}) %collective-permute-start.16) | collective-permute-done | bytes 196640 | tf_op jit(solution)/shard_map/ppermute | solution.py:36
  43.5 2.6 %collective-permute-done.17.refs_4_ = bf16[2,128,384]{2,1,0:T(8,128)(2,1)S(1)} collective-permute-done((bf16[2,128,384]{2,1,0:T(8,128)(2,1)S(1)}, bf16[2,128,384]{2,1,0:T(8,128)(2,1)S(1)}, u32[]{:S(2)}, u32[]{:S(2)}) %collective-permute-start.17) | collective-permute-done | bytes 196640 | tf_op jit(solution)/shard_map/ppermute | solution.py:36
  46.1 1.4 %collective-permute-done.21.refs_8_ = bf16[2,128,384]{2,1,0:T(8,128)(2,1)S(1)} collective-permute-done((bf16[2,128,384]{2,1,0:T(8,128)(2,1)S(1)}, bf16[2,128,384]{2,1,0:T(8,128)(2,1)S(1)}, u32[]{:S(2)}, u32[]{:S(2)}) %collective-permute-start.21) | collective-permute-done | bytes 196640 | tf_op jit(solution)/shard_map/ppermute | solution.py:40
  47.5 3.3 %cube_rows.1 = (bf16[16,128,384]{2,1,0:T(8,128)(2,1)}, bf16[49,128,384]{2,1,0:T(8,128)(2,1)S(1)}) custom-call(s32[24,128]{1,0:T(8,128)S(1)} %get-tuple-element.25.index_ref, bf16[16,128,384]{2,1,0:T(8,128)(2,1)S(1)} %stage_density.1.own_ref.density_ref, bf16[16,128,384]{2,1,0:T(8,128)(2,1)S(1)} %collective-permute-done.1.other_ref, ...), custom_call_target="tpu_custom_call", output_to_operand_aliasing={{1}: (3, {})} | custom-call | flops 1207959552 | bytes 12582912 | tf_op jit(solution)/shard_map/cube_rows/pallas_call | solution.py:333
  (27 shorter events, 1.0 us)
Async XLA Ops:
  0.7 2.1 %collective-permute-start = (s32[8,128]{1,0:T(8,128)S(1)}, s32[8,128]{1,0:T(8,128)S(1)}, u32[]{:S(2)}, u32[]{:S(2)}) collective-permute-start(s32[8,128]{1,0:T(8,128)S(1)} %pad.4), channel_id=1, source_target_pairs={{0,1},{1,0},{2,3},{3,2},{4,5},{5,4},{6,7},{7,6},{8,9},{9,8},{10,11... | collective-permute-start | bytes 12296 | tf_op jit(solution)/shard_map/ppermute | solution.py:40
  1.2 1.4 %copy-start = (bf16[16,128,384]{2,1,0:T(8,128)(2,1)S(1)}, bf16[16,128,384]{2,1,0:T(8,128)(2,1)}, u32[]{:S(2)}) copy-start(bf16[16,128,384]{2,1,0:T(8,128)(2,1)} %density_ref.1) | copy-start | bytes 4718596
  2.8 20.4 %collective-permute-start.1 = (bf16[16,128,384]{2,1,0:T(8,128)(2,1)S(1)}, bf16[16,128,384]{2,1,0:T(8,128)(2,1)S(1)}, u32[]{:S(2)}, u32[]{:S(2)}) collective-permute-start(bf16[16,128,384]{2,1,0:T(8,128)(2,1)S(1)} %stage_density.1.own_ref.density_ref), channel_id=1, source_target_pairs={{0,1},{1,0},{2,3},{3,2},{4,5},{5,4},{6,7},{7,6},{8,9},{9,8},{10,11... | collective-permute-start | bytes 4718600 | tf_op jit(solution)/shard_map/ppermute | solution.py:40
  2.9 8.3 %collective-permute-start.5 = (s32[16,128]{1,0:T(8,128)S(1)}, s32[16,128]{1,0:T(8,128)S(1)}, u32[]{:S(2)}, u32[]{:S(2)}) collective-permute-start(s32[16,128]{1,0:T(8,128)S(1)} %pad_add_fusion.mine_ref), channel_id=1, source_target_pairs={{0,4},{2,6},{4,0},{6,2},{8,12},{10,14},{12,8},{14,10},{1,5},{3,7},... | collective-permute-start | bytes 24584 | tf_op jit(solution)/shard_map/ppermute | solution.py:36
  5.9 6.3 %collective-permute-start.4 = (s32[16,128]{1,0:T(8,128)S(1)}, s32[16,128]{1,0:T(8,128)S(1)}, u32[]{:S(2)}, u32[]{:S(2)}) collective-permute-start(s32[16,128]{1,0:T(8,128)S(1)} %pad_add_fusion.mine_ref), channel_id=1, source_target_pairs={{0,2},{2,0},{4,6},{6,4},{8,10},{10,8},{12,14},{14,12},{1,3},{3,1},... | collective-permute-start | bytes 24584 | tf_op jit(solution)/shard_map/ppermute | solution.py:36
  7.5 5.4 %collective-permute-start.3 = (s32[16,128]{1,0:T(8,128)S(1)}, s32[16,128]{1,0:T(8,128)S(1)}, u32[]{:S(2)}, u32[]{:S(2)}) collective-permute-start(s32[16,128]{1,0:T(8,128)S(1)} %pad_add_fusion.mine_ref), channel_id=1, source_target_pairs={{0,12},{2,14},{4,8},{6,10},{8,4},{10,6},{12,0},{14,2},{1,13},{3,15... | collective-permute-start | bytes 24584 | tf_op jit(solution)/shard_map/ppermute | solution.py:36
  9.9 6.5 %collective-permute-start.2 = (s32[16,128]{1,0:T(8,128)S(1)}, s32[16,128]{1,0:T(8,128)S(1)}, u32[]{:S(2)}, u32[]{:S(2)}) collective-permute-start(s32[16,128]{1,0:T(8,128)S(1)} %pad_add_fusion.mine_ref), channel_id=1, source_target_pairs={{0,14},{2,4},{4,2},{6,8},{8,6},{10,12},{12,10},{14,0},{1,15},{3,5}... | collective-permute-start | bytes 24584 | tf_op jit(solution)/shard_map/ppermute | solution.py:36
  11.5 9.9 %collective-permute-start.9 = (bf16[2,128,384]{2,1,0:T(8,128)(2,1)S(1)}, bf16[2,128,384]{2,1,0:T(8,128)(2,1)S(1)}, u32[]{:S(2)}, u32[]{:S(2)}) collective-permute-start(bf16[2,128,384]{2,1,0:T(8,128)(2,1)S(1)} %gather_rows.7), channel_id=1, source_target_pairs={{0,4},{2,6},{4,0},{6,2},{8,12},{10,14},{12,8},{14,10},{1,5},{3,7},... | collective-permute-start | bytes 589832 | tf_op jit(solution)/shard_map/ppermute | solution.py:36
  12.4 8.9 %collective-permute-start.8 = (bf16[2,128,384]{2,1,0:T(8,128)(2,1)S(1)}, bf16[2,128,384]{2,1,0:T(8,128)(2,1)S(1)}, u32[]{:S(2)}, u32[]{:S(2)}) collective-permute-start(bf16[2,128,384]{2,1,0:T(8,128)(2,1)S(1)} %gather_rows.6), channel_id=1, source_target_pairs={{0,2},{2,0},{4,6},{6,4},{8,10},{10,8},{12,14},{14,12},{1,3},{3,1},... | collective-permute-start | bytes 589832 | tf_op jit(solution)/shard_map/ppermute | solution.py:36
  13.1 10.1 %collective-permute-start.7 = (bf16[2,128,384]{2,1,0:T(8,128)(2,1)S(1)}, bf16[2,128,384]{2,1,0:T(8,128)(2,1)S(1)}, u32[]{:S(2)}, u32[]{:S(2)}) collective-permute-start(bf16[2,128,384]{2,1,0:T(8,128)(2,1)S(1)} %gather_rows.5), channel_id=1, source_target_pairs={{0,12},{2,14},{4,8},{6,10},{8,4},{10,6},{12,0},{14,2},{1,13},{3,15... | collective-permute-start | bytes 589832 | tf_op jit(solution)/shard_map/ppermute | solution.py:36
  16.7 10.9 %collective-permute-start.6 = (bf16[2,128,384]{2,1,0:T(8,128)(2,1)S(1)}, bf16[2,128,384]{2,1,0:T(8,128)(2,1)S(1)}, u32[]{:S(2)}, u32[]{:S(2)}) collective-permute-start(bf16[2,128,384]{2,1,0:T(8,128)(2,1)S(1)} %gather_rows.4), channel_id=1, source_target_pairs={{0,14},{2,4},{4,2},{6,8},{8,6},{10,12},{12,10},{14,0},{1,15},{3,5}... | collective-permute-start | bytes 589832 | tf_op jit(solution)/shard_map/ppermute | solution.py:36
  21.3 6.3 %collective-permute-start.13 = (bf16[2,128,384]{2,1,0:T(8,128)(2,1)S(1)}, bf16[2,128,384]{2,1,0:T(8,128)(2,1)S(1)}, u32[]{:S(2)}, u32[]{:S(2)}) collective-permute-start(bf16[2,128,384]{2,1,0:T(8,128)(2,1)S(1)} %collective-permute-done.9.refs_3_), channel_id=1, source_target_pairs={{0,1},{1,0},{2,3},{3,2},{4,5},{5,4},{6,7},{7,6},{8,9},{9,8},{10,11... | collective-permute-start | bytes 589832 | tf_op jit(solution)/shard_map/ppermute | solution.py:40
  21.4 6.3 %collective-permute-start.12 = (bf16[2,128,384]{2,1,0:T(8,128)(2,1)S(1)}, bf16[2,128,384]{2,1,0:T(8,128)(2,1)S(1)}, u32[]{:S(2)}, u32[]{:S(2)}) collective-permute-start(bf16[2,128,384]{2,1,0:T(8,128)(2,1)S(1)} %collective-permute-done.8.refs_2_), channel_id=1, source_target_pairs={{0,1},{1,0},{2,3},{3,2},{4,5},{5,4},{6,7},{7,6},{8,9},{9,8},{10,11... | collective-permute-start | bytes 589832 | tf_op jit(solution)/shard_map/ppermute | solution.py:40
  23.2 4.4 %collective-permute-start.11 = (bf16[2,128,384]{2,1,0:T(8,128)(2,1)S(1)}, bf16[2,128,384]{2,1,0:T(8,128)(2,1)S(1)}, u32[]{:S(2)}, u32[]{:S(2)}) collective-permute-start(bf16[2,128,384]{2,1,0:T(8,128)(2,1)S(1)} %collective-permute-done.7.refs_1_), channel_id=1, source_target_pairs={{0,1},{1,0},{2,3},{3,2},{4,5},{5,4},{6,7},{7,6},{8,9},{9,8},{10,11... | collective-permute-start | bytes 589832 | tf_op jit(solution)/shard_map/ppermute | solution.py:40
  27.6 1.4 %collective-permute-start.10 = (bf16[2,128,384]{2,1,0:T(8,128)(2,1)S(1)}, bf16[2,128,384]{2,1,0:T(8,128)(2,1)S(1)}, u32[]{:S(2)}, u32[]{:S(2)}) collective-permute-start(bf16[2,128,384]{2,1,0:T(8,128)(2,1)S(1)} %collective-permute-done.6.refs_0_), channel_id=1, source_target_pairs={{0,1},{1,0},{2,3},{3,2},{4,5},{5,4},{6,7},{7,6},{8,9},{9,8},{10,11... | collective-permute-start | bytes 589832 | tf_op jit(solution)/shard_map/ppermute | solution.py:40
  29.6 12.2 %collective-permute-start.14 = (bf16[2,128,384]{2,1,0:T(8,128)(2,1)S(1)}, bf16[2,128,384]{2,1,0:T(8,128)(2,1)S(1)}, u32[]{:S(2)}, u32[]{:S(2)}) collective-permute-start(bf16[2,128,384]{2,1,0:T(8,128)(2,1)S(1)} %get-tuple-element.32), channel_id=1, source_target_pairs={{0,14},{2,4},{4,2},{6,8},{8,6},{10,12},{12,10},{14,0},{1,15},{3,5}... | collective-permute-start | bytes 589832 | tf_op jit(solution)/shard_map/ppermute | solution.py:36
  32.4 10.3 %collective-permute-start.15 = (bf16[2,128,384]{2,1,0:T(8,128)(2,1)S(1)}, bf16[2,128,384]{2,1,0:T(8,128)(2,1)S(1)}, u32[]{:S(2)}, u32[]{:S(2)}) collective-permute-start(bf16[2,128,384]{2,1,0:T(8,128)(2,1)S(1)} %get-tuple-element.34), channel_id=1, source_target_pairs={{0,12},{2,14},{4,8},{6,10},{8,4},{10,6},{12,0},{14,2},{1,13},{3,15... | collective-permute-start | bytes 589832 | tf_op jit(solution)/shard_map/ppermute | solution.py:36
  33.9 9.6 %collective-permute-start.16 = (bf16[2,128,384]{2,1,0:T(8,128)(2,1)S(1)}, bf16[2,128,384]{2,1,0:T(8,128)(2,1)S(1)}, u32[]{:S(2)}, u32[]{:S(2)}) collective-permute-start(bf16[2,128,384]{2,1,0:T(8,128)(2,1)S(1)} %get-tuple-element.36), channel_id=1, source_target_pairs={{0,2},{2,0},{4,6},{6,4},{8,10},{10,8},{12,14},{14,12},{1,3},{3,1},... | collective-permute-start | bytes 589832 | tf_op jit(solution)/shard_map/ppermute | solution.py:36
  36.0 10.0 %collective-permute-start.17 = (bf16[2,128,384]{2,1,0:T(8,128)(2,1)S(1)}, bf16[2,128,384]{2,1,0:T(8,128)(2,1)S(1)}, u32[]{:S(2)}, u32[]{:S(2)}) collective-permute-start(bf16[2,128,384]{2,1,0:T(8,128)(2,1)S(1)} %get-tuple-element.38), channel_id=1, source_target_pairs={{0,4},{2,6},{4,0},{6,2},{8,12},{10,14},{12,8},{14,10},{1,5},{3,7},... | collective-permute-start | bytes 589832 | tf_op jit(solution)/shard_map/ppermute | solution.py:36
  41.8 4.3 %collective-permute-start.18 = (bf16[2,128,384]{2,1,0:T(8,128)(2,1)S(1)}, bf16[2,128,384]{2,1,0:T(8,128)(2,1)S(1)}, u32[]{:S(2)}, u32[]{:S(2)}) collective-permute-start(bf16[2,128,384]{2,1,0:T(8,128)(2,1)S(1)} %collective-permute-done.14.refs_1_), channel_id=1, source_target_pairs={{0,1},{1,0},{2,3},{3,2},{4,5},{5,4},{6,7},{7,6},{8,9},{9,8},{10,11... | collective-permute-start | bytes 589832 | tf_op jit(solution)/shard_map/ppermute | solution.py:40
  42.7 3.4 %collective-permute-start.19 = (bf16[2,128,384]{2,1,0:T(8,128)(2,1)S(1)}, bf16[2,128,384]{2,1,0:T(8,128)(2,1)S(1)}, u32[]{:S(2)}, u32[]{:S(2)}) collective-permute-start(bf16[2,128,384]{2,1,0:T(8,128)(2,1)S(1)} %collective-permute-done.15.refs_2_), channel_id=1, source_target_pairs={{0,1},{1,0},{2,3},{3,2},{4,5},{5,4},{6,7},{7,6},{8,9},{9,8},{10,11... | collective-permute-start | bytes 589832 | tf_op jit(solution)/shard_map/ppermute | solution.py:40
  43.5 2.6 %collective-permute-start.20 = (bf16[2,128,384]{2,1,0:T(8,128)(2,1)S(1)}, bf16[2,128,384]{2,1,0:T(8,128)(2,1)S(1)}, u32[]{:S(2)}, u32[]{:S(2)}) collective-permute-start(bf16[2,128,384]{2,1,0:T(8,128)(2,1)S(1)} %collective-permute-done.16.refs_3_), channel_id=1, source_target_pairs={{0,1},{1,0},{2,3},{3,2},{4,5},{5,4},{6,7},{7,6},{8,9},{9,8},{10,11... | collective-permute-start | bytes 589832 | tf_op jit(solution)/shard_map/ppermute | solution.py:40
  46.1 1.4 %collective-permute-start.21 = (bf16[2,128,384]{2,1,0:T(8,128)(2,1)S(1)}, bf16[2,128,384]{2,1,0:T(8,128)(2,1)S(1)}, u32[]{:S(2)}, u32[]{:S(2)}) collective-permute-start(bf16[2,128,384]{2,1,0:T(8,128)(2,1)S(1)} %collective-permute-done.17.refs_4_), channel_id=1, source_target_pairs={{0,1},{1,0},{2,3},{3,2},{4,5},{5,4},{6,7},{7,6},{8,9},{9,8},{10,11... | collective-permute-start | bytes 589832 | tf_op jit(solution)/shard_map/ppermute | solution.py:40

commit v9 on v8

--- a/solution.py
+++ b/solution.py
@@ -368,7 +368,7 @@
 
     got = [swapped(piece, exchange) for exchange, piece in zip(EXCHANGES, wanted)]
     squares = square(square_index, others_index, own, other, table, half)
-    got = [lax.optimization_barrier((piece, squares))[0] for piece in got]
+    got[0] = lax.optimization_barrier((got[0], squares))[0]
     got += [from_sibling(piece) for piece in got]
     return cube(cube_index, own, other, squares, got, half)
 

time: 51 us -> 51 us (level)
  no operation moved by 1% of the time
where the time goes in v9:
time: 51 us; the launch traced here: 50.8 us
  starting transfers between devices  21.2 us (42%)
  waiting for transfers between devices  15.5 us (30%)
  Pallas kernels  11.8 us (23%)
  local copies, waits for them, and re-layouts  1.41 us (3%)
  other arithmetic  0.71 us (1%)
    ppermute x12, starting transfers between devices, swapped(): return lax.ppermute(value, 'rows', pairs)  19.9 us
    ppermute x12, waiting for transfers between devices, swapped(): return lax.ppermute(value, 'rows', pairs)  12.7 us
    pallas_call x1, Pallas kernels, square(): pl.pallas_call(functools.partial(square_kernel, half), out_shape=like(tab...  5.24 us
    pallas_call x1, Pallas kernels, cube(): pl.pallas_call(functools.partial(cube_kernel, half), out_shape=[like(own)...  3.25 us
    ppermute x10, waiting for transfers between devices, from_sibling(): return lax.ppermute(value, 'layers', [(0, 1), (1, 0)])  2.86 us
    pallas_call x2, Pallas kernels, square_wanted(): pl.pallas_call(functools.partial(wanted_kernel, half, first, len(pieces))...  1.58 us
    unnamed x2, local copies, waits for them, and re-layouts  1.41 us
    ppermute x10, starting transfers between devices, from_sibling(): return lax.ppermute(value, 'layers', [(0, 1), (1, 0)])  1.25 us
  transfers between devices with their start and end apart: 22, of which 10 were waited for; matrix products, arithmetic and copies ran while one was open for 0% of the time, Pallas kernels for 16%

profile of v9, /device:TPU:0, one launch (start us, length us, event | category | flops | bytes accessed | tf_op | source)
XLA Modules:
  0.0 50.8 jit_solution(7811218808833476728)
XLA Ops:
  0.0 0.7 %add_bitcast_fusion = s32[6,16]{1,0:T(8,128)S(1)} fusion(s32[16,3]{0,1:T(4,128)} %param.5, s32[16,3]{0,1:T(4,128)} %param.4), kind=kLoop, calls=%fused_computation.1 | loop fusion | flops 96 | bytes 768 | tf_op jit(solution)/shard_map/transpose | solution.py:63
  0.7 0.5 %collective-permute-start = (s32[8,128]{1,0:T(8,128)S(1)}, s32[8,128]{1,0:T(8,128)S(1)}, u32[]{:S(2)}, u32[]{:S(2)}) collective-permute-start(s32[8,128]{1,0:T(8,128)S(1)} %pad.4), channel_id=1, source_target_pairs={{0,1},{1,0},{2,3},{3,2},{4,5},{5,4},{6,7},{7,6},{8,9},{9,8},{10,11... | collective-permute-start | bytes 12296 | tf_op jit(solution)/shard_map/ppermute | solution.py:40
  1.2 1.4 %copy-done = bf16[16,128,384]{2,1,0:T(8,128)(2,1)S(1)} copy-done((bf16[16,128,384]{2,1,0:T(8,128)(2,1)S(1)}, bf16[16,128,384]{2,1,0:T(8,128)(2,1)}, u32[]{:S(2)}) %copy-start) | copy-done | bytes 1572888
  2.9 3.0 %collective-permute-start.5 = (s32[16,128]{1,0:T(8,128)S(1)}, s32[16,128]{1,0:T(8,128)S(1)}, u32[]{:S(2)}, u32[]{:S(2)}) collective-permute-start(s32[16,128]{1,0:T(8,128)S(1)} %pad_add_fusion.mine_ref), channel_id=1, source_target_pairs={{0,4},{2,6},{4,0},{6,2},{8,12},{10,14},{12,8},{14,10},{1,5},{3,7},... | collective-permute-start | bytes 24584 | tf_op jit(solution)/shard_map/ppermute | solution.py:36
  5.9 1.5 %collective-permute-start.4 = (s32[16,128]{1,0:T(8,128)S(1)}, s32[16,128]{1,0:T(8,128)S(1)}, u32[]{:S(2)}, u32[]{:S(2)}) collective-permute-start(s32[16,128]{1,0:T(8,128)S(1)} %pad_add_fusion.mine_ref), channel_id=1, source_target_pairs={{0,2},{2,0},{4,6},{6,4},{8,10},{10,8},{12,14},{14,12},{1,3},{3,1},... | collective-permute-start | bytes 24584 | tf_op jit(solution)/shard_map/ppermute | solution.py:36
  7.5 2.5 %collective-permute-start.3 = (s32[16,128]{1,0:T(8,128)S(1)}, s32[16,128]{1,0:T(8,128)S(1)}, u32[]{:S(2)}, u32[]{:S(2)}) collective-permute-start(s32[16,128]{1,0:T(8,128)S(1)} %pad_add_fusion.mine_ref), channel_id=1, source_target_pairs={{0,12},{2,14},{4,8},{6,10},{8,4},{10,6},{12,0},{14,2},{1,13},{3,15... | collective-permute-start | bytes 24584 | tf_op jit(solution)/shard_map/ppermute | solution.py:36
  9.9 1.3 %collective-permute-start.2 = (s32[16,128]{1,0:T(8,128)S(1)}, s32[16,128]{1,0:T(8,128)S(1)}, u32[]{:S(2)}, u32[]{:S(2)}) collective-permute-start(s32[16,128]{1,0:T(8,128)S(1)} %pad_add_fusion.mine_ref), channel_id=1, source_target_pairs={{0,14},{2,4},{4,2},{6,8},{8,6},{10,12},{12,10},{14,0},{1,15},{3,5}... | collective-permute-start | bytes 24584 | tf_op jit(solution)/shard_map/ppermute | solution.py:36
  11.2 0.2 gather_rows.7
  11.5 0.7 %collective-permute-start.9 = (bf16[2,128,384]{2,1,0:T(8,128)(2,1)S(1)}, bf16[2,128,384]{2,1,0:T(8,128)(2,1)S(1)}, u32[]{:S(2)}, u32[]{:S(2)}) collective-permute-start(bf16[2,128,384]{2,1,0:T(8,128)(2,1)S(1)} %gather_rows.7), channel_id=1, source_target_pairs={{0,4},{2,6},{4,0},{6,2},{8,12},{10,14},{12,8},{14,10},{1,5},{3,7},... | collective-permute-start | bytes 589832 | tf_op jit(solution)/shard_map/ppermute | solution.py:36
  12.2 0.2 gather_rows.6
  12.4 0.3 collective-permute-start.8
  13.1 3.0 %collective-permute-start.7 = (bf16[2,128,384]{2,1,0:T(8,128)(2,1)S(1)}, bf16[2,128,384]{2,1,0:T(8,128)(2,1)S(1)}, u32[]{:S(2)}, u32[]{:S(2)}) collective-permute-start(bf16[2,128,384]{2,1,0:T(8,128)(2,1)S(1)} %gather_rows.5), channel_id=1, source_target_pairs={{0,12},{2,14},{4,8},{6,10},{8,4},{10,6},{12,0},{14,2},{1,13},{3,15... | collective-permute-start | bytes 589832 | tf_op jit(solution)/shard_map/ppermute | solution.py:36
  16.1 0.3 collective-permute-done.2.refs_0_.numbers_ref
  16.7 1.7 %collective-permute-start.6 = (bf16[2,128,384]{2,1,0:T(8,128)(2,1)S(1)}, bf16[2,128,384]{2,1,0:T(8,128)(2,1)S(1)}, u32[]{:S(2)}, u32[]{:S(2)}) collective-permute-start(bf16[2,128,384]{2,1,0:T(8,128)(2,1)S(1)} %gather_rows.4), channel_id=1, source_target_pairs={{0,14},{2,4},{4,2},{6,8},{8,6},{10,12},{12,10},{14,0},{1,15},{3,5}... | collective-permute-start | bytes 589832 | tf_op jit(solution)/shard_map/ppermute | solution.py:36
  18.4 3.0 %collective-permute-done.9.refs_3_ = bf16[2,128,384]{2,1,0:T(8,128)(2,1)S(1)} collective-permute-done((bf16[2,128,384]{2,1,0:T(8,128)(2,1)S(1)}, bf16[2,128,384]{2,1,0:T(8,128)(2,1)S(1)}, u32[]{:S(2)}, u32[]{:S(2)}) %collective-permute-start.9) | collective-permute-done | bytes 196640 | tf_op jit(solution)/shard_map/ppermute | solution.py:36
  21.4 0.5 %collective-permute-start.12 = (bf16[2,128,384]{2,1,0:T(8,128)(2,1)S(1)}, bf16[2,128,384]{2,1,0:T(8,128)(2,1)S(1)}, u32[]{:S(2)}, u32[]{:S(2)}) collective-permute-start(bf16[2,128,384]{2,1,0:T(8,128)(2,1)S(1)} %collective-permute-done.8.refs_2_), channel_id=1, source_target_pairs={{0,1},{1,0},{2,3},{3,2},{4,5},{5,4},{6,7},{7,6},{8,9},{9,8},{10,11... | collective-permute-start | bytes 589832 | tf_op jit(solution)/shard_map/ppermute | solution.py:40
  21.9 1.4 %collective-permute-done.7.refs_1_ = bf16[2,128,384]{2,1,0:T(8,128)(2,1)S(1)} collective-permute-done((bf16[2,128,384]{2,1,0:T(8,128)(2,1)S(1)}, bf16[2,128,384]{2,1,0:T(8,128)(2,1)S(1)}, u32[]{:S(2)}, u32[]{:S(2)}) %collective-permute-start.7) | collective-permute-done | bytes 196640 | tf_op jit(solution)/shard_map/ppermute | solution.py:36
  23.2 0.7 %block_tables.1 = (s32[24,128]{1,0:T(8,128)S(1)}, s32[24,128]{1,0:T(8,128)S(1)}, s32[24,128]{1,0:T(8,128)S(1)}, s32[24,128]{1,0:T(8,128)S(1)}, bf16[49,128,384]{2,1,0:T(8,128)(2,1)S(1)}) custom-call(s32[16,128]{1,0:T(8,128)S(1)} %pad_add_fusion.mine_ref, bf16[16,128,384]{2,1,0:T(8,128)(2,1)S(1)} %stage_density.1.own_ref.density_ref, ...), custom_call_target="tpu_custom_call" | custom-call | bytes 6291456 | tf_op jit(solution)/shard_map/block_tables/pallas_call | solution.py:206
  23.9 3.7 %collective-permute-done.6.refs_0_ = bf16[2,128,384]{2,1,0:T(8,128)(2,1)S(1)} collective-permute-done((bf16[2,128,384]{2,1,0:T(8,128)(2,1)S(1)}, bf16[2,128,384]{2,1,0:T(8,128)(2,1)S(1)}, u32[]{:S(2)}, u32[]{:S(2)}) %collective-permute-start.6) | collective-permute-done | bytes 196640 | tf_op jit(solution)/shard_map/ppermute | solution.py:36
  27.6 1.4 %collective-permute-done.10.refs_4_ = bf16[2,128,384]{2,1,0:T(8,128)(2,1)S(1)} collective-permute-done((bf16[2,128,384]{2,1,0:T(8,128)(2,1)S(1)}, bf16[2,128,384]{2,1,0:T(8,128)(2,1)S(1)}, u32[]{:S(2)}, u32[]{:S(2)}) %collective-permute-start.10) | collective-permute-done | bytes 196640 | tf_op jit(solution)/shard_map/ppermute | solution.py:40
  29.0 0.5 %square_wanted.2 = (bf16[2,128,384]{2,1,0:T(8,128)(2,1)S(1)}, bf16[49,128,384]{2,1,0:T(8,128)(2,1)S(1)}) custom-call(s32[24,128]{1,0:T(8,128)S(1)} %get-tuple-element.25.index_ref, bf16[16,128,384]{2,1,0:T(8,128)(2,1)S(1)} %stage_density.1.own_ref.density_ref, ...), custom_call_target="tpu_custom_call", output_to_operand_aliasing={{1}: (3, {})} | custom-call | flops 150994944 | bytes 12582912 | tf_op jit(solution)/shard_map/square_wanted/pallas_call | solution.py:275
  29.6 1.8 %collective-permute-start.14 = (bf16[2,128,384]{2,1,0:T(8,128)(2,1)S(1)}, bf16[2,128,384]{2,1,0:T(8,128)(2,1)S(1)}, u32[]{:S(2)}, u32[]{:S(2)}) collective-permute-start(bf16[2,128,384]{2,1,0:T(8,128)(2,1)S(1)} %get-tuple-element.29), channel_id=1, source_target_pairs={{0,14},{2,4},{4,2},{6,8},{8,6},{10,12},{12,10},{14,0},{1,15},{3,5}... | collective-permute-start | bytes 589832 | tf_op jit(solution)/shard_map/ppermute | solution.py:36
  31.3 1.0 %square_wanted.3 = (bf16[2,128,384]{2,1,0:T(8,128)(2,1)S(1)}, bf16[2,128,384]{2,1,0:T(8,128)(2,1)S(1)}, bf16[2,128,384]{2,1,0:T(8,128)(2,1)S(1)}) custom-call(s32[24,128]{1,0:T(8,128)S(1)} %get-tuple-element.25.index_ref, bf16[16,128,384]{2,1,0:T(8,128)(2,1)S(1)} %stage_density.1.own_ref.density_ref, ...), custom_call_target="tpu_custom_call" | custom-call | flops 452984832 | bytes 12582912 | tf_op jit(solution)/shard_map/square_wanted/pallas_call | solution.py:275
  32.4 1.5 %collective-permute-start.15 = (bf16[2,128,384]{2,1,0:T(8,128)(2,1)S(1)}, bf16[2,128,384]{2,1,0:T(8,128)(2,1)S(1)}, u32[]{:S(2)}, u32[]{:S(2)}) collective-permute-start(bf16[2,128,384]{2,1,0:T(8,128)(2,1)S(1)} %get-tuple-element.31), channel_id=1, source_target_pairs={{0,12},{2,14},{4,8},{6,10},{8,4},{10,6},{12,0},{14,2},{1,13},{3,15... | collective-permute-start | bytes 589832 | tf_op jit(solution)/shard_map/ppermute | solution.py:36
  33.9 2.2 %collective-permute-start.16 = (bf16[2,128,384]{2,1,0:T(8,128)(2,1)S(1)}, bf16[2,128,384]{2,1,0:T(8,128)(2,1)S(1)}, u32[]{:S(2)}, u32[]{:S(2)}) collective-permute-start(bf16[2,128,384]{2,1,0:T(8,128)(2,1)S(1)} %get-tuple-element.32), channel_id=1, source_target_pairs={{0,2},{2,0},{4,6},{6,4},{8,10},{10,8},{12,14},{14,12},{1,3},{3,1},... | collective-permute-start | bytes 589832 | tf_op jit(solution)/shard_map/ppermute | solution.py:36
  36.1 0.5 collective-permute-start.17
  36.5 5.2 %square_rows.1.refs_0_ = bf16[49,128,384]{2,1,0:T(8,128)(2,1)S(1)} custom-call(s32[24,128]{1,0:T(8,128)S(1)} %get-tuple-element.23.index_ref, s32[24,128]{1,0:T(8,128)S(1)} %get-tuple-element.24.others_ref, bf16[16,128,384]{2,1,0:T(8,128)(2,1)S(1)} %stage_density.1.own_ref.density_ref, bf16[16,128,384]{2,1,0:T(8,128)(2,1)S(1)} %collective-permute-done.1.other_ref, ...), custom_call_target="tpu_custom_call" | custom-call | flops 2415919104 | bytes 12582912 | tf_op jit(solution)/shard_map/square_rows/pallas_call | solution.py:303
  41.9 0.8 %collective-permute-done.15.refs_2_ = bf16[2,128,384]{2,1,0:T(8,128)(2,1)S(1)} collective-permute-done((bf16[2,128,384]{2,1,0:T(8,128)(2,1)S(1)}, bf16[2,128,384]{2,1,0:T(8,128)(2,1)S(1)}, u32[]{:S(2)}, u32[]{:S(2)}) %collective-permute-start.15) | collective-permute-done | bytes 196640 | tf_op jit(solution)/shard_map/ppermute | solution.py:36
  42.7 0.8 %collective-permute-done.16.refs_3_ = bf16[2,128,384]{2,1,0:T(8,128)(2,1)S(1)} collective-permute-done((bf16[2,128,384]{2,1,0:T(8,128)(2,1)S(1)}, bf16[2,128,384]{2,1,0:T(8,128)(2,1)S(1)}, u32[]{:S(2)}, u32[]{:S(2)}) %collective-permute-start.16) | collective-permute-done | bytes 196640 | tf_op jit(solution)/shard_map/ppermute | solution.py:36
  43.5 2.6 %collective-permute-done.17.refs_4_ = bf16[2,128,384]{2,1,0:T(8,128)(2,1)S(1)} collective-permute-done((bf16[2,128,384]{2,1,0:T(8,128)(2,1)S(1)}, bf16[2,128,384]{2,1,0:T(8,128)(2,1)S(1)}, u32[]{:S(2)}, u32[]{:S(2)}) %collective-permute-start.17) | collective-permute-done | bytes 196640 | tf_op jit(solution)/shard_map/ppermute | solution.py:36
  46.1 1.4 %collective-permute-done.21.refs_8_ = bf16[2,128,384]{2,1,0:T(8,128)(2,1)S(1)} collective-permute-done((bf16[2,128,384]{2,1,0:T(8,128)(2,1)S(1)}, bf16[2,128,384]{2,1,0:T(8,128)(2,1)S(1)}, u32[]{:S(2)}, u32[]{:S(2)}) %collective-permute-start.21) | collective-permute-done | bytes 196640 | tf_op jit(solution)/shard_map/ppermute | solution.py:40
  47.5 3.3 %cube_rows.1 = (bf16[16,128,384]{2,1,0:T(8,128)(2,1)}, bf16[49,128,384]{2,1,0:T(8,128)(2,1)S(1)}) custom-call(s32[24,128]{1,0:T(8,128)S(1)} %get-tuple-element.22.index_ref, bf16[16,128,384]{2,1,0:T(8,128)(2,1)S(1)} %stage_density.1.own_ref.density_ref, bf16[16,128,384]{2,1,0:T(8,128)(2,1)S(1)} %collective-permute-done.1.other_ref, ...), custom_call_target="tpu_custom_call", output_to_operand_aliasing={{1}: (3, {})} | custom-call | flops 1207959552 | bytes 12582912 | tf_op jit(solution)/shard_map/cube_rows/pallas_call | solution.py:333
  (27 shorter events, 1.0 us)
Async XLA Ops:
  0.7 2.1 %collective-permute-start = (s32[8,128]{1,0:T(8,128)S(1)}, s32[8,128]{1,0:T(8,128)S(1)}, u32[]{:S(2)}, u32[]{:S(2)}) collective-permute-start(s32[8,128]{1,0:T(8,128)S(1)} %pad.4), channel_id=1, source_target_pairs={{0,1},{1,0},{2,3},{3,2},{4,5},{5,4},{6,7},{7,6},{8,9},{9,8},{10,11... | collective-permute-start | bytes 12296 | tf_op jit(solution)/shard_map/ppermute | solution.py:40
  1.2 1.4 %copy-start = (bf16[16,128,384]{2,1,0:T(8,128)(2,1)S(1)}, bf16[16,128,384]{2,1,0:T(8,128)(2,1)}, u32[]{:S(2)}) copy-start(bf16[16,128,384]{2,1,0:T(8,128)(2,1)} %density_ref.1) | copy-start | bytes 4718596
  2.8 20.4 %collective-permute-start.1 = (bf16[16,128,384]{2,1,0:T(8,128)(2,1)S(1)}, bf16[16,128,384]{2,1,0:T(8,128)(2,1)S(1)}, u32[]{:S(2)}, u32[]{:S(2)}) collective-permute-start(bf16[16,128,384]{2,1,0:T(8,128)(2,1)S(1)} %stage_density.1.own_ref.density_ref), channel_id=1, source_target_pairs={{0,1},{1,0},{2,3},{3,2},{4,5},{5,4},{6,7},{7,6},{8,9},{9,8},{10,11... | collective-permute-start | bytes 4718600 | tf_op jit(solution)/shard_map/ppermute | solution.py:40
  2.9 8.3 %collective-permute-start.5 = (s32[16,128]{1,0:T(8,128)S(1)}, s32[16,128]{1,0:T(8,128)S(1)}, u32[]{:S(2)}, u32[]{:S(2)}) collective-permute-start(s32[16,128]{1,0:T(8,128)S(1)} %pad_add_fusion.mine_ref), channel_id=1, source_target_pairs={{0,4},{2,6},{4,0},{6,2},{8,12},{10,14},{12,8},{14,10},{1,5},{3,7},... | collective-permute-start | bytes 24584 | tf_op jit(solution)/shard_map/ppermute | solution.py:36
  5.9 6.3 %collective-permute-start.4 = (s32[16,128]{1,0:T(8,128)S(1)}, s32[16,128]{1,0:T(8,128)S(1)}, u32[]{:S(2)}, u32[]{:S(2)}) collective-permute-start(s32[16,128]{1,0:T(8,128)S(1)} %pad_add_fusion.mine_ref), channel_id=1, source_target_pairs={{0,2},{2,0},{4,6},{6,4},{8,10},{10,8},{12,14},{14,12},{1,3},{3,1},... | collective-permute-start | bytes 24584 | tf_op jit(solution)/shard_map/ppermute | solution.py:36
  7.5 5.4 %collective-permute-start.3 = (s32[16,128]{1,0:T(8,128)S(1)}, s32[16,128]{1,0:T(8,128)S(1)}, u32[]{:S(2)}, u32[]{:S(2)}) collective-permute-start(s32[16,128]{1,0:T(8,128)S(1)} %pad_add_fusion.mine_ref), channel_id=1, source_target_pairs={{0,12},{2,14},{4,8},{6,10},{8,4},{10,6},{12,0},{14,2},{1,13},{3,15... | collective-permute-start | bytes 24584 | tf_op jit(solution)/shard_map/ppermute | solution.py:36
  9.9 6.5 %collective-permute-start.2 = (s32[16,128]{1,0:T(8,128)S(1)}, s32[16,128]{1,0:T(8,128)S(1)}, u32[]{:S(2)}, u32[]{:S(2)}) collective-permute-start(s32[16,128]{1,0:T(8,128)S(1)} %pad_add_fusion.mine_ref), channel_id=1, source_target_pairs={{0,14},{2,4},{4,2},{6,8},{8,6},{10,12},{12,10},{14,0},{1,15},{3,5}... | collective-permute-start | bytes 24584 | tf_op jit(solution)/shard_map/ppermute | solution.py:36
  11.5 9.9 %collective-permute-start.9 = (bf16[2,128,384]{2,1,0:T(8,128)(2,1)S(1)}, bf16[2,128,384]{2,1,0:T(8,128)(2,1)S(1)}, u32[]{:S(2)}, u32[]{:S(2)}) collective-permute-start(bf16[2,128,384]{2,1,0:T(8,128)(2,1)S(1)} %gather_rows.7), channel_id=1, source_target_pairs={{0,4},{2,6},{4,0},{6,2},{8,12},{10,14},{12,8},{14,10},{1,5},{3,7},... | collective-permute-start | bytes 589832 | tf_op jit(solution)/shard_map/ppermute | solution.py:36
  12.4 8.9 %collective-permute-start.8 = (bf16[2,128,384]{2,1,0:T(8,128)(2,1)S(1)}, bf16[2,128,384]{2,1,0:T(8,128)(2,1)S(1)}, u32[]{:S(2)}, u32[]{:S(2)}) collective-permute-start(bf16[2,128,384]{2,1,0:T(8,128)(2,1)S(1)} %gather_rows.6), channel_id=1, source_target_pairs={{0,2},{2,0},{4,6},{6,4},{8,10},{10,8},{12,14},{14,12},{1,3},{3,1},... | collective-permute-start | bytes 589832 | tf_op jit(solution)/shard_map/ppermute | solution.py:36
  13.1 10.1 %collective-permute-start.7 = (bf16[2,128,384]{2,1,0:T(8,128)(2,1)S(1)}, bf16[2,128,384]{2,1,0:T(8,128)(2,1)S(1)}, u32[]{:S(2)}, u32[]{:S(2)}) collective-permute-start(bf16[2,128,384]{2,1,0:T(8,128)(2,1)S(1)} %gather_rows.5), channel_id=1, source_target_pairs={{0,12},{2,14},{4,8},{6,10},{8,4},{10,6},{12,0},{14,2},{1,13},{3,15... | collective-permute-start | bytes 589832 | tf_op jit(solution)/shard_map/ppermute | solution.py:36
  16.7 10.9 %collective-permute-start.6 = (bf16[2,128,384]{2,1,0:T(8,128)(2,1)S(1)}, bf16[2,128,384]{2,1,0:T(8,128)(2,1)S(1)}, u32[]{:S(2)}, u32[]{:S(2)}) collective-permute-start(bf16[2,128,384]{2,1,0:T(8,128)(2,1)S(1)} %gather_rows.4), channel_id=1, source_target_pairs={{0,14},{2,4},{4,2},{6,8},{8,6},{10,12},{12,10},{14,0},{1,15},{3,5}... | collective-permute-start | bytes 589832 | tf_op jit(solution)/shard_map/ppermute | solution.py:36
  21.3 6.3 %collective-permute-start.13 = (bf16[2,128,384]{2,1,0:T(8,128)(2,1)S(1)}, bf16[2,128,384]{2,1,0:T(8,128)(2,1)S(1)}, u32[]{:S(2)}, u32[]{:S(2)}) collective-permute-start(bf16[2,128,384]{2,1,0:T(8,128)(2,1)S(1)} %collective-permute-done.9.refs_3_), channel_id=1, source_target_pairs={{0,1},{1,0},{2,3},{3,2},{4,5},{5,4},{6,7},{7,6},{8,9},{9,8},{10,11... | collective-permute-start | bytes 589832 | tf_op jit(solution)/shard_map/ppermute | solution.py:40
  21.4 6.3 %collective-permute-start.12 = (bf16[2,128,384]{2,1,0:T(8,128)(2,1)S(1)}, bf16[2,128,384]{2,1,0:T(8,128)(2,1)S(1)}, u32[]{:S(2)}, u32[]{:S(2)}) collective-permute-start(bf16[2,128,384]{2,1,0:T(8,128)(2,1)S(1)} %collective-permute-done.8.refs_2_), channel_id=1, source_target_pairs={{0,1},{1,0},{2,3},{3,2},{4,5},{5,4},{6,7},{7,6},{8,9},{9,8},{10,11... | collective-permute-start | bytes 589832 | tf_op jit(solution)/shard_map/ppermute | solution.py:40
  23.2 4.4 %collective-permute-start.11 = (bf16[2,128,384]{2,1,0:T(8,128)(2,1)S(1)}, bf16[2,128,384]{2,1,0:T(8,128)(2,1)S(1)}, u32[]{:S(2)}, u32[]{:S(2)}) collective-permute-start(bf16[2,128,384]{2,1,0:T(8,128)(2,1)S(1)} %collective-permute-done.7.refs_1_), channel_id=1, source_target_pairs={{0,1},{1,0},{2,3},{3,2},{4,5},{5,4},{6,7},{7,6},{8,9},{9,8},{10,11... | collective-permute-start | bytes 589832 | tf_op jit(solution)/shard_map/ppermute | solution.py:40
  27.6 1.4 %collective-permute-start.10 = (bf16[2,128,384]{2,1,0:T(8,128)(2,1)S(1)}, bf16[2,128,384]{2,1,0:T(8,128)(2,1)S(1)}, u32[]{:S(2)}, u32[]{:S(2)}) collective-permute-start(bf16[2,128,384]{2,1,0:T(8,128)(2,1)S(1)} %collective-permute-done.6.refs_0_), channel_id=1, source_target_pairs={{0,1},{1,0},{2,3},{3,2},{4,5},{5,4},{6,7},{7,6},{8,9},{9,8},{10,11... | collective-permute-start | bytes 589832 | tf_op jit(solution)/shard_map/ppermute | solution.py:40
  29.6 12.2 %collective-permute-start.14 = (bf16[2,128,384]{2,1,0:T(8,128)(2,1)S(1)}, bf16[2,128,384]{2,1,0:T(8,128)(2,1)S(1)}, u32[]{:S(2)}, u32[]{:S(2)}) collective-permute-start(bf16[2,128,384]{2,1,0:T(8,128)(2,1)S(1)} %get-tuple-element.29), channel_id=1, source_target_pairs={{0,14},{2,4},{4,2},{6,8},{8,6},{10,12},{12,10},{14,0},{1,15},{3,5}... | collective-permute-start | bytes 589832 | tf_op jit(solution)/shard_map/ppermute | solution.py:36
  32.4 10.3 %collective-permute-start.15 = (bf16[2,128,384]{2,1,0:T(8,128)(2,1)S(1)}, bf16[2,128,384]{2,1,0:T(8,128)(2,1)S(1)}, u32[]{:S(2)}, u32[]{:S(2)}) collective-permute-start(bf16[2,128,384]{2,1,0:T(8,128)(2,1)S(1)} %get-tuple-element.31), channel_id=1, source_target_pairs={{0,12},{2,14},{4,8},{6,10},{8,4},{10,6},{12,0},{14,2},{1,13},{3,15... | collective-permute-start | bytes 589832 | tf_op jit(solution)/shard_map/ppermute | solution.py:36
  33.9 9.6 %collective-permute-start.16 = (bf16[2,128,384]{2,1,0:T(8,128)(2,1)S(1)}, bf16[2,128,384]{2,1,0:T(8,128)(2,1)S(1)}, u32[]{:S(2)}, u32[]{:S(2)}) collective-permute-start(bf16[2,128,384]{2,1,0:T(8,128)(2,1)S(1)} %get-tuple-element.32), channel_id=1, source_target_pairs={{0,2},{2,0},{4,6},{6,4},{8,10},{10,8},{12,14},{14,12},{1,3},{3,1},... | collective-permute-start | bytes 589832 | tf_op jit(solution)/shard_map/ppermute | solution.py:36
  36.1 10.0 %collective-permute-start.17 = (bf16[2,128,384]{2,1,0:T(8,128)(2,1)S(1)}, bf16[2,128,384]{2,1,0:T(8,128)(2,1)S(1)}, u32[]{:S(2)}, u32[]{:S(2)}) collective-permute-start(bf16[2,128,384]{2,1,0:T(8,128)(2,1)S(1)} %get-tuple-element.33), channel_id=1, source_target_pairs={{0,4},{2,6},{4,0},{6,2},{8,12},{10,14},{12,8},{14,10},{1,5},{3,7},... | collective-permute-start | bytes 589832 | tf_op jit(solution)/shard_map/ppermute | solution.py:36
  41.8 4.3 %collective-permute-start.18 = (bf16[2,128,384]{2,1,0:T(8,128)(2,1)S(1)}, bf16[2,128,384]{2,1,0:T(8,128)(2,1)S(1)}, u32[]{:S(2)}, u32[]{:S(2)}) collective-permute-start(bf16[2,128,384]{2,1,0:T(8,128)(2,1)S(1)} %collective-permute-done.14.refs_1_), channel_id=1, source_target_pairs={{0,1},{1,0},{2,3},{3,2},{4,5},{5,4},{6,7},{7,6},{8,9},{9,8},{10,11... | collective-permute-start | bytes 589832 | tf_op jit(solution)/shard_map/ppermute | solution.py:40
  42.7 3.4 %collective-permute-start.19 = (bf16[2,128,384]{2,1,0:T(8,128)(2,1)S(1)}, bf16[2,128,384]{2,1,0:T(8,128)(2,1)S(1)}, u32[]{:S(2)}, u32[]{:S(2)}) collective-permute-start(bf16[2,128,384]{2,1,0:T(8,128)(2,1)S(1)} %collective-permute-done.15.refs_2_), channel_id=1, source_target_pairs={{0,1},{1,0},{2,3},{3,2},{4,5},{5,4},{6,7},{7,6},{8,9},{9,8},{10,11... | collective-permute-start | bytes 589832 | tf_op jit(solution)/shard_map/ppermute | solution.py:40
  43.5 2.6 %collective-permute-start.20 = (bf16[2,128,384]{2,1,0:T(8,128)(2,1)S(1)}, bf16[2,128,384]{2,1,0:T(8,128)(2,1)S(1)}, u32[]{:S(2)}, u32[]{:S(2)}) collective-permute-start(bf16[2,128,384]{2,1,0:T(8,128)(2,1)S(1)} %collective-permute-done.16.refs_3_), channel_id=1, source_target_pairs={{0,1},{1,0},{2,3},{3,2},{4,5},{5,4},{6,7},{7,6},{8,9},{9,8},{10,11... | collective-permute-start | bytes 589832 | tf_op jit(solution)/shard_map/ppermute | solution.py:40
  46.1 1.4 %collective-permute-start.21 = (bf16[2,128,384]{2,1,0:T(8,128)(2,1)S(1)}, bf16[2,128,384]{2,1,0:T(8,128)(2,1)S(1)}, u32[]{:S(2)}, u32[]{:S(2)}) collective-permute-start(bf16[2,128,384]{2,1,0:T(8,128)(2,1)S(1)} %collective-permute-done.17.refs_4_), channel_id=1, source_target_pairs={{0,1},{1,0},{2,3},{3,2},{4,5},{5,4},{6,7},{7,6},{8,9},{9,8},{10,11... | collective-permute-start | bytes 589832 | tf_op jit(solution)/shard_map/ppermute | solution.py:40
